TPU v7x, 32 devices: a whole 2x2x4 slice. The times are simulated.
32 devices in a mesh: section: 2 (over core), mp: 2 (over y), dp: 8 (over z, x).
Axes of the slice: x: 2, y: 2, z: 4, core: 2. Of those that a mesh axis runs over, the one named last changes fastest.
Arguments:
- inputs: bfloat16 [2, 16, 1024, 1024], P('section', 'dp', 'mp'), may hold values from -6 to 6
- segment_ids: int32 [2, 16, 1024], P(None, 'dp'), may hold values from 0 to 3, never falling along the last dimension, each value on 1 to 512 neighbouring positions
- cotangent: bfloat16 [2, 16, 1024, 1024], P('section', 'dp', 'mp'), may hold values from -6 to 6
- norm_gains: float32 [2, 2, 1024], P('section'), may hold values from 0.1 to 1.9
- cross_gain: float32 [1024], replicated, may hold values from 0.1 to 1.9
- self_qkv: bfloat16 [2, 1024, 3, 1024], P('section', None, None, 'mp'), may hold values from -0.1875 to 0.1875
- self_out: bfloat16 [2, 1024, 1024], P('section', 'mp'), may hold values from -1.5 to 1.5
- cross_kv: bfloat16 [2, 1024, 1024], P('section', None, 'mp'), may hold values from -0.1875 to 0.1875
- cross_vo: bfloat16 [2, 1024, 1024], P('section', None, 'mp'), may hold values from -0.5 to 0.5
- ffn_in: bfloat16 [2, 1024, 4096], P('section', None, 'mp'), may hold values from -0.1875 to 0.1875
- ffn_out: bfloat16 [2, 4096, 1024], P('section', 'mp'), may hold values from -0.09375 to 0.09375
- adapter_down: bfloat16 [2, 1024, 512], P('section', None, 'mp'), may hold values from -0.1875 to 0.1875
- adapter_down_bias: float32 [2, 512], P('section', 'mp'), may hold values from -3 to 3
- adapter_up: bfloat16 [2, 512, 1024], P('section', 'mp'), may hold values from -0.0625 to 0.0625
- adapter_up_bias: float32 [2, 1024], P('section'), may hold values from -0.5 to 0.5
Outputs:
- outputs: bfloat16 [2, 16, 1024, 1024], P('section', 'dp', 'mp')
- input_grads: float32 [2, 16, 1024, 1024], P('section', 'dp', 'mp')
- down_grad: float32 [2, 1024, 512], P('section', None, 'mp')
- down_bias_grad: float32 [2, 512], P('section', 'mp')
- up_grad: float32 [2, 512, 1024], P('section', 'mp')
- up_bias_grad: float32 [2, 1024], P('section')
Inputs may be any that keep to these rules, and one draw needn't show every extreme that they name: `segment_ids`: in each packed row the document numbers run 0 to 3 in order, each document taking 1 to 512 slots and one exactly 512.
All inputs are finite; a program needn't handle non-finite values.
Results may differ from a plain program's by a relative error of at most 0.025.
Values may be sent and summed in bfloat16 or wider, within the bound.
No kernel may reach another device: no remote copies, remote signals or barrier semaphores. Data moves between devices by JAX's collectives and lax.ppermute only.
A program may use at most 320 MiB of HBM per device.

v0:
```python
import jax
import jax.numpy as jnp
from jax import lax
from jax.sharding import PartitionSpec as P

HEADDIM = 64


def passed_along(block, axis, distance):
    devices = range(lax.axis_size(axis))
    route = [(i - distance, i) for i in devices if i - distance in devices]
    return lax.ppermute(block, axis, route)


def as_sent(shard):
    return jax.tree.map(lambda a: a.astype(jnp.bfloat16) if a.dtype == jnp.float32 else a, shard)


def product(left, right):
    return jnp.dot(left, right, preferred_element_type=jnp.float32)


def times_transpose(left, right):
    return lax.dot_general(
        left, right, (((1,), (1,)), ((), ())), preferred_element_type=jnp.float32
    )


def transpose_times(left, right):
    return lax.dot_general(
        left, right, (((0,), (0,)), ((), ())), preferred_element_type=jnp.float32
    )


def layer_norm(value, gain_vec):
    center = value - jnp.mean(value, -1, keepdims=True)
    spread = jnp.mean(center * center, -1, keepdims=True)
    return center * lax.rsqrt(spread + 1e-05) * gain_vec


def gelu_exact(value):
    return jax.nn.gelu(value, approximate=False)


def gelu_slope(value, grad_in):
    return jax.vjp(gelu_exact, value)[1](grad_in)[0]


def norm_backward(pre_norm, gain_vec, grad_in):
    return jax.vjp(lambda v: layer_norm(v, gain_vec), pre_norm)[1](grad_in)[0]


def block_mask(row_seg, col_seg, causal, first_row, block_rows):
    same_doc = row_seg[first_row : first_row + block_rows][:, None] == col_seg[None, :]
    row_pos = first_row + jnp.arange(block_rows)
    col_pos = jnp.arange(col_seg.shape[0])
    not_ahead = row_pos[:, None] >= col_pos[None, :]
    return same_doc & (not_ahead | jnp.logical_not(causal))


def attend_forward(queries, key_rows, value_rows, row_seg, col_seg, causal):
    query_count, head_cols = queries.shape
    heads_here = head_cols // HEADDIM
    score_scale = HEADDIM ** (-0.5)
    key_heads = key_rows.reshape(-1, heads_here, HEADDIM)
    value_heads = value_rows.reshape(-1, heads_here, HEADDIM)
    block_rows = min(512, query_count)
    pieces = []
    lse_pieces = []
    for first_row in range(0, query_count, block_rows):
        query_heads = queries[first_row : first_row + block_rows].reshape(
            block_rows, heads_here, HEADDIM
        )
        allowed = block_mask(row_seg, col_seg, causal, first_row, block_rows)
        scores = (
            jnp.einsum("qhd,khd->hqk", query_heads, key_heads, preferred_element_type=jnp.float32)
            * score_scale
        )
        scores = jnp.where(allowed[None], scores, -1e30)
        row_peak = jnp.max(scores, -1, keepdims=True)
        exponent = jnp.exp(scores - row_peak)
        row_total = jnp.sum(exponent, -1, keepdims=True)
        attn_probs = (exponent / row_total).astype(jnp.bfloat16)
        mixed_rows = jnp.einsum(
            "hqk,khd->qhd", attn_probs, value_heads, preferred_element_type=jnp.float32
        )
        pieces.append(mixed_rows.reshape(block_rows, head_cols).astype(jnp.bfloat16))
        lse_pieces.append(row_peak + jnp.log(row_total))
    return (jnp.concatenate(pieces, 0), jnp.concatenate(lse_pieces, 1))


def attend_backward(queries, key_rows, value_rows, row_seg, col_seg, causal, row_lse, out_grad):
    query_count, head_cols = queries.shape
    heads_here = head_cols // HEADDIM
    score_scale = HEADDIM ** (-0.5)
    key_heads = key_rows.reshape(-1, heads_here, HEADDIM)
    value_heads = value_rows.reshape(-1, heads_here, HEADDIM)
    key_grad = jnp.zeros(key_heads.shape, jnp.float32)
    value_grad = jnp.zeros(value_heads.shape, jnp.float32)
    block_rows = min(512, query_count)
    query_pieces = []
    for first_row in range(0, query_count, block_rows):
        query_heads = queries[first_row : first_row + block_rows].reshape(
            block_rows, heads_here, HEADDIM
        )
        grad_heads = out_grad[first_row : first_row + block_rows].reshape(
            block_rows, heads_here, HEADDIM
        )
        allowed = block_mask(row_seg, col_seg, causal, first_row, block_rows)
        scores = (
            jnp.einsum("qhd,khd->hqk", query_heads, key_heads, preferred_element_type=jnp.float32)
            * score_scale
        )
        scores = jnp.where(allowed[None], scores, -1e30)
        attn_probs = jnp.exp(scores - row_lse[:, first_row : first_row + block_rows])
        probs_low = attn_probs.astype(jnp.bfloat16)
        prob_grad = jnp.einsum(
            "qhd,khd->hqk", grad_heads, value_heads, preferred_element_type=jnp.float32
        )
        inner_sum = jnp.sum(attn_probs * prob_grad, -1, keepdims=True)
        score_grad = (attn_probs * (prob_grad - inner_sum)).astype(jnp.bfloat16)
        query_grad = (
            jnp.einsum("hqk,khd->qhd", score_grad, key_heads, preferred_element_type=jnp.float32)
            * score_scale
        )
        query_pieces.append(query_grad.reshape(block_rows, head_cols))
        key_grad = (
            key_grad
            + jnp.einsum(
                "hqk,qhd->khd", score_grad, query_heads, preferred_element_type=jnp.float32
            )
            * score_scale
        )
        value_grad = value_grad + jnp.einsum(
            "hqk,qhd->khd", probs_low, grad_heads, preferred_element_type=jnp.float32
        )
    query_all = jnp.concatenate(query_pieces, 0).astype(jnp.bfloat16)
    return (
        query_all,
        key_grad.reshape(-1, head_cols).astype(jnp.bfloat16),
        value_grad.reshape(-1, head_cols).astype(jnp.bfloat16),
    )


def per_device(
    inputs,
    segment_ids,
    cotangent,
    norm_gains,
    cross_gain,
    self_qkv,
    self_out,
    cross_kv,
    cross_vo,
    ffn_in,
    ffn_out,
    adapter_down,
    adapter_down_bias,
    adapter_up,
    adapter_up_bias,
):
    model_width = inputs.shape[3]
    seq_rows = segment_ids.shape[2]
    section_index = lax.axis_index("section")
    is_decoder = section_index == 1
    gain_rows = norm_gains[0]
    adapt_up_bias = adapter_up_bias[0]
    qkv_weight = self_qkv[0].reshape(model_width, -1)
    out_weight = self_out[0]
    cross_first = cross_kv[0]
    cross_second = cross_vo[0]
    up_weight = ffn_in[0]
    down_weight = ffn_out[0]
    adapt_down = adapter_down[0]
    adapt_bias = adapter_down_bias[0]
    adapt_up = adapter_up[0]
    x_local = inputs[0]
    cot_local = cotangent[0]
    micro_count = x_local.shape[0]
    share_rows = x_local.shape[1]
    head_cols = qkv_weight.shape[1] // 3
    second_gain = jnp.where(is_decoder, cross_gain, gain_rows[1])

    def fwd_gather(value):
        return lax.all_gather(value, "mp", axis=0, tiled=True)

    def fwd_sum(value):
        return lax.psum_scatter(value, "mp", scatter_dimension=0, tiled=True)

    def bwd_gather(value):
        return lax.all_gather(value, "mp", axis=0, tiled=True)

    def bwd_sum(value):
        return lax.psum_scatter(
            value.astype(jnp.bfloat16), "mp", scatter_dimension=0, tiled=True
        ).astype(jnp.float32)

    def zero_grads():
        return (
            jnp.zeros(adapt_down.shape, jnp.float32),
            jnp.zeros(adapt_bias.shape, jnp.float32),
            jnp.zeros(adapt_up.shape, jnp.float32),
            jnp.zeros(adapt_up_bias.shape, jnp.float32),
        )

    def branch_partial(rows_in):
        hidden = gelu_exact(product(rows_in, up_weight)).astype(jnp.bfloat16)
        adapter_act = gelu_exact(product(rows_in, adapt_down) + adapt_bias).astype(jnp.bfloat16)
        return product(hidden, down_weight) + 4.0 * product(adapter_act, adapt_up)

    def branch_backward(rows_in, grad_rows):
        pre_hidden = product(rows_in, up_weight)
        pre_adapter = product(rows_in, adapt_down) + adapt_bias
        adapter_act = gelu_exact(pre_adapter).astype(jnp.bfloat16)
        hidden_grad = gelu_slope(pre_hidden, times_transpose(grad_rows, down_weight)).astype(
            jnp.bfloat16
        )
        adapter_grad = gelu_slope(pre_adapter, 4.0 * times_transpose(grad_rows, adapt_up)).astype(
            jnp.bfloat16
        )
        partial_sum = times_transpose(hidden_grad, up_weight) + times_transpose(
            adapter_grad, adapt_down
        )
        grad_terms = (
            transpose_times(rows_in, adapter_grad),
            jnp.sum(adapter_grad.astype(jnp.float32), 0),
            4.0 * transpose_times(adapter_act, grad_rows),
            4.0 * jnp.sum(grad_rows.astype(jnp.float32), 0),
        )
        return (partial_sum, grad_terms)

    def layer_forward(x_share, own_seg, enc_seg, kv_rows, send_kv):
        x_rows = fwd_gather(x_share.astype(jnp.bfloat16))
        packed = product(x_rows, qkv_weight).astype(jnp.bfloat16)
        queries = packed[:, :head_cols]
        key_rows = packed[:, head_cols : 2 * head_cols]
        value_rows = packed[:, 2 * head_cols :]
        self_mixed, self_lse = attend_forward(
            queries, key_rows, value_rows, own_seg, own_seg, is_decoder
        )
        first_pre = x_share + fwd_sum(product(self_mixed, out_weight))
        first = layer_norm(first_pre, gain_rows[0])
        first_rows = fwd_gather(first.astype(jnp.bfloat16))

        def cross_partial():
            cross_query = product(first_rows, cross_first).astype(jnp.bfloat16)
            cross_mixed = attend_forward(
                cross_query, kv_rows[:, :head_cols], kv_rows[:, head_cols:], own_seg, enc_seg, False
            )[0]
            return times_transpose(cross_mixed, cross_second)

        mid_part = lax.cond(is_decoder, cross_partial, lambda: branch_partial(first_rows))
        second_pre = first + fwd_sum(mid_part) + jnp.where(is_decoder, 0.0, 4.0) * adapt_up_bias
        second = layer_norm(second_pre, second_gain)
        second_rows = fwd_gather(second.astype(jnp.bfloat16))
        last_part = lax.cond(
            is_decoder,
            lambda: branch_partial(second_rows),
            lambda: jnp.zeros((seq_rows, model_width), jnp.float32),
        )
        third_pre = second + fwd_sum(last_part) + 4.0 * adapt_up_bias
        layer_out = jnp.where(is_decoder, layer_norm(third_pre, gain_rows[1]), second)
        kv_out = None
        if send_kv:

            def enc_pairs():
                return jnp.concatenate(
                    [product(second_rows, cross_first), product(second_rows, cross_second)], 1
                ).astype(jnp.bfloat16)

            kv_out = lax.cond(
                is_decoder, lambda: jnp.zeros((seq_rows, 2 * head_cols), jnp.bfloat16), enc_pairs
            )
        saved = (
            queries,
            key_rows,
            value_rows,
            self_lse,
            first_pre,
            first_rows,
            second_pre,
            second_rows,
            third_pre,
        )
        return (layer_out, kv_out, saved)

    def layer_backward(saved, own_seg, enc_seg, kv_rows, out_grad, kv_grad):
        (
            queries,
            key_rows,
            value_rows,
            self_lse,
            first_pre,
            first_rows,
            second_pre,
            second_rows,
            third_pre,
        ) = saved
        third_grad = norm_backward(third_pre, gain_rows[1], out_grad)
        last_grad_rows = bwd_gather(third_grad.astype(jnp.bfloat16))

        def enc_last():
            partial_sum = times_transpose(kv_grad[:, :head_cols], cross_first) + times_transpose(
                kv_grad[:, head_cols:], cross_second
            )
            return (partial_sum, zero_grads())

        last_partial, last_adapter = lax.cond(
            is_decoder, lambda: branch_backward(second_rows, last_grad_rows), enc_last
        )
        second_grad = jnp.where(is_decoder, third_grad, out_grad) + bwd_sum(last_partial)
        mid_grad = norm_backward(second_pre, second_gain, second_grad)
        mid_grad_rows = bwd_gather(mid_grad.astype(jnp.bfloat16))

        def dec_mid():
            cross_query = product(first_rows, cross_first).astype(jnp.bfloat16)
            kv_keys = kv_rows[:, :head_cols]
            kv_values = kv_rows[:, head_cols:]
            cross_lse = attend_forward(cross_query, kv_keys, kv_values, own_seg, enc_seg, False)[1]
            mixed_grad = product(mid_grad_rows, cross_second).astype(jnp.bfloat16)
            query_grad, key_grad, value_grad = attend_backward(
                cross_query, kv_keys, kv_values, own_seg, enc_seg, False, cross_lse, mixed_grad
            )
            return (
                times_transpose(query_grad, cross_first),
                jnp.concatenate([key_grad, value_grad], 1),
                zero_grads(),
            )

        def enc_mid():
            partial_sum, grad_terms = branch_backward(first_rows, mid_grad_rows)
            return (partial_sum, jnp.zeros((seq_rows, 2 * head_cols), jnp.bfloat16), grad_terms)

        mid_partial, kv_grad_out, mid_adapter = lax.cond(is_decoder, dec_mid, enc_mid)
        first_grad = mid_grad + bwd_sum(mid_partial)
        self_grad = norm_backward(first_pre, gain_rows[0], first_grad)
        self_grad_rows = bwd_gather(self_grad.astype(jnp.bfloat16))
        mixed_grad = times_transpose(self_grad_rows, out_weight).astype(jnp.bfloat16)
        query_grad, key_grad, value_grad = attend_backward(
            queries, key_rows, value_rows, own_seg, own_seg, is_decoder, self_lse, mixed_grad
        )
        partial_sum = times_transpose(
            jnp.concatenate([query_grad, key_grad, value_grad], 1), qkv_weight
        )
        x_grad = self_grad + bwd_sum(partial_sum)
        adapter_terms = tuple((a + b for a, b in zip(last_adapter, mid_adapter)))
        return (x_grad, kv_grad_out, adapter_terms)

    def pick_micro(micro_index):
        seg_pair = lax.dynamic_index_in_dim(segment_ids, micro_index, 1, keepdims=False)
        own_seg = lax.dynamic_index_in_dim(seg_pair, section_index, 0, keepdims=False)
        x_share = lax.dynamic_index_in_dim(x_local, micro_index, 0, keepdims=False).astype(
            jnp.float32
        )
        return (x_share, own_seg, seg_pair[0])

    def forward_step(section_step, carried):
        y_buffer, kv_cache, kv_flight = carried
        index_raw = section_step - section_index
        active = (index_raw >= 0) & (index_raw < micro_count)
        micro_index = jnp.clip(index_raw, 0, micro_count - 1)
        x_share, own_seg, enc_seg = pick_micro(micro_index)
        layer_out, kv_out, saved = layer_forward(x_share, own_seg, enc_seg, kv_flight, True)
        previous = lax.dynamic_index_in_dim(y_buffer, micro_index, 0, keepdims=False)
        y_buffer = lax.dynamic_update_index_in_dim(
            y_buffer, jnp.where(active, layer_out.astype(jnp.bfloat16), previous), micro_index, 0
        )
        cached = lax.dynamic_index_in_dim(kv_cache, micro_index, 0, keepdims=False)
        kv_cache = lax.dynamic_update_index_in_dim(
            kv_cache, jnp.where(active, kv_flight, cached), micro_index, 0
        )
        kv_flight = passed_along(kv_out, "section", 1)
        return (y_buffer, kv_cache, kv_flight)

    start_forward = (
        jnp.zeros((micro_count, share_rows, model_width), jnp.bfloat16),
        jnp.zeros((micro_count, seq_rows, 2 * head_cols), jnp.bfloat16),
        jnp.zeros((seq_rows, 2 * head_cols), jnp.bfloat16),
    )
    y_buffer, kv_cache, kv_flight = lax.fori_loop(0, micro_count + 1, forward_step, start_forward)

    def backward_step(section_step, carried):
        dx_buffer, grad_acc, kv_grad_flight = carried
        index_raw = micro_count - section_step - section_index
        active = (index_raw >= 0) & (index_raw < micro_count)
        micro_index = jnp.clip(index_raw, 0, micro_count - 1)
        x_share, own_seg, enc_seg = pick_micro(micro_index)
        kv_rows = lax.dynamic_index_in_dim(kv_cache, micro_index, 0, keepdims=False)
        saved = layer_forward(x_share, own_seg, enc_seg, kv_rows, False)[2]
        out_grad = lax.dynamic_index_in_dim(cot_local, micro_index, 0, keepdims=False).astype(
            jnp.float32
        )
        x_grad, kv_grad_out, adapter_terms = layer_backward(
            saved, own_seg, enc_seg, kv_rows, out_grad, kv_grad_flight
        )
        weight_on = active.astype(jnp.float32)
        adapter_terms = tuple((g * weight_on for g in adapter_terms))
        grad_acc = tuple((a + g for a, g in zip(grad_acc, adapter_terms)))
        previous = lax.dynamic_index_in_dim(dx_buffer, micro_index, 0, keepdims=False)
        dx_buffer = lax.dynamic_update_index_in_dim(
            dx_buffer, jnp.where(active, x_grad, previous), micro_index, 0
        )
        kv_grad_flight = passed_along(as_sent(kv_grad_out), "section", -1).astype(kv_grad_out.dtype)
        return (dx_buffer, grad_acc, kv_grad_flight)

    start_backward = (
        jnp.zeros((micro_count, share_rows, model_width), jnp.float32),
        zero_grads(),
        jnp.zeros((seq_rows, 2 * head_cols), jnp.bfloat16),
    )
    dx_buffer, grad_acc, kv_grad_flight = lax.fori_loop(
        0, micro_count + 1, backward_step, start_backward
    )
    totals = (
        lax.psum(grad_acc[0].astype(jnp.bfloat16), "dp").astype(jnp.float32),
        lax.psum(grad_acc[1].astype(jnp.bfloat16), "dp").astype(jnp.float32),
        lax.psum(grad_acc[2].astype(jnp.bfloat16), "dp").astype(jnp.float32),
        lax.psum(grad_acc[3].astype(jnp.bfloat16), "dp").astype(jnp.float32),
    )
    down_total = totals[0]
    bias_total = totals[1]
    up_total = totals[2]
    return (
        y_buffer[None],
        dx_buffer[None],
        down_total[None],
        bias_total[None],
        up_total[None],
        totals[3][None],
    )


def solution(mesh):
    in_specs = (
        P("section", "dp", "mp", None),
        P(None, "dp", None),
        P("section", "dp", "mp", None),
        P("section", None, None),
        P(),
        P("section", None, None, "mp"),
        P("section", "mp", None),
        P("section", None, "mp"),
        P("section", None, "mp"),
        P("section", None, "mp"),
        P("section", "mp", None),
        P("section", None, "mp"),
        P("section", "mp"),
        P("section", "mp", None),
        P("section", None),
    )
    out_specs = (
        P("section", "dp", "mp", None),
        P("section", "dp", "mp", None),
        P("section", None, "mp"),
        P("section", "mp"),
        P("section", "mp", None),
        P("section", None),
    )
    return jax.shard_map(
        per_device, mesh=mesh, in_specs=in_specs, out_specs=out_specs, check_vma=False
    )
```

profile of v0, /device:TPU:0, one launch (start us, length us, event | category | flops | bytes accessed | tf_op | source)
XLA Modules:
  0.0 4277.1 jit_solution(10851905690660336519)
XLA Ops:
  21.2 1298.0 %while.47 = (s32[]{:T(128)}, bf16[2,512,1024]{2,1,0:T(8,128)(2,1)}, bf16[2,1024,1024]{1,2,0:T(8,128)(2,1)}, bf16[1024,1024]{0,1:T(8,128)(2,1)}, s32[]{:T(128)}, ...) while((s32[]{:T(128)}, bf16[2,512,1024]{2,1,0:T(8,128)(2,1)}, ...), condition=%wide.region_24.25_spmd, body=%wide.region_0.24_spmd.sunk | while | flops 28318371840 | bytes 440800064 | solution.py:380
  255.4 63.2 %reduce-scatter.12.cloned.1.call-done = f32[512,1024]{1,0:T(8,128)} async-done(((f32[1024,1024]{1,0:T(8,128)}), f32[512,1024]{1,0:T(8,128)}) %reduce-scatter.12.cloned.1.call-update) | async-done | bytes 2097168 | tf_op jit(solution)/shard_map/while/body/eval_jaxpr/reduce_scatter | solution.py:188
  686.4 63.7 %reduce-scatter.12.cloned.1.call-done = f32[512,1024]{1,0:T(8,128)} async-done(((f32[1024,1024]{1,0:T(8,128)}), f32[512,1024]{1,0:T(8,128)}) %reduce-scatter.12.cloned.1.call-update) | async-done | bytes 2097168 | tf_op jit(solution)/shard_map/while/body/eval_jaxpr/reduce_scatter | solution.py:188
  1117.7 63.5 %reduce-scatter.12.cloned.1.call-done = f32[512,1024]{1,0:T(8,128)} async-done(((f32[1024,1024]{1,0:T(8,128)}), f32[512,1024]{1,0:T(8,128)}) %reduce-scatter.12.cloned.1.call-update) | async-done | bytes 2097168 | tf_op jit(solution)/shard_map/while/body/eval_jaxpr/reduce_scatter | solution.py:188
  1323.4 2858.7 %while.48 = (s32[]{:T(128)}, f32[2,512,1024]{2,1,0:T(8,128)}, f32[1024,256]{0,1:T(8,128)}, f32[256]{0:T(256)}, f32[256,1024]{1,0:T(8,128)}, /*index=5*/f32[1024]...) while((s32[]{:T(128)}, f32[2,512,1024]{2,1,0:T(8,128)}, ...), condition=%wide.region_72.73_spmd.clone, body=%wide.region_25.72_spmd.clone.sunk | while | flops 66413662208 | bytes 1761810432 | solution.py:411
  1406.9 53.8 %reduce-scatter.16.cloned.1.call-done = f32[512,1024]{1,0:T(8,128)} async-done(((f32[1024,1024]{1,0:T(8,128)}), f32[512,1024]{1,0:T(8,128)}) %reduce-scatter.16.cloned.1.call-update) | async-done | bytes 2097168 | tf_op jit(solution)/shard_map/while/body/eval_jaxpr/reduce_scatter | solution.py:188
  1547.4 76.9 %reduce-scatter.18.cloned.1.call-done = f32[512,1024]{1,0:T(8,128)} async-done(((f32[1024,1024]{1,0:T(8,128)}), f32[512,1024]{1,0:T(8,128)}) %reduce-scatter.18.cloned.1.call-update) | async-done | bytes 2097168 | tf_op jit(solution)/shard_map/while/body/eval_jaxpr/reduce_scatter | solution.py:188
  1672.9 83.2 %reduce-scatter.20.cloned.1.call-done = f32[512,1024]{1,0:T(8,128)} async-done(((f32[1024,1024]{1,0:T(8,128)}), f32[512,1024]{1,0:T(8,128)}) %reduce-scatter.20.cloned.1.call-update) | async-done | bytes 2097168 | tf_op jit(solution)/shard_map/while/body/eval_jaxpr/reduce_scatter | solution.py:188
  1820.2 71.7 %reduce-scatter.22.cloned.1.call-done = bf16[512,1024]{1,0:T(8,128)(2,1)} async-done(((bf16[1024,1024]{1,0:T(8,128)(2,1)}), bf16[512,1024]{1,0:T(8,128)(2,1)}) %reduce-scatter.22.cloned.1.call-update) | async-done | bytes 1048592 | tf_op jit(solution)/shard_map/while/body/eval_jaxpr/reduce_scatter | solution.py:194
  1934.1 76.5 %conditional.24 = (bf16[1024,1024]{1,0:T(8,128)(2,1)}, bf16[1024,1024]{1,0:T(8,128)(2,1)}, f32[1024,256]{0,1:T(8,128)}, f32[256]{0:T(256)S(1)}, f32[256,1024]{1,0:T(8,128)}, /*index=5*/f32[1024]{0:T(1024)}) conditional(s32[]{:T(128)} %convert_element_type.871, (bf16[1024,1024]{1,0:T(8,128)(2,1)}, bf16[1024,2048]{1,0:T(8,128)(2,1)}, ...), branch_computations={%region_56.58_spmd, %region_59.65_spmd} | conditional | flops 15761670144 | bytes 546821568 | solution.py:334
  2010.7 88.8 %reduce-scatter.24.cloned.1.call-done = bf16[512,1024]{1,0:T(8,128)(2,1)} async-done(((bf16[1024,1024]{1,0:T(8,128)(2,1)}), bf16[512,1024]{1,0:T(8,128)(2,1)}) %reduce-scatter.24.cloned.1.call-update) | async-done | bytes 1048592 | tf_op jit(solution)/shard_map/while/body/eval_jaxpr/reduce_scatter | solution.py:194
  2357.8 53.8 %reduce-scatter.16.cloned.1.call-done = f32[512,1024]{1,0:T(8,128)} async-done(((f32[1024,1024]{1,0:T(8,128)}), f32[512,1024]{1,0:T(8,128)}) %reduce-scatter.16.cloned.1.call-update) | async-done | bytes 2097168 | tf_op jit(solution)/shard_map/while/body/eval_jaxpr/reduce_scatter | solution.py:188
  2498.5 76.8 %reduce-scatter.18.cloned.1.call-done = f32[512,1024]{1,0:T(8,128)} async-done(((f32[1024,1024]{1,0:T(8,128)}), f32[512,1024]{1,0:T(8,128)}) %reduce-scatter.18.cloned.1.call-update) | async-done | bytes 2097168 | tf_op jit(solution)/shard_map/while/body/eval_jaxpr/reduce_scatter | solution.py:188
  2623.9 83.2 %reduce-scatter.20.cloned.1.call-done = f32[512,1024]{1,0:T(8,128)} async-done(((f32[1024,1024]{1,0:T(8,128)}), f32[512,1024]{1,0:T(8,128)}) %reduce-scatter.20.cloned.1.call-update) | async-done | bytes 2097168 | tf_op jit(solution)/shard_map/while/body/eval_jaxpr/reduce_scatter | solution.py:188
  2771.1 71.7 %reduce-scatter.22.cloned.1.call-done = bf16[512,1024]{1,0:T(8,128)(2,1)} async-done(((bf16[1024,1024]{1,0:T(8,128)(2,1)}), bf16[512,1024]{1,0:T(8,128)(2,1)}) %reduce-scatter.22.cloned.1.call-update) | async-done | bytes 1048592 | tf_op jit(solution)/shard_map/while/body/eval_jaxpr/reduce_scatter | solution.py:194
  2885.0 76.5 %conditional.24 = (bf16[1024,1024]{1,0:T(8,128)(2,1)}, bf16[1024,1024]{1,0:T(8,128)(2,1)}, f32[1024,256]{0,1:T(8,128)}, f32[256]{0:T(256)S(1)}, f32[256,1024]{1,0:T(8,128)}, /*index=5*/f32[1024]{0:T(1024)}) conditional(s32[]{:T(128)} %convert_element_type.871, (bf16[1024,1024]{1,0:T(8,128)(2,1)}, bf16[1024,2048]{1,0:T(8,128)(2,1)}, ...), branch_computations={%region_56.58_spmd, %region_59.65_spmd} | conditional | flops 15761670144 | bytes 546821568 | solution.py:334
  2961.7 88.8 %reduce-scatter.24.cloned.1.call-done = bf16[512,1024]{1,0:T(8,128)(2,1)} async-done(((bf16[1024,1024]{1,0:T(8,128)(2,1)}), bf16[512,1024]{1,0:T(8,128)(2,1)}) %reduce-scatter.24.cloned.1.call-update) | async-done | bytes 1048592 | tf_op jit(solution)/shard_map/while/body/eval_jaxpr/reduce_scatter | solution.py:194
  3308.8 53.8 %reduce-scatter.16.cloned.1.call-done = f32[512,1024]{1,0:T(8,128)} async-done(((f32[1024,1024]{1,0:T(8,128)}), f32[512,1024]{1,0:T(8,128)}) %reduce-scatter.16.cloned.1.call-update) | async-done | bytes 2097168 | tf_op jit(solution)/shard_map/while/body/eval_jaxpr/reduce_scatter | solution.py:188
  3449.5 76.8 %reduce-scatter.18.cloned.1.call-done = f32[512,1024]{1,0:T(8,128)} async-done(((f32[1024,1024]{1,0:T(8,128)}), f32[512,1024]{1,0:T(8,128)}) %reduce-scatter.18.cloned.1.call-update) | async-done | bytes 2097168 | tf_op jit(solution)/shard_map/while/body/eval_jaxpr/reduce_scatter | solution.py:188
  3574.8 83.2 %reduce-scatter.20.cloned.1.call-done = f32[512,1024]{1,0:T(8,128)} async-done(((f32[1024,1024]{1,0:T(8,128)}), f32[512,1024]{1,0:T(8,128)}) %reduce-scatter.20.cloned.1.call-update) | async-done | bytes 2097168 | tf_op jit(solution)/shard_map/while/body/eval_jaxpr/reduce_scatter | solution.py:188
  3722.1 71.7 %reduce-scatter.22.cloned.1.call-done = bf16[512,1024]{1,0:T(8,128)(2,1)} async-done(((bf16[1024,1024]{1,0:T(8,128)(2,1)}), bf16[512,1024]{1,0:T(8,128)(2,1)}) %reduce-scatter.22.cloned.1.call-update) | async-done | bytes 1048592 | tf_op jit(solution)/shard_map/while/body/eval_jaxpr/reduce_scatter | solution.py:194
  3836.0 76.5 %conditional.24 = (bf16[1024,1024]{1,0:T(8,128)(2,1)}, bf16[1024,1024]{1,0:T(8,128)(2,1)}, f32[1024,256]{0,1:T(8,128)}, f32[256]{0:T(256)S(1)}, f32[256,1024]{1,0:T(8,128)}, /*index=5*/f32[1024]{0:T(1024)}) conditional(s32[]{:T(128)} %convert_element_type.871, (bf16[1024,1024]{1,0:T(8,128)(2,1)}, bf16[1024,2048]{1,0:T(8,128)(2,1)}, ...), branch_computations={%region_56.58_spmd, %region_59.65_spmd} | conditional | flops 15761670144 | bytes 546821568 | solution.py:334
  3912.7 88.8 %reduce-scatter.24.cloned.1.call-done = bf16[512,1024]{1,0:T(8,128)(2,1)} async-done(((bf16[1024,1024]{1,0:T(8,128)(2,1)}), bf16[512,1024]{1,0:T(8,128)(2,1)}) %reduce-scatter.24.cloned.1.call-update) | async-done | bytes 1048592 | tf_op jit(solution)/shard_map/while/body/eval_jaxpr/reduce_scatter | solution.py:194
  4211.3 54.0 %all-reduce.4.cloned.1.call-done = (bf16[1,1024,256]{2,1,0:T(8,128)(2,1)}, bf16[1,256,1024]{2,1,0:T(8,128)(2,1)}) async-done(((bf16[1,1024,256]{2,1,0:T(8,128)(2,1)}, bf16[1,256,1024]{2,1,0:T(8,128)(2,1)}), (bf16[1,1024,256]{2,1,0:T(8,128)(2,1)}, bf16[1,256,1024]{2,1,0:T(8,128)(2,1)})) %all-reduce.4.cloned.1.call-update) | async-done | bytes 1048592 | tf_op jit(solution)/shard_map/psum | solution.py:415
  (1149 shorter events, 3131.1 us)
Async XLA Ops:
  23.9 141.1 %reduce-scatter.10.cloned.1.call-start = ((), (), s32[]{:S(2)}) async-start(), calls=%async_computation.11 | async-start | bytes 6291456 | tf_op jit(solution)/shard_map/while/body/eval_jaxpr/reduce_scatter | solution.py:188
  172.7 145.9 %reduce-scatter.12.cloned.1.call-start = ((), (), s32[]{:S(2)}) async-start(), calls=%async_computation.13 | async-start | bytes 6291456 | tf_op jit(solution)/shard_map/while/body/eval_jaxpr/reduce_scatter | solution.py:188
  457.9 138.3 %reduce-scatter.10.cloned.1.call-start = ((), (), s32[]{:S(2)}) async-start(), calls=%async_computation.11 | async-start | bytes 6291456 | tf_op jit(solution)/shard_map/while/body/eval_jaxpr/reduce_scatter | solution.py:188
  604.0 146.1 %reduce-scatter.12.cloned.1.call-start = ((), (), s32[]{:S(2)}) async-start(), calls=%async_computation.13 | async-start | bytes 6291456 | tf_op jit(solution)/shard_map/while/body/eval_jaxpr/reduce_scatter | solution.py:188
  889.2 138.3 %reduce-scatter.10.cloned.1.call-start = ((), (), s32[]{:S(2)}) async-start(), calls=%async_computation.11 | async-start | bytes 6291456 | tf_op jit(solution)/shard_map/while/body/eval_jaxpr/reduce_scatter | solution.py:188
  1035.2 146.0 %reduce-scatter.12.cloned.1.call-start = ((), (), s32[]{:S(2)}) async-start(), calls=%async_computation.13 | async-start | bytes 6291456 | tf_op jit(solution)/shard_map/while/body/eval_jaxpr/reduce_scatter | solution.py:188
  1330.4 130.3 %reduce-scatter.16.cloned.1.call-start = ((), (), s32[]{:S(2)}) async-start(), calls=%async_computation.17 | async-start | bytes 6291456 | tf_op jit(solution)/shard_map/while/body/eval_jaxpr/reduce_scatter | solution.py:188
  1464.5 159.8 %reduce-scatter.18.cloned.1.call-start = ((), (), s32[]{:S(2)}) async-start(), calls=%async_computation.19 | async-start | bytes 6291456 | tf_op jit(solution)/shard_map/while/body/eval_jaxpr/reduce_scatter | solution.py:188
  1763.7 128.2 %reduce-scatter.22.cloned.1.call-start = ((), (), s32[]{:S(2)}) async-start(), calls=%async_computation.23 | async-start | bytes 3145728 | tf_op jit(solution)/shard_map/while/body/eval_jaxpr/reduce_scatter | solution.py:194
  1900.8 198.6 %reduce-scatter.24.cloned.1.call-start = ((), (), s32[]{:S(2)}) async-start(), calls=%async_computation.25 | async-start | bytes 3145728 | tf_op jit(solution)/shard_map/while/body/eval_jaxpr/reduce_scatter | solution.py:194
  2010.6 131.4 %all-gather.33.cloned.1.call-start = ((), (), s32[]{:S(2)}) async-start(), calls=%async_computation.26 | async-start | bytes 3145728 | tf_op jit(solution)/shard_map/while/body/eval_jaxpr/all_gather | solution.py:191
  2108.8 166.2 %reduce-scatter.26.cloned.1.call-start = ((), (), s32[]{:S(2)}) async-start(), calls=%async_computation.27 | async-start | bytes 3145728 | tf_op jit(solution)/shard_map/while/body/eval_jaxpr/reduce_scatter | solution.py:194
  2281.3 130.3 %reduce-scatter.16.cloned.1.call-start = ((), (), s32[]{:S(2)}) async-start(), calls=%async_computation.17 | async-start | bytes 6291456 | tf_op jit(solution)/shard_map/while/body/eval_jaxpr/reduce_scatter | solution.py:188
  2415.4 159.8 %reduce-scatter.18.cloned.1.call-start = ((), (), s32[]{:S(2)}) async-start(), calls=%async_computation.19 | async-start | bytes 6291456 | tf_op jit(solution)/shard_map/while/body/eval_jaxpr/reduce_scatter | solution.py:188
  2714.6 128.2 %reduce-scatter.22.cloned.1.call-start = ((), (), s32[]{:S(2)}) async-start(), calls=%async_computation.23 | async-start | bytes 3145728 | tf_op jit(solution)/shard_map/while/body/eval_jaxpr/reduce_scatter | solution.py:194
  2851.8 198.7 %reduce-scatter.24.cloned.1.call-start = ((), (), s32[]{:S(2)}) async-start(), calls=%async_computation.25 | async-start | bytes 3145728 | tf_op jit(solution)/shard_map/while/body/eval_jaxpr/reduce_scatter | solution.py:194
  2961.6 131.4 %all-gather.33.cloned.1.call-start = ((), (), s32[]{:S(2)}) async-start(), calls=%async_computation.26 | async-start | bytes 3145728 | tf_op jit(solution)/shard_map/while/body/eval_jaxpr/all_gather | solution.py:191
  3059.7 166.2 %reduce-scatter.26.cloned.1.call-start = ((), (), s32[]{:S(2)}) async-start(), calls=%async_computation.27 | async-start | bytes 3145728 | tf_op jit(solution)/shard_map/while/body/eval_jaxpr/reduce_scatter | solution.py:194
  3232.3 130.3 %reduce-scatter.16.cloned.1.call-start = ((), (), s32[]{:S(2)}) async-start(), calls=%async_computation.17 | async-start | bytes 6291456 | tf_op jit(solution)/shard_map/while/body/eval_jaxpr/reduce_scatter | solution.py:188
  3366.4 159.8 %reduce-scatter.18.cloned.1.call-start = ((), (), s32[]{:S(2)}) async-start(), calls=%async_computation.19 | async-start | bytes 6291456 | tf_op jit(solution)/shard_map/while/body/eval_jaxpr/reduce_scatter | solution.py:188
  3665.6 128.2 %reduce-scatter.22.cloned.1.call-start = ((), (), s32[]{:S(2)}) async-start(), calls=%async_computation.23 | async-start | bytes 3145728 | tf_op jit(solution)/shard_map/while/body/eval_jaxpr/reduce_scatter | solution.py:194
  3802.8 198.7 %reduce-scatter.24.cloned.1.call-start = ((), (), s32[]{:S(2)}) async-start(), calls=%async_computation.25 | async-start | bytes 3145728 | tf_op jit(solution)/shard_map/while/body/eval_jaxpr/reduce_scatter | solution.py:194
  3912.6 131.4 %all-gather.33.cloned.1.call-start = ((), (), s32[]{:S(2)}) async-start(), calls=%async_computation.26 | async-start | bytes 3145728 | tf_op jit(solution)/shard_map/while/body/eval_jaxpr/all_gather | solution.py:191
  4010.7 166.2 %reduce-scatter.26.cloned.1.call-start = ((), (), s32[]{:S(2)}) async-start(), calls=%async_computation.27 | async-start | bytes 3145728 | tf_op jit(solution)/shard_map/while/body/eval_jaxpr/reduce_scatter | solution.py:194
  (309 other events, 14609.8 us)
Sparse Core Ops, SparseCore 0:
  110.6 54.3 reduce-scatter.9
  255.4 63.1 reduce-scatter.11
  364.5 86.0 reduce-scatter.13
  541.9 54.3 reduce-scatter.9
  686.5 63.5 reduce-scatter.11
  796.0 85.8 reduce-scatter.13
  973.2 54.2 reduce-scatter.9
  1117.7 63.3 reduce-scatter.11
  1227.0 86.0 reduce-scatter.13
  1406.3 54.2 reduce-scatter.15
  1547.5 76.7 reduce-scatter.17
  1673.0 83.0 reduce-scatter.19
  1820.2 71.6 reduce-scatter.21
  2010.7 88.6 reduce-scatter.23
  2357.2 54.2 reduce-scatter.15
  2498.5 76.6 reduce-scatter.17
  2623.9 83.0 reduce-scatter.19
  2771.2 71.6 reduce-scatter.21
  2961.7 88.6 reduce-scatter.23
  3308.2 54.2 reduce-scatter.15
  3449.5 76.6 reduce-scatter.17
  3574.9 83.0 reduce-scatter.19
  3722.2 71.6 reduce-scatter.21
  3912.7 88.6 reduce-scatter.23
  (30 shorter events, 990.6 us)
Sparse Core Ops, SparseCore 1:
  4186.8 78.4 all-reduce.3
where the time goes:
time: 4280 us
  waiting for transfers between devices  2570 us (60%)
  matrix products  882 us (21%)
  other arithmetic  318 us (7%)
  loops' own time  186 us (4%)
  local copies, waits for them, and re-layouts  185 us (4%)
  starting transfers between devices  95 us (2%)
    reduce_scatter x18, waiting for transfers between devices, fwd_sum(): return lax.psum_scatter(value, 'mp', scatter_dimension=0, tiled=True)  1110 us
    all_gather x18, waiting for transfers between devices, fwd_gather(): return lax.all_gather(value, 'mp', axis=0, tiled=True)  571 us
    reduce_scatter x9, waiting for transfers between devices, bwd_sum(): lax.psum_scatter(value.astype(jnp.bfloat16), 'mp', scatter_dimension=0, t...  542 us
    dot_general x36, matrix products, product(): return jnp.dot(left, right, preferred_element_type=jnp.float32)  335 us
    all_gather x9, waiting for transfers between devices, bwd_gather(): return lax.all_gather(value, 'mp', axis=0, tiled=True)  297 us
    dot_general x21, matrix products, times_transpose(): lax.dot_general(left, right, (((1,), (1,)), ((), ())), preferred_element_...  191 us
    ppermute x6, starting transfers between devices, passed_along(): return lax.ppermute(block, axis, route)  92.7 us
  transfers between devices with their start and end apart: 61, of which 55 were waited for; matrix products, arithmetic and copies ran while one was open for 3% of the time, Pallas kernels for 0%

commit v1 on v0

v1 whole, which is shorter than its diff:
```python
import functools

import jax
import jax.numpy as jnp
from jax import lax
from jax.experimental import pallas as pl
from jax.experimental.pallas import tpu as pltpu
from jax.sharding import PartitionSpec as P

HEADDIM = 64
BUNCH = 4
WIDE = BUNCH * HEADDIM
CHUNK = 512
SCALE = HEADDIM**-0.5
HIDDEN_MASK = -1e30
VMEM_LIMIT = 60 * 1024 * 1024
BF16 = jnp.bfloat16
F32 = jnp.float32


def dot_nn(left, right):
    return lax.dot_general(left, right, (((1,), (0,)), ((), ())), preferred_element_type=F32)


def dot_nt(left, right):
    return lax.dot_general(left, right, (((1,), (1,)), ((), ())), preferred_element_type=F32)


def dot_tn(left, right):
    return lax.dot_general(left, right, (((0,), (0,)), ((), ())), preferred_element_type=F32)


class Stream:
    def __init__(self, parts, cut, count):
        self.parts = parts
        self.cut = cut
        self.count = count

    @property
    def arrays(self):
        return [a for part in self.parts for a in part]


def column_cut(width):
    return lambda ref, k: ref.at[:, pl.ds(pl.multiple_of(k * width, width), width)]


def row_cut(width):
    return lambda ref, k: ref.at[pl.ds(pl.multiple_of(k * width, width), width), :]


def stack_cut(width):
    return lambda ref, k: ref.at[:, :, pl.ds(pl.multiple_of(k * width, width), width)]


def issue(stream, refs, buf, sem, layer, step, slot):
    mine = lax.axis_index("section") == layer
    base = 0
    for i in range(len(stream.parts)):
        own, other = refs[2 * i], refs[2 * i + 1]
        here = (step >= base) & (step < base + stream.count)
        k = jnp.clip(step - base, 0, stream.count - 1)

        @pl.when(here & mine)
        def _():
            pltpu.make_async_copy(stream.cut(own, k), buf.at[slot], sem.at[slot]).start()

        @pl.when(here & jnp.logical_not(mine))
        def _():
            pltpu.make_async_copy(stream.cut(other, k), buf.at[slot], sem.at[slot]).start()

        base += stream.count


def await_chunk(stream, refs, buf, sem, slot):
    pltpu.make_async_copy(stream.cut(refs[0], 0), buf.at[slot], sem.at[slot]).wait()


def advance(streams, stream_refs, bufs, sems, layer, step, steps):
    slot = lax.rem(step, 2)

    @pl.when(step == 0)
    def _():
        for s, r, b, m in zip(streams, stream_refs, bufs, sems):
            issue(s, r, b, m, layer, 0, 0)

    @pl.when(step + 1 < steps)
    def _():
        for s, r, b, m in zip(streams, stream_refs, bufs, sems):
            issue(s, r, b, m, layer, step + 1, 1 - slot)

    for s, r, b, m in zip(streams, stream_refs, bufs, sems):
        await_chunk(s, r, b, m, slot)
    return slot


def call(body, steps, operands, in_blocks, streams, out_shapes, out_blocks, bufs, scratch, cost):
    arrays = [a for s in streams for a in s.arrays]
    counts = [len(s.arrays) for s in streams]
    n_ops, n_out = len(operands), len(out_shapes)

    def kernel(*refs):
        ins, rest = refs[:n_ops], refs[n_ops:]
        stream_refs = []
        for n in counts:
            stream_refs.append(rest[:n])
            rest = rest[n:]
        outs, rest = rest[:n_out], rest[n_out:]
        buf_refs, rest = rest[: len(bufs)], rest[len(bufs) :]
        sems, extra = rest[: len(bufs)], rest[len(bufs) :]
        body(ins, stream_refs, outs, buf_refs, sems, extra)

    return pl.pallas_call(
        kernel,
        grid=(steps,),
        in_specs=list(in_blocks) + [pl.BlockSpec(memory_space=pl.ANY)] * len(arrays),
        out_specs=tuple(out_blocks),
        out_shape=tuple(out_shapes),
        scratch_shapes=[pltpu.VMEM((2,) + tuple(b), BF16) for b in bufs]
        + [pltpu.SemaphoreType.DMA((2,)) for _ in bufs]
        + list(scratch),
        compiler_params=pltpu.CompilerParams(
            dimension_semantics=("arbitrary",), vmem_limit_bytes=VMEM_LIMIT
        ),
        cost_estimate=pl.CostEstimate(
            flops=int(cost), bytes_accessed=int(cost // 500), transcendentals=0
        ),
    )(*operands, *arrays)


def whole(shape):
    zeros = (0,) * len(shape)
    return pl.BlockSpec(tuple(shape), lambda i: zeros)


def per_step(shape, first=0, last=None):
    def index(i):
        k = jnp.maximum(i - first, 0)
        if last is not None:
            k = jnp.minimum(k, last)
        return (k,) + (0,) * len(shape)

    return pl.BlockSpec((1,) + tuple(shape), index)


def shaped(shape, dtype):
    return jax.ShapeDtypeStruct(tuple(shape), dtype)


def normalized(value):
    center = value - jnp.mean(value, -1, keepdims=True)
    spread = jnp.mean(center * center, -1, keepdims=True)
    inverse = lax.rsqrt(spread + 1e-05)
    return center * inverse, inverse


def norm_slope(grad, hat, inverse, gain):
    scaled = grad * gain
    along = jnp.mean(scaled * hat, -1, keepdims=True)
    return inverse * (scaled - jnp.mean(scaled, -1, keepdims=True) - hat * along)


def gelu_pair(value):
    below = 0.5 + 0.5 * lax.erf(value * (0.5**0.5))
    density = jnp.exp(value * value * -0.5) * 0.3989422804014327
    return value * below, below + value * density


def only_head(value, head):
    lane = lax.broadcasted_iota(jnp.int32, (1, WIDE), 1)
    keep = (lane >= head * HEADDIM) & (lane < (head + 1) * HEADDIM)
    return jnp.where(keep, value, jnp.zeros_like(value))


def attend(q, k, v, bias_ref, out_ref, block):
    rows = q.shape[0]
    scaled = q * jnp.asarray(SCALE, BF16)
    for first in range(0, rows, block):
        part = slice(first, first + block)
        total = None
        for head in range(BUNCH):
            scores = dot_nt(only_head(scaled[part], head), k) + bias_ref[part, :]
            peak = jnp.max(scores, -1, keepdims=True)
            powers = jnp.exp(scores - peak)
            share = 1.0 / jnp.sum(powers, -1, keepdims=True)
            mixed = dot_nn((powers * share).astype(BF16), only_head(v, head))
            total = mixed if total is None else total + mixed
        out_ref[part, :] = total


def attend_slope(q, k, v, grad, bias_ref, dq_ref, dk_ref, dv_ref, block):
    rows = q.shape[0]
    scaled = q * jnp.asarray(SCALE, BF16)
    for first in range(0, rows, block):
        part = slice(first, first + block)
        dq_total = None
        for head in range(BUNCH):
            q_head = only_head(scaled[part], head)
            g_head = only_head(grad[part], head)
            scores = dot_nt(k, q_head) + bias_ref[:, part]
            peak = jnp.max(scores, 0, keepdims=True)
            powers = jnp.exp(scores - peak)
            share = 1.0 / jnp.sum(powers, 0, keepdims=True)
            probs = powers * share
            prob_grad = dot_nt(v, g_head)
            inner = jnp.sum(probs * prob_grad, 0, keepdims=True)
            score_grad = (probs * (prob_grad - inner)).astype(BF16)
            dv_part = dot_nn(probs.astype(BF16), g_head)
            dk_part = dot_nn(score_grad, q_head)
            if first == 0 and head == 0:
                dv_ref[...] = dv_part
                dk_ref[...] = dk_part
            else:
                dv_ref[...] += dv_part
                dk_ref[...] += dk_part
            dq_part = dot_tn(score_grad, only_head(k, head))
            dq_total = dq_part if dq_total is None else dq_total + dq_part
        dq_ref[part, :] = dq_total * SCALE


def fill_bias(bias_ref, row_seg, col_seg, order):
    seen = row_seg == col_seg
    if order:
        shape = bias_ref.shape
        r = lax.broadcasted_iota(jnp.int32, shape, 0)
        c = lax.broadcasted_iota(jnp.int32, shape, 1)
        seen = seen & ((c <= r) if order == 1 else (r <= c))
    bias_ref[...] = jnp.where(seen, 0.0, HIDDEN_MASK)


def self_forward(layer, x, seg_col, seg_row, gain, qkv, out):
    rows, width = x.shape
    steps = len(qkv.parts) * qkv.count

    def body(ins, wrefs, outs, bufs, sems, extra):
        x_ref, segc_ref, segr_ref, gain_ref = ins
        qkv_ref, hat_ref, inv_ref = outs
        acc, bias, mixed = extra
        step = pl.program_id(0)
        slot = advance((qkv, out), wrefs, bufs, sems, layer, step, steps)

        @pl.when(step == 0)
        def _():
            fill_bias(bias, segc_ref[...], segr_ref[...], 1 if layer == 1 else 0)
            acc[...] = x_ref[...].astype(F32)

        x_rows = x_ref[...]
        w = bufs[0].at[slot]
        q = dot_nn(x_rows, w[0]).astype(BF16)
        k = dot_nn(x_rows, w[1]).astype(BF16)
        v = dot_nn(x_rows, w[2]).astype(BF16)
        qkv_ref[0, 0] = q
        qkv_ref[0, 1] = k
        qkv_ref[0, 2] = v
        attend(q, k, v, bias, mixed, 256)
        acc[...] += dot_nn(mixed[...].astype(BF16), bufs[1][slot])

        @pl.when(step == steps - 1)
        def _():
            hat, inverse = normalized(acc[...])
            hat_ref[...] = hat.astype(BF16)
            inv_ref[...] = inverse

    return call(
        body,
        steps,
        [x, seg_col, seg_row, gain],
        [whole(x.shape), whole(seg_col.shape), whole(seg_row.shape), whole(gain.shape)],
        [qkv, out],
        [shaped((steps, 3, rows, WIDE), BF16), shaped((rows, width), BF16), shaped((rows, 1), F32)],
        [per_step((3, rows, WIDE)), whole((rows, width)), whole((rows, 1))],
        [(3, width, WIDE), (WIDE, width)],
        [
            pltpu.VMEM((rows, width), F32),
            pltpu.VMEM((rows, rows), F32),
            pltpu.VMEM((rows, WIDE), F32),
        ],
        steps * (2 * rows * width * WIDE * 4 + 16 * rows * rows * WIDE),
    )


def self_backward(layer, grad, saved, seg_col, seg_row, qkv, out):
    rows, width = grad.shape
    steps = len(qkv.parts) * qkv.count

    def body(ins, wrefs, outs, bufs, sems, extra):
        g_ref, saved_ref, segc_ref, segr_ref = ins
        (dx_ref,) = outs
        acc, bias, dq, dk, dv = extra
        step = pl.program_id(0)
        slot = advance((qkv, out), wrefs, bufs, sems, layer, step, steps)

        @pl.when(step == 0)
        def _():
            fill_bias(bias, segc_ref[...], segr_ref[...], 2 if layer == 1 else 0)
            acc[...] = g_ref[...].astype(F32)

        mixed_grad = dot_nt(g_ref[...], bufs[1][slot]).astype(BF16)
        attend_slope(
            saved_ref[0, 0], saved_ref[0, 1], saved_ref[0, 2], mixed_grad, bias, dq, dk, dv, 256
        )
        w = bufs[0].at[slot]
        acc[...] += (
            dot_nt(dq[...].astype(BF16), w[0])
            + dot_nt(dk[...].astype(BF16), w[1])
            + dot_nt(dv[...].astype(BF16), w[2])
        )

        @pl.when(step == steps - 1)
        def _():
            dx_ref[...] = acc[...].astype(BF16)

    return call(
        body,
        steps,
        [grad, saved, seg_col, seg_row],
        [whole(grad.shape), per_step((3, rows, WIDE)), whole(seg_col.shape), whole(seg_row.shape)],
        [qkv, out],
        [shaped((rows, width), BF16)],
        [whole((rows, width))],
        [(3, width, WIDE), (WIDE, width)],
        [
            pltpu.VMEM((rows, width), F32),
            pltpu.VMEM((rows, rows), F32),
            pltpu.VMEM((rows, WIDE), F32),
            pltpu.VMEM((rows, WIDE), F32),
            pltpu.VMEM((rows, WIDE), F32),
        ],
        steps * (2 * rows * width * WIDE * 4 + 40 * rows * rows * WIDE),
    )[0]


def cross_forward(hat, gain, kv_own, kv_away, seg_col, keys_row, query_w, out_w):
    rows, width = hat.shape
    steps = len(query_w.parts) * query_w.count

    def body(ins, wrefs, outs, bufs, sems, extra):
        hat_ref, gain_ref, own_ref, away_ref, segc_ref, keysr_ref = ins
        q_ref, nhat_ref, inv_ref = outs
        acc, low, bias, mixed, keys, values = extra
        step = pl.program_id(0)
        slot = advance((query_w, out_w), wrefs, bufs, sems, 1, step, steps)

        @pl.when(step == 0)
        def _():
            fill_bias(bias, segc_ref[...], keysr_ref[...], 0)
            first = hat_ref[...].astype(F32) * gain_ref[...]
            acc[...] = first
            low[...] = first.astype(BF16)

        q = dot_nn(low[...], bufs[0][slot]).astype(BF16)
        q_ref[0] = q
        keys[:rows] = own_ref[0, 0]
        keys[rows:] = away_ref[0, 0]
        values[:rows] = own_ref[0, 1]
        values[rows:] = away_ref[0, 1]
        attend(q, keys[...], values[...], bias, mixed, 256)
        acc[...] += dot_nt(mixed[...].astype(BF16), bufs[1][slot])

        @pl.when(step == steps - 1)
        def _():
            nhat, inverse = normalized(acc[...])
            nhat_ref[...] = nhat.astype(BF16)
            inv_ref[...] = inverse

    return call(
        body,
        steps,
        [hat, gain, kv_own, kv_away, seg_col, keys_row],
        [
            whole(hat.shape),
            whole(gain.shape),
            per_step((2, rows, WIDE)),
            per_step((2, rows, WIDE)),
            whole(seg_col.shape),
            whole(keys_row.shape),
        ],
        [query_w, out_w],
        [shaped((steps, rows, WIDE), BF16), shaped((rows, width), BF16), shaped((rows, 1), F32)],
        [per_step((rows, WIDE)), whole((rows, width)), whole((rows, 1))],
        [(width, WIDE), (width, WIDE)],
        [
            pltpu.VMEM((rows, width), F32),
            pltpu.VMEM((rows, width), BF16),
            pltpu.VMEM((rows, 2 * rows), F32),
            pltpu.VMEM((rows, WIDE), F32),
            pltpu.VMEM((2 * rows, WIDE), BF16),
            pltpu.VMEM((2 * rows, WIDE), BF16),
        ],
        steps * (2 * rows * width * WIDE * 2 + 32 * rows * rows * WIDE),
    )


def cross_backward(grad, hat, inv, gain, saved_q, kv_own, kv_away, keys_col, seg_row, query_w, out_w):
    rows, width = grad.shape
    steps = len(query_w.parts) * query_w.count

    def body(ins, wrefs, outs, bufs, sems, extra):
        g_ref, hat_ref, inv_ref, gain_ref, q_ref, own_ref, away_ref, keysc_ref, segr_ref = ins
        dx_ref, own_grad_ref, away_grad_ref = outs
        acc, bias, dq, dk, dv, keys, values = extra
        step = pl.program_id(0)
        slot = advance((query_w, out_w), wrefs, bufs, sems, 1, step, steps)

        @pl.when(step == 0)
        def _():
            fill_bias(bias, keysc_ref[...], segr_ref[...], 0)
            acc[...] = g_ref[...].astype(F32)

        mixed_grad = dot_nn(g_ref[...], bufs[1][slot]).astype(BF16)
        keys[:rows] = own_ref[0, 0]
        keys[rows:] = away_ref[0, 0]
        values[:rows] = own_ref[0, 1]
        values[rows:] = away_ref[0, 1]
        attend_slope(q_ref[0], keys[...], values[...], mixed_grad, bias, dq, dk, dv, 256)
        own_grad_ref[0, 0] = dk[:rows].astype(BF16)
        own_grad_ref[0, 1] = dv[:rows].astype(BF16)
        away_grad_ref[0, 0] = dk[rows:].astype(BF16)
        away_grad_ref[0, 1] = dv[rows:].astype(BF16)
        acc[...] += dot_nt(dq[...].astype(BF16), bufs[0][slot])

        @pl.when(step == steps - 1)
        def _():
            dx_ref[...] = norm_slope(
                acc[...], hat_ref[...].astype(F32), inv_ref[...], gain_ref[...]
            ).astype(BF16)

    return call(
        body,
        steps,
        [grad, hat, inv, gain, saved_q, kv_own, kv_away, keys_col, seg_row],
        [
            whole(grad.shape),
            whole(hat.shape),
            whole(inv.shape),
            whole(gain.shape),
            per_step((rows, WIDE)),
            per_step((2, rows, WIDE)),
            per_step((2, rows, WIDE)),
            whole(keys_col.shape),
            whole(seg_row.shape),
        ],
        [query_w, out_w],
        [
            shaped((rows, width), BF16),
            shaped((steps, 2, rows, WIDE), BF16),
            shaped((steps, 2, rows, WIDE), BF16),
        ],
        [whole((rows, width)), per_step((2, rows, WIDE)), per_step((2, rows, WIDE))],
        [(width, WIDE), (width, WIDE)],
        [
            pltpu.VMEM((rows, width), F32),
            pltpu.VMEM((2 * rows, rows), F32),
            pltpu.VMEM((rows, WIDE), F32),
            pltpu.VMEM((2 * rows, WIDE), F32),
            pltpu.VMEM((2 * rows, WIDE), F32),
            pltpu.VMEM((2 * rows, WIDE), BF16),
            pltpu.VMEM((2 * rows, WIDE), BF16),
        ],
        steps * (2 * rows * width * WIDE * 2 + 80 * rows * rows * WIDE),
    )


def keys_forward(y, key_w, value_w):
    rows, width = y.shape
    steps = len(key_w.parts) * key_w.count

    def body(ins, wrefs, outs, bufs, sems, extra):
        (kv_ref,) = outs
        slot = advance((key_w, value_w), wrefs, bufs, sems, 0, pl.program_id(0), steps)
        kv_ref[0, 0] = dot_nn(ins[0][...], bufs[0][slot]).astype(BF16)
        kv_ref[0, 1] = dot_nn(ins[0][...], bufs[1][slot]).astype(BF16)

    return call(
        body,
        steps,
        [y],
        [whole(y.shape)],
        [key_w, value_w],
        [shaped((steps, 2, rows, WIDE), BF16)],
        [per_step((2, rows, WIDE))],
        [(width, WIDE), (width, WIDE)],
        [],
        steps * 4 * rows * width * WIDE,
    )[0]


def keys_backward(out_grad, kv_grad, kv_grad_away, key_w, value_w):
    rows, width = out_grad.shape
    steps = len(key_w.parts) * key_w.count

    def body(ins, wrefs, outs, bufs, sems, extra):
        g_ref, own_ref, away_ref = ins
        (sum_ref,) = outs
        (acc,) = extra
        step = pl.program_id(0)
        slot = advance((key_w, value_w), wrefs, bufs, sems, 0, step, steps)

        @pl.when(step == 0)
        def _():
            acc[...] = g_ref[...].astype(F32)

        both = (own_ref[0].astype(F32) + away_ref[0].astype(F32)).astype(BF16)
        acc[...] += dot_nt(both[0], bufs[0][slot]) + dot_nt(both[1], bufs[1][slot])

        @pl.when(step == steps - 1)
        def _():
            sum_ref[...] = acc[...].astype(BF16)

    return call(
        body,
        steps,
        [out_grad, kv_grad, kv_grad_away],
        [whole(out_grad.shape), per_step((2, rows, WIDE)), per_step((2, rows, WIDE))],
        [key_w, value_w],
        [shaped((rows, width), BF16)],
        [whole((rows, width))],
        [(width, WIDE), (width, WIDE)],
        [pltpu.VMEM((rows, width), F32)],
        steps * 4 * rows * width * WIDE,
    )[0]


def two_phase(layer, streams_a, refs_a, bufs_a, sems_a, streams_b, refs_b, bufs_b, sems_b, step, na, nb):
    slot = lax.rem(step, 2)

    def start_a(at, to):
        for s, r, b, m in zip(streams_a, refs_a, bufs_a, sems_a):
            issue(s, r, b, m, layer, at, to)

    def start_b(at, to):
        for s, r, b, m in zip(streams_b, refs_b, bufs_b, sems_b):
            issue(s, r, b, m, layer, at - na, to)

    @pl.when(step == 0)
    def _():
        start_a(0, 0)

    @pl.when(step + 1 < na)
    def _():
        start_a(step + 1, 1 - slot)

    @pl.when((step + 1 >= na) & (step + 1 < na + nb))
    def _():
        start_b(step + 1, 1 - slot)

    @pl.when(step < na)
    def _():
        for s, r, b, m in zip(streams_a, refs_a, bufs_a, sems_a):
            await_chunk(s, r, b, m, slot)

    @pl.when(step >= na)
    def _():
        for s, r, b, m in zip(streams_b, refs_b, bufs_b, sems_b):
            await_chunk(s, r, b, m, slot)

    return slot


def branch_forward(layer, hat, gain, out_gain, down_bias, up_bias, ffn, adapter):
    rows, width = hat.shape
    up_w, down_w = ffn
    adown, aup = adapter
    na = len(up_w.parts) * up_w.count
    nb = len(adown.parts) * adown.count
    units = down_bias.shape[-1]
    steps = na + nb

    def body(ins, wrefs, outs, bufs, sems, extra):
        hat_ref, gain_ref, ogain_ref, dbias_ref, ubias_ref = ins
        slope_ref, aslope_ref, aact_ref, nhat_ref, inv_ref, y_ref = outs
        acc, low = extra
        step = pl.program_id(0)
        slot = two_phase(
            layer, ffn, wrefs[:2], bufs[:2], sems[:2], adapter, wrefs[2:], bufs[2:], sems[2:],
            step, na, nb,
        )

        @pl.when(step == 0)
        def _():
            first = hat_ref[...].astype(F32) * gain_ref[...]
            low[...] = first.astype(BF16)
            acc[...] = first + 4.0 * ubias_ref[...]

        @pl.when(step < na)
        def _():
            for at in range(0, rows, 256):
                part = slice(at, at + 256)
                act, slope = gelu_pair(dot_nn(low[part, :], bufs[0][slot]))
                slope_ref[0, part, :] = slope.astype(BF16)
                acc[part, :] += dot_nn(act.astype(BF16), bufs[1][slot])

        @pl.when(step >= na)
        def _():
            act, slope = gelu_pair(dot_nn(low[...], bufs[2][slot]) + dbias_ref[0])
            low_act = act.astype(BF16)
            aslope_ref[0] = slope.astype(BF16)
            aact_ref[0] = low_act
            acc[...] += dot_nn(low_act * jnp.asarray(4.0, BF16), bufs[3][slot])

        @pl.when(step == steps - 1)
        def _():
            nhat, inverse = normalized(acc[...])
            nhat_ref[...] = nhat.astype(BF16)
            inv_ref[...] = inverse
            y_ref[...] = (nhat * ogain_ref[...]).astype(BF16)

    return call(
        body,
        steps,
        [hat, gain, out_gain, down_bias, up_bias],
        [
            whole(hat.shape),
            whole(gain.shape),
            whole(out_gain.shape),
            per_step((1, units), na),
            whole(up_bias.shape),
        ],
        [up_w, down_w, adown, aup],
        [
            shaped((na, rows, CHUNK), BF16),
            shaped((nb, rows, units), BF16),
            shaped((nb, rows, units), BF16),
            shaped((rows, width), BF16),
            shaped((rows, 1), F32),
            shaped((rows, width), BF16),
        ],
        [
            per_step((rows, CHUNK), 0, na - 1),
            per_step((rows, units), na),
            per_step((rows, units), na),
            whole((rows, width)),
            whole((rows, 1)),
            whole((rows, width)),
        ],
        [(width, CHUNK), (CHUNK, width), (width, units), (units, width)],
        [pltpu.VMEM((rows, width), F32), pltpu.VMEM((rows, width), BF16)],
        4 * rows * width * (na * CHUNK + nb * units),
    )


def branch_backward(layer, out_grad, nhat, ninv, out_gain, hat, inv, gain, slope, aslope, aact, ffn, adapter):
    rows, width = hat.shape
    up_w, down_w = ffn
    adown, aup = adapter
    na = len(up_w.parts) * up_w.count
    nb = len(adown.parts) * adown.count
    units = aact.shape[-1]
    steps = na + nb

    def body(ins, wrefs, outs, bufs, sems, extra):
        g_ref, nhat_ref, ninv_ref, ogain_ref, hat_ref, inv_ref, gain_ref, slope_ref, aslope_ref, aact_ref = ins
        dx_ref, down_ref, dbias_ref, up_ref, ubias_ref = outs
        acc, low, rows_low = extra
        step = pl.program_id(0)
        slot = two_phase(
            layer, ffn, wrefs[:2], bufs[:2], sems[:2], adapter, wrefs[2:], bufs[2:], sems[2:],
            step, na, nb,
        )

        @pl.when(step == 0)
        def _():
            grad = norm_slope(
                g_ref[...].astype(F32), nhat_ref[...].astype(F32), ninv_ref[...], ogain_ref[...]
            )
            acc[...] = grad
            small = grad.astype(BF16)
            low[...] = small
            ubias_ref[...] = 4.0 * jnp.sum(small.astype(F32), 0, keepdims=True)
            rows_low[...] = (hat_ref[...].astype(F32) * gain_ref[...]).astype(BF16)

        @pl.when(step < na)
        def _():
            for at in range(0, rows, 256):
                part = slice(at, at + 256)
                hidden = dot_nt(low[part, :], bufs[1][slot]) * slope_ref[0, part, :].astype(F32)
                acc[part, :] += dot_nt(hidden.astype(BF16), bufs[0][slot])

        @pl.when(step >= na)
        def _():
            hidden = 4.0 * dot_nt(low[...], bufs[3][slot]) * aslope_ref[0].astype(F32)
            small = hidden.astype(BF16)
            acc[...] += dot_nt(small, bufs[2][slot])
            down_ref[0] = dot_tn(rows_low[...], small)
            dbias_ref[0] = jnp.sum(small.astype(F32), 0, keepdims=True)
            up_ref[0] = 4.0 * dot_tn(aact_ref[0], low[...])

        @pl.when(step == steps - 1)
        def _():
            dx_ref[...] = norm_slope(
                acc[...], hat_ref[...].astype(F32), inv_ref[...], gain_ref[...]
            ).astype(BF16)

    return call(
        body,
        steps,
        [out_grad, nhat, ninv, out_gain, hat, inv, gain, slope, aslope, aact],
        [
            whole(out_grad.shape),
            whole(nhat.shape),
            whole(ninv.shape),
            whole(out_gain.shape),
            whole(hat.shape),
            whole(inv.shape),
            whole(gain.shape),
            per_step((rows, CHUNK), 0, na - 1),
            per_step((rows, units), na),
            per_step((rows, units), na),
        ],
        [up_w, down_w, adown, aup],
        [
            shaped((rows, width), BF16),
            shaped((nb, width, units), F32),
            shaped((nb, 1, units), F32),
            shaped((nb, units, width), F32),
            shaped((1, width), F32),
        ],
        [
            whole((rows, width)),
            per_step((width, units), na),
            per_step((1, units), na),
            per_step((units, width), na),
            whole((1, width)),
        ],
        [(width, CHUNK), (CHUNK, width), (width, units), (units, width)],
        [
            pltpu.VMEM((rows, width), F32),
            pltpu.VMEM((rows, width), BF16),
            pltpu.VMEM((rows, width), BF16),
        ],
        4 * rows * width * (na * CHUNK + nb * units),
    )


def swap(value, axis):
    return jax.tree.map(lambda a: lax.ppermute(a, axis, [(0, 1), (1, 0)]), value)


def rotated(pieces, start, count):
    return lax.dynamic_slice_in_dim(jnp.concatenate(pieces, 0), start, count, 0)


def per_device(
    inputs,
    segment_ids,
    cotangent,
    norm_gains,
    cross_gain,
    self_qkv,
    self_out,
    cross_kv,
    cross_vo,
    ffn_in,
    ffn_out,
    adapter_down,
    adapter_down_bias,
    adapter_up,
    adapter_up_bias,
):
    core = lax.axis_index("section")
    side = lax.axis_index("mp")
    first_core = core == 0
    seq = segment_ids.shape[2]
    half = seq // 2
    width = inputs.shape[3]
    units = adapter_down.shape[2]

    qkv = jnp.transpose(self_qkv[0], (1, 0, 2))
    near = (
        qkv, self_out[0], cross_kv[0], cross_vo[0], ffn_in[0], ffn_out[0],
        adapter_down[0], adapter_up[0],
    )
    far = swap(near, "mp")
    near_other = swap(near, "section")
    far_other = swap(far, "section")
    parts = [
        [(near[i], near_other[i]), (far[i], far_other[i])] for i in range(len(near))
    ]
    w_qkv = Stream(parts[0], stack_cut(WIDE), near[0].shape[2] // WIDE)
    w_out = Stream(parts[1], row_cut(WIDE), near[1].shape[0] // WIDE)
    w_ckv = Stream(parts[2], column_cut(WIDE), near[2].shape[1] // WIDE)
    w_cvo = Stream(parts[3], column_cut(WIDE), near[3].shape[1] // WIDE)
    w_up = Stream(parts[4], column_cut(CHUNK), near[4].shape[1] // CHUNK)
    w_down = Stream(parts[5], row_cut(CHUNK), near[5].shape[0] // CHUNK)
    w_adown = Stream(parts[6], column_cut(units), 1)
    w_aup = Stream(parts[7], row_cut(units), 1)
    ffn = (w_up, w_down)
    adapter = (w_adown, w_aup)

    bias_near = adapter_down_bias[0][None]
    bias_far = swap(bias_near, "mp")
    small = jnp.concatenate(
        [
            norm_gains[0],
            adapter_up_bias,
            jnp.concatenate([bias_near, bias_far, jnp.zeros((1, width - 2 * units), F32)], 1),
        ],
        0,
    )
    small_other = swap(small, "section")
    enc_small = jnp.where(first_core, small, small_other)
    dec_small = jnp.where(first_core, small_other, small)

    def small_of(s):
        down_bias = jnp.stack([s[3:4, :units], s[3:4, units : 2 * units]], 0)
        return s[0:1], s[1:2], s[2:3], down_bias

    enc_gain1, enc_gain2, enc_upb, enc_downb = small_of(enc_small)
    dec_gain1, dec_gain2, dec_upb, dec_downb = small_of(dec_small)
    mid_gain = cross_gain[None]

    segs = lax.dynamic_index_in_dim(segment_ids, side, 1, keepdims=False)
    docs = jnp.arange(seq)
    counts = jnp.sum(segs[:, :, None] == docs[None, None, :8], 1)
    largest = jnp.argmax(counts, 1)
    starts = jnp.sum(segs < largest[:, None], 1).astype(jnp.int32)

    def halves_of_seg(seg, start):
        twice = jnp.concatenate([seg, seg], 0)
        mine = lax.dynamic_slice_in_dim(twice, start + half * core, half, 0)
        away = lax.dynamic_slice_in_dim(twice, start + half * (1 - core), half, 0)
        return mine, away

    enc_seg, enc_seg_away = halves_of_seg(segs[0], starts[0])
    dec_seg, _ = halves_of_seg(segs[1], starts[1])
    own_start = jnp.where(first_core, starts[0], starts[1])

    def rows_here(value):
        keep = lax.dynamic_index_in_dim(value[0], side, 0, keepdims=False)
        give = lax.dynamic_index_in_dim(value[0], 1 - side, 0, keepdims=False)
        got = swap(give, "mp")
        at = lax.rem(own_start + seq - half * side, seq)
        ring = (keep, got, keep, got)
        mine = rotated(ring, at + half * core, half)
        away = rotated(ring, lax.rem(at + half * (1 - core), seq), half)
        other = swap(away, "section")
        return jnp.where(first_core, mine, other), jnp.where(first_core, other, mine)

    def rows_back(enc, dec):
        mine = jnp.where(first_core, enc, dec)
        away = jnp.where(first_core, dec, enc)
        other = swap(away, "section")
        big = jnp.where(first_core, mine, other)
        rest = jnp.where(first_core, other, mine)
        ring = (big, rest, big, rest)
        keep = rotated(ring, lax.rem(half * side + seq - own_start, seq), half)
        give = rotated(ring, lax.rem(half * (1 - side) + seq - own_start, seq), half)
        got = swap(give, "mp")
        return jnp.where(side == 0, jnp.stack([keep, got]), jnp.stack([got, keep]))

    x_enc, x_dec = rows_here(inputs)
    g_enc, g_dec = rows_here(cotangent)

    enc_col, enc_row = enc_seg[:, None], enc_seg[None, :]
    dec_col, dec_row = dec_seg[:, None], dec_seg[None, :]
    all_keys = jnp.concatenate([enc_seg, enc_seg_away], 0)

    e_qkv, e_hat1, e_inv1 = self_forward(0, x_enc, enc_col, enc_row, enc_gain1, w_qkv, w_out)
    e_slope, e_aslope, e_aact, e_hat2, e_inv2, y_enc = branch_forward(
        0, e_hat1, enc_gain1, enc_gain2, enc_downb, enc_upb, ffn, adapter
    )
    kv = keys_forward(y_enc, w_ckv, w_cvo)
    kv_away = swap(kv, "section")
    d_qkv, d_hat1, d_inv1 = self_forward(1, x_dec, dec_col, dec_row, dec_gain1, w_qkv, w_out)
    d_q, d_hat2, d_inv2 = cross_forward(
        d_hat1, dec_gain1, kv, kv_away, dec_col, all_keys[None, :], w_ckv, w_cvo
    )
    d_slope, d_aslope, d_aact, d_hat3, d_inv3, y_dec = branch_forward(
        1, d_hat2, mid_gain, dec_gain2, dec_downb, dec_upb, ffn, adapter
    )

    d_mid, d_down, d_dbias, d_up, d_ubias = branch_backward(
        1, g_dec, d_hat3, d_inv3, dec_gain2, d_hat2, d_inv2, mid_gain,
        d_slope, d_aslope, d_aact, ffn, adapter,
    )
    d_first, kv_grad, kv_grad_give = cross_backward(
        d_mid, d_hat1, d_inv1, dec_gain1, d_q, kv, kv_away, all_keys[:, None], dec_row, w_ckv, w_cvo
    )
    kv_grad_away = swap(kv_grad_give, "section")
    dx_dec = self_backward(1, d_first, d_qkv, dec_col, dec_row, w_qkv, w_out)
    e_out = keys_backward(g_enc, kv_grad, kv_grad_away, w_ckv, w_cvo)
    e_first, e_down, e_dbias, e_up, e_ubias = branch_backward(
        0, e_out, e_hat2, e_inv2, enc_gain2, e_hat1, e_inv1, enc_gain1,
        e_slope, e_aslope, e_aact, ffn, adapter,
    )
    dx_enc = self_backward(0, e_first, e_qkv, enc_col, enc_row, w_qkv, w_out)

    def gathered(enc, dec):
        mine = jnp.where(first_core, enc, dec).astype(BF16)
        away = jnp.where(first_core, dec, enc).astype(BF16)
        both = mine.astype(F32) + swap(away, "section").astype(F32)
        return both

    def to_side(both):
        return both[0] + swap(both[1].astype(BF16), "mp").astype(F32)

    def over_dp(value):
        return lax.psum(value.astype(BF16), "dp").astype(F32)

    down_total = over_dp(to_side(gathered(e_down, d_down)))
    up_total = over_dp(to_side(gathered(e_up, d_up)))
    dbias_total = over_dp(to_side(gathered(e_dbias, d_dbias)))
    ubias = gathered(e_ubias, d_ubias)
    ubias_total = over_dp(ubias + swap(ubias.astype(BF16), "mp").astype(F32))

    return (
        rows_back(y_enc, y_dec)[None],
        rows_back(dx_enc, dx_dec).astype(F32)[None],
        down_total[None],
        dbias_total,
        up_total[None],
        ubias_total,
    )


def solution(mesh):
    in_specs = (
        P("section", "dp", "mp", None),
        P(None, "dp", None),
        P("section", "dp", "mp", None),
        P("section", None, None),
        P(),
        P("section", None, None, "mp"),
        P("section", "mp", None),
        P("section", None, "mp"),
        P("section", None, "mp"),
        P("section", None, "mp"),
        P("section", "mp", None),
        P("section", None, "mp"),
        P("section", "mp"),
        P("section", "mp", None),
        P("section", None),
    )
    out_specs = (
        P("section", "dp", "mp", None),
        P("section", "dp", "mp", None),
        P("section", None, "mp"),
        P("section", "mp"),
        P("section", "mp", None),
        P("section", None),
    )
    return jax.shard_map(
        per_device, mesh=mesh, in_specs=in_specs, out_specs=out_specs, check_vma=False
    )
```

time: 4280 us -> 860 us (0.20)
  waiting for transfers between devices: 2570 us -> 436 us
  matrix products: 882 us -> 0 us
  Pallas kernels: 0 us -> 291 us
  other arithmetic: 318 us -> 34.6 us
  loops' own time: 186 us -> 0 us
  local copies, waits for them, and re-layouts: 185 us -> 22.1 us
  starting transfers between devices: 95 us -> 25.7 us
    reduce_scatter x27 -> x0, waiting for transfers between devices: 1650 us -> none  [the longest x18 1110 us: fwd_sum(): return lax.psum_scatter(value, 'mp', scatter_dimension=0, tiled=True)]
    all_gather x27 -> x0, waiting for transfers between devices: 868 us -> none  [the longest x18 571 us: fwd_gather(): return lax.all_gather(value, 'mp', axis=0, tiled=True)]
    dot_general x105 -> x0, matrix products: 821 us -> none  [the longest x36 335 us: product(): return jnp.dot(left, right, preferred_element_type=jnp.float32)]
    ppermute x6 -> x44, waiting for transfers between devices: 0.02 us -> 402 us  [swap(): lax.ppermute(a, axis, [(0, 1), (1, 0)])]
    pallas_call x0 -> x12, Pallas kernels: none -> 291 us  [call(): pl.pallas_call(kernel, grid=(steps,), in_specs=list(in_blocks) + [pl.Bloc...]
    another operation x23 -> x0, loops' own time: 186 us -> none  [the longest x6 62.2 us: layer_forward(): lax.cond(is_decoder, cross_partial, lambda: branch_partial(first_rows))]
    reduce_sum x60 -> x2, other arithmetic: 123 us -> 0.38 us  [the longest x1 0.19 us: per_device(): counts = jnp.sum(segs[:, :, None] == docs[None, None, :8], 1)]
    convert_element_type x32 -> x10, other arithmetic: 119 us -> 5.11 us  [the longest x1 2.39 us: per_device(): rows_back(dx_enc, dx_dec).astype(F32)[None]]
  transfers between devices with their start and end apart: 61 -> 45, of which waited for: 55 -> 14; matrix products, arithmetic and copies ran while one was open for 3% -> 5% of each run, Pallas kernels for 0% -> 24%
where the time goes in v1:
time: 860 us; the launch traced here: 849 us
  waiting for transfers between devices  436 us (51%)
  Pallas kernels  291 us (34%)
  other arithmetic  34.6 us (4%)
  starting transfers between devices  25.7 us (3%)
  local copies, waits for them, and re-layouts  22.1 us (3%)
  blocking collectives  22 us (3%)
  between operations  18.2 us (2%)
    ppermute x44, waiting for transfers between devices, swap(): lax.ppermute(a, axis, [(0, 1), (1, 0)])  402 us
    pallas_call x12, Pallas kernels, call(): pl.pallas_call(kernel, grid=(steps,), in_specs=list(in_blocks) + [pl.Bloc...  291 us
    psum x1, waiting for transfers between devices, over_dp(): return lax.psum(value.astype(BF16), 'dp').astype(F32)  33.4 us
    ppermute x44, starting transfers between devices, swap(): lax.ppermute(a, axis, [(0, 1), (1, 0)])  25.7 us
    psum x1, blocking collectives, over_dp(): return lax.psum(value.astype(BF16), 'dp').astype(F32)  22 us
  transfers between devices with their start and end apart: 45, of which 14 were waited for; matrix products, arithmetic and copies ran while one was open for 5% of the time, Pallas kernels for 24%

profile of v1, /device:TPU:0, one launch (start us, length us, event | category | flops | bytes accessed | tf_op | source)
XLA Modules:
  0.0 849.4 jit_solution(10291277566588969523)
XLA Ops:
  18.2 7.1 collective-permute-done.17.refs_15_.refs_20_
  27.4 31.7 %collective-permute-done.20.refs_19_.refs_24_ = bf16[256,1024]{1,0:T(8,128)(2,1)S(1)} collective-permute-done((bf16[256,1024]{1,0:T(8,128)(2,1)S(1)}, bf16[256,1024]{1,0:T(8,128)(2,1)S(1)}, u32[]{:S(2)}, u32[]{:S(2)}) %collective-permute-start.20) | collective-permute-done | bytes 524320 | tf_op jit(solution)/shard_map/ppermute | solution.py:736
  60.2 21.3 %collective-permute-done.8.refs_10_ = bf16[512,1024]{1,0:T(8,128)(2,1)S(1)} collective-permute-done((bf16[512,1024]{1,0:T(8,128)(2,1)}, bf16[512,1024]{1,0:T(8,128)(2,1)S(1)}, u32[]{:S(2)}, u32[]{:S(2)}) %collective-permute-start.8) | collective-permute-done | bytes 1048608 | tf_op jit(solution)/shard_map/ppermute | solution.py:736
  87.7 16.4 %collective-permute-done.23.refs_3_.refs_8_.refs_11_.refs_5_ = bf16[1024,512]{1,0:T(8,128)(2,1)} collective-permute-done((bf16[1024,512]{1,0:T(8,128)(2,1)}, bf16[1024,512]{1,0:T(8,128)(2,1)}, u32[]{:S(2)}, u32[]{:S(2)}) %collective-permute-start.23) | collective-permute-done | bytes 1048608 | tf_op jit(solution)/shard_map/ppermute | solution.py:736
  112.0 194.3 %collective-permute-done.26.refs_7_.refs_12_.refs_15_.refs_9_ = bf16[1024,512]{1,0:T(8,128)(2,1)} collective-permute-done((bf16[1024,512]{1,0:T(8,128)(2,1)}, bf16[1024,512]{1,0:T(8,128)(2,1)}, u32[]{:S(2)}, u32[]{:S(2)}) %collective-permute-start.26) | collective-permute-done | bytes 1048608 | tf_op jit(solution)/shard_map/ppermute | solution.py:736
  306.3 21.7 %collective-permute-done.31 = bf16[512,1024]{1,0:T(8,128)(2,1)} collective-permute-done((bf16[512,1024]{1,0:T(8,128)(2,1)}, bf16[512,1024]{1,0:T(8,128)(2,1)}, u32[]{:S(2)}, u32[]{:S(2)}) %collective-permute-start.31) | collective-permute-done | bytes 1048608 | tf_op jit(solution)/shard_map/ppermute | solution.py:736
  332.0 65.6 %collective-permute-done.5.refs_6_ = bf16[3,1024,512]{2,1,0:T(8,128)(2,1)} collective-permute-done((bf16[3,1024,512]{2,1,0:T(8,128)(2,1)}, bf16[3,1024,512]{2,1,0:T(8,128)(2,1)}, u32[]{:S(2)}, u32[]{:S(2)}) %collective-permute-start.5) | collective-permute-done | bytes 3145760 | tf_op jit(solution)/shard_map/ppermute | solution.py:736
  411.3 20.9 %shard_map.190 = (bf16[4,3,512,256]{3,2,1,0:T(8,128)(2,1)}, bf16[512,1024]{1,0:T(8,128)(2,1)}, f32[512,1]{1,0:T(8,128)}) custom-call(bf16[512,1024]{1,0:T(8,128)(2,1)} %get-tuple-element.84.refs_0_, s32[512,1]{1,0:T(8,128)} %copy.27.refs_1_.refs_2_, s32[1,512]{1,0:T(1,128)} %bitcast.99, f32[1,1024]{1,0:T(1,128)} %get-tuple-element.107.refs_3_.refs_1_.refs_6_, ...), custom_call_target="tpu_custom_call" | custom-call | flops 8589934592 | bytes 17179868 | tf_op jit(solution)/shard_map/pallas_call | solution.py:113
  432.7 23.1 %shard_map.191 = (bf16[8,512,512]{2,1,0:T(8,128)(2,1)}, bf16[2,512,256]{2,1,0:T(8,128)(2,1)}, bf16[2,512,256]{2,1,0:T(8,128)(2,1)}, bf16[512,1024]{1,0:T(8,128)(...) custom-call(bf16[512,1024]{1,0:T(8,128)(2,1)} %get-tuple-element.42.refs_0_.refs_4_, ...), custom_call_target="tpu_custom_call" | custom-call | flops 9663676416 | bytes 19327352 | tf_op jit(solution)/shard_map/pallas_call | solution.py:113
  457.4 7.2 shard_map.193.refs_2_.refs_5_
  472.2 20.9 %shard_map.192 = (bf16[4,3,512,256]{3,2,1,0:T(8,128)(2,1)}, bf16[512,1024]{1,0:T(8,128)(2,1)}, f32[512,1]{1,0:T(8,128)}) custom-call(bf16[512,1024]{1,0:T(8,128)(2,1)} %get-tuple-element.85.refs_0_, s32[512,1]{1,0:T(8,128)} %copy.28.refs_1_.refs_4_.refs_2_, s32[1,512]{1,0:T(1,128)} %bitcast.108, f32[1,1024]{1,0:T(1,128)} %get-tuple-element.102.refs_3_.refs_1_, ...), custom_call_target="tpu_custom_call" | custom-call | flops 8589934592 | bytes 17179868 | tf_op jit(solution)/shard_map/pallas_call | solution.py:113
  494.4 27.8 %shard_map.194 = (bf16[4,512,256]{2,1,0:T(8,128)(2,1)}, bf16[512,1024]{1,0:T(8,128)(2,1)}, f32[512,1]{1,0:T(8,128)}) custom-call(bf16[512,1024]{1,0:T(8,128)(2,1)} %get-tuple-element.44.refs_0_.refs_1_, f32[1,1024]{1,0:T(1,128)} %get-tuple-element.102.refs_3_.refs_1_, bf16[4,2,512,256]{3,2,1,0:T(8,128)(2,1)} %shard_map.193.refs_2_.refs_5_, ...), custom_call_target="tpu_custom_call" | custom-call | flops 10737418240 | bytes 21474836 | tf_op jit(solution)/shard_map/pallas_call | solution.py:113
  522.2 23.6 %shard_map.195 = (bf16[8,512,512]{2,1,0:T(8,128)(2,1)}, bf16[2,512,256]{2,1,0:T(8,128)(2,1)}, bf16[2,512,256]{2,1,0:T(8,128)(2,1)}, bf16[512,1024]{1,0:T(8,128)(...) custom-call(bf16[512,1024]{1,0:T(8,128)(2,1)} %get-tuple-element.45.refs_0_.refs_4_, f32[1,1024]{1,0:T(1,128)} %bitcast.101, ...), custom_call_target="tpu_custom_call" | custom-call | flops 9663676416 | bytes 19327352 | tf_op jit(solution)/shard_map/pallas_call | solution.py:113
  547.2 25.1 %shard_map.196 = (bf16[512,1024]{1,0:T(8,128)(2,1)}, f32[2,1024,256]{2,1,0:T(8,128)}, f32[2,1,256]{2,1,0:T(1,128)}, f32[2,256,1024]{2,1,0:T(8,128)}, f32[1,1024]{1,0:T(1,128)}) custom-call(bf16[512,1024]{1,0:T(8,128)(2,1)} %get-tuple-element.83.refs_0_, bf16[512,1024]{1,0:T(8,128)(2,1)} %get-tuple-element.47.refs_1_, f32[512,1]{1,0:T(8,128)} %get-tuple-element.48.refs_2_, ...), custom_call_target="tpu_custom_call" | custom-call | flops 9663676416 | bytes 19327352 | tf_op jit(solution)/shard_map/pallas_call | solution.py:113
  572.4 47.6 %shard_map.197 = (bf16[512,1024]{1,0:T(8,128)(2,1)}, bf16[4,2,512,256]{3,2,1,0:T(8,128)(2,1)}, bf16[4,2,512,256]{3,2,1,0:T(8,128)(2,1)}) custom-call(bf16[512,1024]{1,0:T(8,128)(2,1)} %get-tuple-element.53.refs_0_, bf16[512,1024]{1,0:T(8,128)(2,1)} %get-tuple-element.44.refs_0_.refs_1_, f32[512,1]{1,0:T(8,128)} %get-tuple-element.54.refs_2_, ...), custom_call_target="tpu_custom_call" | custom-call | flops 23622320128 | bytes 47244640 | tf_op jit(solution)/shard_map/pallas_call | solution.py:113
  623.8 30.4 %shard_map.201 = bf16[512,1024]{1,0:T(8,128)(2,1)} custom-call(bf16[512,1024]{1,0:T(8,128)(2,1)} %get-tuple-element.66.refs_0_, bf16[4,3,512,256]{3,2,1,0:T(8,128)(2,1)} %get-tuple-element.67.refs_1_, s32[512,1]{1,0:T(8,128)} %copy.28.refs_1_.refs_4_.refs_2_, s32[1,512]{1,0:T(1,128)} %bitcast.110, bf16[3,1024,512]{2,1,0:T(8,128)(2,1)} %bitcast.9.refs_4_, ...), custom_call_target="tpu_custom_call" | custom-call | flops 15032385536 | bytes 30064772 | tf_op jit(solution)/shard_map/pallas_call | solution.py:113
  655.9 8.1 shard_map.198.refs_0_
  664.0 25.5 %shard_map.199 = (bf16[512,1024]{1,0:T(8,128)(2,1)}, f32[2,1024,256]{2,1,0:T(8,128)}, f32[2,1,256]{2,1,0:T(1,128)}, f32[2,256,1024]{2,1,0:T(8,128)}, f32[1,1024]{1,0:T(1,128)}) custom-call(bf16[512,1024]{1,0:T(8,128)(2,1)} %shard_map.198.refs_0_, bf16[512,1024]{1,0:T(8,128)(2,1)} %get-tuple-element.58.refs_1_, f32[512,1]{1,0:T(8,128)} %get-tuple-element.59.refs_2_, ...), custom_call_target="tpu_custom_call" | custom-call | flops 9663676416 | bytes 19327352 | tf_op jit(solution)/shard_map/pallas_call | solution.py:113
  692.2 30.9 %shard_map.200 = bf16[512,1024]{1,0:T(8,128)(2,1)} custom-call(bf16[512,1024]{1,0:T(8,128)(2,1)} %get-tuple-element.64.refs_0_, bf16[4,3,512,256]{3,2,1,0:T(8,128)(2,1)} %get-tuple-element.65.refs_1_, s32[512,1]{1,0:T(8,128)} %copy.27.refs_1_.refs_2_, s32[1,512]{1,0:T(1,128)} %bitcast.100, bf16[3,1024,512]{2,1,0:T(8,128)(2,1)} %bitcast.9.refs_4_, ...), custom_call_target="tpu_custom_call" | custom-call | flops 15032385536 | bytes 30064772 | tf_op jit(solution)/shard_map/pallas_call | solution.py:113
  737.1 8.9 %collective-permute-done.37 = bf16[1024,256]{1,0:T(8,128)(2,1)S(1)} collective-permute-done((bf16[1024,256]{1,0:T(8,128)(2,1)S(1)}, bf16[1024,256]{1,0:T(8,128)(2,1)S(1)}, u32[]{:S(2)}, u32[]{:S(2)}) %collective-permute-start.37) | collective-permute-done | bytes 524320 | tf_op jit(solution)/shard_map/ppermute | solution.py:736
  746.9 10.3 %collective-permute-done.41 = bf16[256,1024]{1,0:T(8,128)(2,1)S(1)} collective-permute-done((bf16[256,1024]{1,0:T(8,128)(2,1)S(1)}, bf16[256,1024]{1,0:T(8,128)(2,1)S(1)}, u32[]{:S(2)}, u32[]{:S(2)}) %collective-permute-start.41) | collective-permute-done | bytes 524320 | tf_op jit(solution)/shard_map/ppermute | solution.py:736
  760.4 18.9 %collective-permute-done.39 = bf16[1,256]{1,0:T(2,128)(2,1)S(1)} collective-permute-done((bf16[1,256]{1,0:T(2,128)(2,1)S(1)}, bf16[1,256]{1,0:T(2,128)(2,1)S(1)}, u32[]{:S(2)}, u32[]{:S(2)}) %collective-permute-start.39) | collective-permute-done | bytes 544 | tf_op jit(solution)/shard_map/ppermute | solution.py:736
  779.3 22.0 %all-reduce = (bf16[1,256]{1,0:T(2,128)(2,1)S(1)}, bf16[1,1024]{1,0:T(2,128)(2,1)S(1)}) all-reduce(bf16[1,256]{1,0:T(2,128)(2,1)S(1)} %fusion.23, bf16[1,1024]{1,0:T(2,128)(2,1)S(1)} %add_convert_fusion), channel_id=1, replica_groups=mesh['section'=2,'mp'=2,'dp'=8] {'dp'}, use_global_device_ids=true, to_apply=%region_4.5 | all-reduce | flops 1280 | bytes 5120 | tf_op jit(solution)/shard_map/psum | solution.py:898
  804.8 33.4 %all-reduce.4.cloned.1.call-done = (bf16[1,1024,256]{2,1,0:T(8,128)(2,1)}, bf16[1,256,1024]{2,1,0:T(8,128)(2,1)}) async-done(((bf16[1,1024,256]{2,1,0:T(8,128)(2,1)}, bf16[1,256,1024]{2,1,0:T(8,128)(2,1)}), (bf16[1,1024,256]{2,1,0:T(8,128)(2,1)}, bf16[1,256,1024]{2,1,0:T(8,128)(2,1)})) %all-reduce.4.cloned.1.call-update) | async-done | bytes 1048592 | tf_op jit(solution)/shard_map/psum | solution.py:898
  (214 shorter events, 88.5 us)
Async XLA Ops:
  7.2 831.0 %all-reduce.4.cloned.1.call-start = ((), (), s32[]{:S(2)}) async-start(), calls=%async_computation | async-start | bytes 2097152 | tf_op jit(solution)/shard_map/psum | solution.py:898
  15.6 43.5 %collective-permute-start = (bf16[512,1024]{1,0:T(8,128)(2,1)S(1)}, bf16[512,1024]{1,0:T(8,128)(2,1)S(1)}, u32[]{:S(2)}, u32[]{:S(2)}) collective-permute-start(bf16[512,1024]{1,0:T(8,128)(2,1)S(1)} %get-tuple-element.97), channel_id=1, source_target_pairs={{0,8},{8,0},{1,9},{9,1},{2,10},{10,2},{3,11},{11,3},{4,12},{12,4},... | collective-permute-start | bytes 3145736 | tf_op jit(solution)/shard_map/ppermute | solution.py:736
  17.6 42.5 %collective-permute-start.7 = (bf16[512,1024]{1,0:T(8,128)(2,1)}, bf16[512,1024]{1,0:T(8,128)(2,1)S(1)}, u32[]{:S(2)}, u32[]{:S(2)}) collective-permute-start(bf16[512,1024]{1,0:T(8,128)(2,1)} %bitcast.11.refs_8_), channel_id=1, source_target_pairs={{0,16},{16,0},{1,17},{17,1},{2,18},{18,2},{3,19},{19,3},{4,20},{20... | collective-permute-start | bytes 3145736 | tf_op jit(solution)/shard_map/ppermute | solution.py:736
  18.2 40.9 %collective-permute-start.20 = (bf16[256,1024]{1,0:T(8,128)(2,1)S(1)}, bf16[256,1024]{1,0:T(8,128)(2,1)S(1)}, u32[]{:S(2)}, u32[]{:S(2)}) collective-permute-start(bf16[256,1024]{1,0:T(8,128)(2,1)S(1)} %bitcast.92), channel_id=1, source_target_pairs={{0,8},{8,0},{1,9},{9,1},{2,10},{10,2},{3,11},{11,3},{4,12},{12,4},... | collective-permute-start | bytes 1572872 | tf_op jit(solution)/shard_map/ppermute | solution.py:736
  25.3 56.2 %collective-permute-start.8 = (bf16[512,1024]{1,0:T(8,128)(2,1)}, bf16[512,1024]{1,0:T(8,128)(2,1)S(1)}, u32[]{:S(2)}, u32[]{:S(2)}) collective-permute-start(bf16[512,1024]{1,0:T(8,128)(2,1)} %bitcast.11.refs_8_), channel_id=1, source_target_pairs={{0,8},{8,0},{1,9},{9,1},{2,10},{10,2},{3,11},{11,3},{4,12},{12,4},... | collective-permute-start | bytes 3145736 | tf_op jit(solution)/shard_map/ppermute | solution.py:736
  25.4 78.7 %collective-permute-start.23 = (bf16[1024,512]{1,0:T(8,128)(2,1)}, bf16[1024,512]{1,0:T(8,128)(2,1)}, u32[]{:S(2)}, u32[]{:S(2)}) collective-permute-start(bf16[1024,512]{1,0:T(8,128)(2,1)} %bitcast.21.refs_1_.refs_6_.refs_9_.refs_3_), channel_id=1, source_target_pairs={{0,8},{8,0},{1,9},{9,1},{2,10},{10,2},{3,11},{11,3},{4,12},{12,4},... | collective-permute-start | bytes 3145736 | tf_op jit(solution)/shard_map/ppermute | solution.py:736
  59.0 272.5 %collective-permute-start.11 = (bf16[1024,2048]{1,0:T(8,128)(2,1)}, bf16[1024,2048]{1,0:T(8,128)(2,1)}, u32[]{:S(2)}, u32[]{:S(2)}) collective-permute-start(bf16[1024,2048]{1,0:T(8,128)(2,1)} %bitcast.14.refs_5_.refs_10_), channel_id=1, source_target_pairs={{0,8},{8,0},{1,9},{9,1},{2,10},{10,2},{3,11},{11,3},{4,12},{12,4},... | collective-permute-start | bytes 12582920 | tf_op jit(solution)/shard_map/ppermute | solution.py:736
  82.5 249.2 %collective-permute-start.14 = (bf16[2048,1024]{1,0:T(8,128)(2,1)}, bf16[2048,1024]{1,0:T(8,128)(2,1)}, u32[]{:S(2)}, u32[]{:S(2)}) collective-permute-start(bf16[2048,1024]{1,0:T(8,128)(2,1)} %bitcast.15.refs_9_.refs_14_), channel_id=1, source_target_pairs={{0,8},{8,0},{1,9},{9,1},{2,10},{10,2},{3,11},{11,3},{4,12},{12,4},... | collective-permute-start | bytes 12582920 | tf_op jit(solution)/shard_map/ppermute | solution.py:736
  85.6 245.5 %collective-permute-start.4 = (bf16[3,1024,512]{2,1,0:T(8,128)(2,1)}, bf16[3,1024,512]{2,1,0:T(8,128)(2,1)}, u32[]{:S(2)}, u32[]{:S(2)}) collective-permute-start(bf16[3,1024,512]{2,1,0:T(8,128)(2,1)} %bitcast.9.refs_4_), channel_id=1, source_target_pairs={{0,16},{16,0},{1,17},{17,1},{2,18},{18,2},{3,19},{19,3},{4,20},{20... | collective-permute-start | bytes 9437192 | tf_op jit(solution)/shard_map/ppermute | solution.py:736
  85.7 220.7 %collective-permute-start.26 = (bf16[1024,512]{1,0:T(8,128)(2,1)}, bf16[1024,512]{1,0:T(8,128)(2,1)}, u32[]{:S(2)}, u32[]{:S(2)}) collective-permute-start(bf16[1024,512]{1,0:T(8,128)(2,1)} %bitcast.22.refs_5_.refs_10_.refs_13_.refs_7_), channel_id=1, source_target_pairs={{0,8},{8,0},{1,9},{9,1},{2,10},{10,2},{3,11},{11,3},{4,12},{12,4},... | collective-permute-start | bytes 3145736 | tf_op jit(solution)/shard_map/ppermute | solution.py:736
  104.1 223.9 %collective-permute-start.31 = (bf16[512,1024]{1,0:T(8,128)(2,1)}, bf16[512,1024]{1,0:T(8,128)(2,1)}, u32[]{:S(2)}, u32[]{:S(2)}) collective-permute-start(bf16[512,1024]{1,0:T(8,128)(2,1)} %get-tuple-element.95), channel_id=1, source_target_pairs={{0,8},{8,0},{1,9},{9,1},{2,10},{10,2},{3,11},{11,3},{4,12},{12,4},... | collective-permute-start | bytes 3145736 | tf_op jit(solution)/shard_map/ppermute | solution.py:736
  328.0 69.7 %collective-permute-start.5 = (bf16[3,1024,512]{2,1,0:T(8,128)(2,1)}, bf16[3,1024,512]{2,1,0:T(8,128)(2,1)}, u32[]{:S(2)}, u32[]{:S(2)}) collective-permute-start(bf16[3,1024,512]{2,1,0:T(8,128)(2,1)} %bitcast.9.refs_4_), channel_id=1, source_target_pairs={{0,8},{8,0},{1,9},{9,1},{2,10},{10,2},{3,11},{11,3},{4,12},{12,4},... | collective-permute-start | bytes 9437192 | tf_op jit(solution)/shard_map/ppermute | solution.py:736
  331.0 79.2 %collective-permute-start.10 = (bf16[1024,2048]{1,0:T(8,128)(2,1)}, bf16[1024,2048]{1,0:T(8,128)(2,1)}, u32[]{:S(2)}, u32[]{:S(2)}) collective-permute-start(bf16[1024,2048]{1,0:T(8,128)(2,1)} %bitcast.14.refs_5_.refs_10_), channel_id=1, source_target_pairs={{0,16},{16,0},{1,17},{17,1},{2,18},{18,2},{3,19},{19,3},{4,20},{20... | collective-permute-start | bytes 12582920 | tf_op jit(solution)/shard_map/ppermute | solution.py:736
  331.1 79.6 %collective-permute-start.13 = (bf16[2048,1024]{1,0:T(8,128)(2,1)}, bf16[2048,1024]{1,0:T(8,128)(2,1)}, u32[]{:S(2)}, u32[]{:S(2)}) collective-permute-start(bf16[2048,1024]{1,0:T(8,128)(2,1)} %bitcast.15.refs_9_.refs_14_), channel_id=1, source_target_pairs={{0,16},{16,0},{1,17},{17,1},{2,18},{18,2},{3,19},{19,3},{4,20},{20... | collective-permute-start | bytes 12582920 | tf_op jit(solution)/shard_map/ppermute | solution.py:736
  331.5 79.7 %collective-permute-start.12 = (bf16[1024,2048]{1,0:T(8,128)(2,1)}, bf16[1024,2048]{1,0:T(8,128)(2,1)}, u32[]{:S(2)}, u32[]{:S(2)}) collective-permute-start(bf16[1024,2048]{1,0:T(8,128)(2,1)} %collective-permute-done.11.refs_7_.refs_12_), channel_id=1, source_target_pairs={{0,16},{16,0},{1,17},{17,1},{2,18},{18,2},{3,19},{19,3},{4,20},{20... | collective-permute-start | bytes 12582920 | tf_op jit(solution)/shard_map/ppermute | solution.py:736
  331.7 100.5 %collective-permute-start.15 = (bf16[2048,1024]{1,0:T(8,128)(2,1)}, bf16[2048,1024]{1,0:T(8,128)(2,1)}, u32[]{:S(2)}, u32[]{:S(2)}) collective-permute-start(bf16[2048,1024]{1,0:T(8,128)(2,1)} %collective-permute-done.14.refs_11_.refs_16_), channel_id=1, source_target_pairs={{0,16},{16,0},{1,17},{17,1},{2,18},{18,2},{3,19},{19,3},{4,20},{20... | collective-permute-start | bytes 12582920 | tf_op jit(solution)/shard_map/ppermute | solution.py:736
  410.2 45.6 %collective-permute-start.22 = (bf16[1024,512]{1,0:T(8,128)(2,1)}, bf16[1024,512]{1,0:T(8,128)(2,1)S(1)}, u32[]{:S(2)}, u32[]{:S(2)}) collective-permute-start(bf16[1024,512]{1,0:T(8,128)(2,1)} %bitcast.21.refs_1_.refs_6_.refs_9_.refs_3_), channel_id=1, source_target_pairs={{0,16},{16,0},{1,17},{17,1},{2,18},{18,2},{3,19},{19,3},{4,20},{20... | collective-permute-start | bytes 3145736 | tf_op jit(solution)/shard_map/ppermute | solution.py:736
  410.7 45.1 %collective-permute-start.25 = (bf16[1024,512]{1,0:T(8,128)(2,1)}, bf16[1024,512]{1,0:T(8,128)(2,1)S(1)}, u32[]{:S(2)}, u32[]{:S(2)}) collective-permute-start(bf16[1024,512]{1,0:T(8,128)(2,1)} %bitcast.22.refs_5_.refs_10_.refs_13_.refs_7_), channel_id=1, source_target_pairs={{0,16},{16,0},{1,17},{17,1},{2,18},{18,2},{3,19},{19,3},{4,20},{20... | collective-permute-start | bytes 3145736 | tf_op jit(solution)/shard_map/ppermute | solution.py:736
  410.8 45.0 %collective-permute-start.24 = (bf16[1024,512]{1,0:T(8,128)(2,1)}, bf16[1024,512]{1,0:T(8,128)(2,1)S(1)}, u32[]{:S(2)}, u32[]{:S(2)}) collective-permute-start(bf16[1024,512]{1,0:T(8,128)(2,1)} %collective-permute-done.23.refs_3_.refs_8_.refs_11_.refs_5_), channel_id=1, source_target_pairs={{0,16},{16,0},{1,17},{17,1},{2,18},{18,2},{3,19},{19,3},{4,20},{20... | collective-permute-start | bytes 3145736 | tf_op jit(solution)/shard_map/ppermute | solution.py:736
  411.2 44.6 %collective-permute-start.27 = (bf16[1024,512]{1,0:T(8,128)(2,1)}, bf16[1024,512]{1,0:T(8,128)(2,1)}, u32[]{:S(2)}, u32[]{:S(2)}) collective-permute-start(bf16[1024,512]{1,0:T(8,128)(2,1)} %collective-permute-done.26.refs_7_.refs_12_.refs_15_.refs_9_), channel_id=1, source_target_pairs={{0,16},{16,0},{1,17},{17,1},{2,18},{18,2},{3,19},{19,3},{4,20},{20... | collective-permute-start | bytes 3145736 | tf_op jit(solution)/shard_map/ppermute | solution.py:736
  432.2 36.4 %collective-permute-start.32 = (bf16[512,1024]{1,0:T(8,128)(2,1)}, bf16[512,1024]{1,0:T(8,128)(2,1)}, u32[]{:S(2)}, u32[]{:S(2)}) collective-permute-start(bf16[512,1024]{1,0:T(8,128)(2,1)} %constant_dynamic-slice_fusion.3), channel_id=1, source_target_pairs={{0,16},{16,0},{1,17},{17,1},{2,18},{18,2},{3,19},{19,3},{4,20},{20... | collective-permute-start | bytes 3145736 | tf_op jit(solution)/shard_map/ppermute | solution.py:736
  547.1 73.3 %collective-permute-start.29 = (bf16[512,1024]{1,0:T(8,128)(2,1)S(1)}, bf16[512,1024]{1,0:T(8,128)(2,1)}, u32[]{:S(2)}, u32[]{:S(2)}) collective-permute-start(bf16[512,1024]{1,0:T(8,128)(2,1)S(1)} %broadcast_select_fusion.8), channel_id=1, source_target_pairs={{0,16},{16,0},{1,17},{17,1},{2,18},{18,2},{3,19},{19,3},{4,20},{20... | collective-permute-start | bytes 3145736 | tf_op jit(solution)/shard_map/ppermute | solution.py:736
  690.7 38.6 %collective-permute-start.36 = (bf16[2,1024,256]{2,1,0:T(8,128)(2,1)}, bf16[2,1024,256]{2,1,0:T(8,128)(2,1)}, u32[]{:S(2)}, u32[]{:S(2)}) collective-permute-start(bf16[2,1024,256]{2,1,0:T(8,128)(2,1)} %select_convert_fusion.2), channel_id=1, source_target_pairs={{0,16},{16,0},{1,17},{17,1},{2,18},{18,2},{3,19},{19,3},{4,20},{20... | collective-permute-start | bytes 3145736 | tf_op jit(solution)/shard_map/ppermute | solution.py:736
  735.5 66.9 %collective-permute-start.35 = (bf16[512,1024]{1,0:T(8,128)(2,1)S(1)}, bf16[512,1024]{1,0:T(8,128)(2,1)S(1)}, u32[]{:S(2)}, u32[]{:S(2)}) collective-permute-start(bf16[512,1024]{1,0:T(8,128)(2,1)S(1)} %get-tuple-element.87), channel_id=1, source_target_pairs={{0,8},{8,0},{1,9},{9,1},{2,10},{10,2},{3,11},{11,3},{4,12},{12,4},... | collective-permute-start | bytes 3145736 | tf_op jit(solution)/shard_map/ppermute | solution.py:736
  (58 other events, 2193.7 us)
Sparse Core Ops, SparseCore 0:
  758.3 79.8 all-reduce.3

commit v2 on v1

v2 whole, which is shorter than its diff:
```python
import functools

import jax
import jax.numpy as jnp
from jax import lax
from jax.experimental import pallas as pl
from jax.experimental.pallas import tpu as pltpu
from jax.sharding import PartitionSpec as P

HEADDIM = 64
BUNCH = 4
WIDE = BUNCH * HEADDIM
CHUNK = 512
SCALE = HEADDIM**-0.5
LANES = 128
PART = 256
EXTRA = 16
HIDDEN_MASK = -1e30
VMEM_LIMIT = 60 * 1024 * 1024
BF16 = jnp.bfloat16
F32 = jnp.float32


def dot_nn(left, right):
    return lax.dot_general(left, right, (((1,), (0,)), ((), ())), preferred_element_type=F32)


def dot_nt(left, right):
    return lax.dot_general(left, right, (((1,), (1,)), ((), ())), preferred_element_type=F32)


def dot_tn(left, right):
    return lax.dot_general(left, right, (((0,), (0,)), ((), ())), preferred_element_type=F32)


class Plan:
    def __init__(self, bufs):
        self.pairs = []
        self.steps = []
        self.bufs = bufs

    def part(self, first, count):
        some = Plan(self.bufs)
        for copies in self.steps[first : first + count]:
            some.steps.append([(some.add(*self.pairs[c[0]]),) + tuple(c[1:]) for c in copies])
        return some

    def add(self, *arrays):
        for i, pair in enumerate(self.pairs):
            if pair[0] is arrays[0]:
                return i
        self.pairs.append(arrays)
        return len(self.pairs) - 1


def at(index):
    return lambda: index


def block(start, size):
    return pl.ds(start, size)


def advance(plan, refs, bufs, sems, layer, step):
    count = len(plan.steps)
    mine = lax.axis_index("section") == layer
    slot = lax.rem(step, 2)

    firsts = [sum(len(p) for p in plan.pairs[:i]) for i in range(len(plan.pairs))]

    def start(copies, side, to):
        for pair, source, buf, place in copies:
            src = refs[firsts[pair] + side].at[source()]
            dst = bufs[buf].at[(to,) + tuple(place())]
            pltpu.make_async_copy(src, dst, sems[buf].at[to]).start()

    def issue(which, to):
        start([c for c in plan.steps[which] if len(plan.pairs[c[0]]) == 1], 0, to)
        layered = [c for c in plan.steps[which] if len(plan.pairs[c[0]]) == 2]
        if layered:

            @pl.when(mine)
            def _():
                start(layered, 0, to)

            @pl.when(jnp.logical_not(mine))
            def _():
                start(layered, 1, to)

    @pl.when(step == 0)
    def _():
        issue(0, 0)

    for which in range(1, count):

        @pl.when(step + 1 == which)
        def _():
            issue(which, which % 2)

    used = [sorted({c[2] for c in copies}) for copies in plan.steps]

    def settle(buf):
        pltpu.make_async_copy(bufs[buf].at[slot], bufs[buf].at[slot], sems[buf].at[slot]).wait()

    first = 0
    for which in range(1, count + 1):
        if which == count or used[which] != used[first]:
            if first == 0 and which == count:
                for buf in used[first]:
                    settle(buf)
            else:

                @pl.when((step >= first) & (step < which))
                def _():
                    for buf in used[first]:
                        settle(buf)

            first = which
    return slot


def call(body, operands, in_blocks, plan, out_shapes, out_blocks, scratch, cost):
    arrays = [a for pair in plan.pairs for a in pair]
    n_ops, n_out, n_buf = len(operands), len(out_shapes), len(plan.bufs)

    def kernel(*refs):
        ins, rest = refs[:n_ops], refs[n_ops:]
        wrefs, rest = rest[: len(arrays)], rest[len(arrays) :]
        outs, rest = rest[:n_out], rest[n_out:]
        bufs, rest = rest[:n_buf], rest[n_buf:]
        sems, extra = rest[:n_buf], rest[n_buf:]
        body(ins, wrefs, outs, bufs, sems, extra)

    return pl.pallas_call(
        kernel,
        grid=(len(plan.steps),),
        in_specs=list(in_blocks) + [pl.BlockSpec(memory_space=pltpu.HBM)] * len(arrays),
        out_specs=tuple(out_blocks),
        out_shape=tuple(out_shapes),
        scratch_shapes=[pltpu.VMEM((2,) + tuple(b), BF16) for b in plan.bufs]
        + [pltpu.SemaphoreType.DMA((2,)) for _ in plan.bufs]
        + list(scratch),
        compiler_params=pltpu.CompilerParams(
            dimension_semantics=("arbitrary",), vmem_limit_bytes=VMEM_LIMIT
        ),
        cost_estimate=pl.CostEstimate(
            flops=int(3 * cost), bytes_accessed=int(cost // 200), transcendentals=0
        ),
    )(*operands, *arrays)


ALL = slice(None)
QUARTER = 128


def self_plan(near, far):
    width = near[0][0].shape[1]
    plan = Plan([(3, width, WIDE), (WIDE, width)])
    qkv, out = plan.add(*near[0]), plan.add(*near[1])
    for g in range(near[0][0].shape[2] // WIDE):
        cols = block(g * WIDE, WIDE)
        plan.steps.append(
            [(qkv, at((ALL, ALL, cols)), 0, at(())), (out, at((cols, ALL)), 1, at(()))]
        )
    for g in range(len(far) // 2):
        copies = []
        for j in range(2):
            first, second, base = far[2 * g + j]
            a, b = plan.add(*first), plan.add(*second)
            lanes = block(j * QUARTER, QUARTER)
            copies.append((a, at((block(0, 2),)), 0, at((block(0, 2), ALL, lanes))))
            copies.append((b, at((base,)), 0, at((2, ALL, lanes))))
            for k in range(width // QUARTER):
                here = block(k * QUARTER, QUARTER)
                copies.append((b, at((base + 1, here, ALL)), 1, at((lanes, here))))
        plan.steps.append(copies)
    return plan


def cross_plan(near, far):
    width = near[0][0].shape[0]
    plan = Plan([(width, WIDE), (width, WIDE)])
    ckv, cvo = plan.add(*near[0]), plan.add(*near[1])
    for g in range(near[0][0].shape[1] // WIDE):
        cols = block(g * WIDE, WIDE)
        plan.steps.append([(ckv, at((ALL, cols)), 0, at(())), (cvo, at((ALL, cols)), 1, at(()))])
    for g in range(len(far) // 2):
        copies = []
        for j in range(2):
            first, second, base = far[2 * g + j]
            a, b = plan.add(*first), plan.add(*second)
            lanes = block(j * QUARTER, QUARTER)
            copies.append((a, at((0,)), 0, at((ALL, lanes))))
            copies.append((b, at((base,)), 1, at((ALL, lanes))))
        plan.steps.append(copies)
    return plan


def branch_plan(near, far, stride):
    width, hidden = near[0][0].shape
    units = near[2][0].shape[1]
    piece = width // 8
    plan = Plan([(width, CHUNK), (CHUNK, width), (width, units), (units, width)])
    up, down, adown, aup = [plan.add(*pair) for pair in near]
    for g in range(hidden // CHUNK):
        cols = block(g * CHUNK, CHUNK)
        plan.steps.append([(up, at((ALL, cols)), 0, at(())), (down, at((cols, ALL)), 1, at(()))])
    adapter = []
    for j, both in enumerate(far):
        copies = []
        for k, (first, second, base) in enumerate(both):
            a, b = plan.add(first), plan.add(second)
            cols = block(k * WIDE, WIDE)
            copies.append((a, at((block(0, width), ALL)), 0, at((ALL, cols))))
            for n in range(width // WIDE):
                rows = block(base + n * WIDE, WIDE)
                copies.append((b, at((rows, ALL)), 1, at((cols, block(n * WIDE, WIDE)))))

            def spot(j=j, k=k):
                return block(pl.multiple_of(eighth_of(j, k, stride) * piece, piece), piece)

            rows = block(base + width, piece)
            adapter.append((b, at((rows, ALL)), 2, lambda spot=spot: (spot(), ALL)))
            for n in range(units // piece):
                rows = block(base + width + piece, piece)
                here = block(n * piece, piece)
                adapter.append(
                    (b, at((rows, here)), 3, lambda spot=spot, here=here: (here, spot()))
                )
        plan.steps.append(copies)
    plan.steps.append([(adown, at(()), 2, at(())), (aup, at(()), 3, at(()))])
    plan.steps.append(adapter)
    return plan


def share_of(j, stride):
    place = lax.axis_index("dp")
    x = lax.rem(place, 2)
    z = lax.rem(lax.div(place, stride), 2)
    x = 1 - x if j in (1, 3) else x
    z = 1 - z if j in (2, 3) else z
    return 2 * x + z


def eighth_of(j, k, stride):
    core = lax.axis_index("section")
    return 4 * (1 - core if k else core) + share_of(j, stride)


def cut_piece(pairs, layer, shape, moves):
    plan = Plan([])
    plan.pairs = pairs
    firsts = [sum(len(p) for p in pairs[:i]) for i in range(len(pairs))]
    arrays = [a for pair in pairs for a in pair]

    def kernel(*refs):
        ins, out, sem = refs[: len(arrays)], refs[-2], refs[-1]

        def start(side):
            for pair, index, place in moves:
                src = ins[firsts[pair] + side].at[index()]
                pltpu.make_async_copy(src, out.at[place()], sem).start()

        if layer is None:
            start(0)
        else:
            mine = lax.axis_index("section") == layer

            @pl.when(mine)
            def _():
                start(0)

            @pl.when(jnp.logical_not(mine))
            def _():
                start(1)

        pltpu.make_async_copy(out, out, sem).wait()

    return pl.pallas_call(
        kernel,
        in_specs=[pl.BlockSpec(memory_space=pltpu.HBM)] * len(arrays),
        out_specs=pl.BlockSpec(memory_space=pltpu.VMEM),
        out_shape=shaped(shape, BF16),
        scratch_shapes=[pltpu.SemaphoreType.DMA],
        compiler_params=pltpu.CompilerParams(vmem_limit_bytes=8 * 1024 * 1024),
    )(*arrays)


def whole(shape):
    zeros = (0,) * len(shape)
    return pl.BlockSpec(tuple(shape), lambda i: zeros)


def per_step(shape, first=0, last=None):
    def index(i):
        k = jnp.maximum(i - first, 0)
        if last is not None:
            k = jnp.minimum(k, last)
        return (k,) + (0,) * len(shape)

    return pl.BlockSpec((1,) + tuple(shape), index)


def shaped(shape, dtype):
    return jax.ShapeDtypeStruct(tuple(shape), dtype)


def normalized(value):
    center = value - jnp.mean(value, -1, keepdims=True)
    spread = jnp.mean(center * center, -1, keepdims=True)
    inverse = lax.rsqrt(spread + 1e-05)
    return center * inverse, inverse


def norm_slope(grad, hat, inverse, gain):
    scaled = grad * gain
    along = jnp.mean(scaled * hat, -1, keepdims=True)
    return inverse * (scaled - jnp.mean(scaled, -1, keepdims=True) - hat * along)


def gelu_pair(value):
    below = 0.5 + 0.5 * lax.erf(value * (0.5**0.5))
    density = jnp.exp(value * value * -0.5) * 0.3989422804014327
    return value * below, below + value * density


def lanes_of(head):
    first = head * HEADDIM // LANES * LANES
    return slice(first, first + LANES)


def only_head(value, head):
    lane = lax.broadcasted_iota(jnp.int32, (1, LANES), 1)
    inside = head * HEADDIM % LANES
    keep = (lane >= inside) & (lane < inside + HEADDIM)
    part = value[:, lanes_of(head)]
    return jnp.where(keep, part, jnp.zeros_like(part))


def attend(blocks, q_ref, k_ref, v_ref, bias_ref, valid_ref, lse_ref, out_ref):
    units = [(rows, keys, head) for rows, keys in blocks for head in range(BUNCH)]

    def scores_of(unit):
        rows, keys, head = unit
        q_head = only_head(q_ref[rows, :] * jnp.asarray(SCALE, BF16), head)
        return dot_nt(k_ref[keys, lanes_of(head)], q_head)

    ahead = scores_of(units[0])
    for i, (rows, keys, head) in enumerate(units):
        scores = ahead + bias_ref[keys, rows]
        if i + 1 < len(units):
            ahead = scores_of(units[i + 1])
        peak = jnp.max(scores, 0, keepdims=True)
        powers = jnp.exp(scores - peak)
        total = jnp.sum(powers, 0, keepdims=True)
        share = 1.0 / total
        lse = peak + jnp.log(total)
        if valid_ref is not None:
            valid = valid_ref[:, rows] > 0.0
            share = jnp.where(valid, share, 0.0)
            lse = jnp.where(valid, lse, -HIDDEN_MASK)
        lse_ref[head : head + 1, rows] = lse
        mixed = dot_tn((powers * share).astype(BF16), only_head(v_ref[keys, :], head))
        out_ref[rows, lanes_of(head)] += mixed


def attend_slope(blocks, q_ref, k_ref, v_ref, g_ref, bias_ref, lse_ref, dq_ref, dk_ref, dv_ref):
    units = [(rows, keys, head) for rows, keys in blocks for head in range(BUNCH)]

    def products_of(unit):
        rows, keys, head = unit
        q_head = only_head(q_ref[rows, :] * jnp.asarray(SCALE, BF16), head)
        g_head = only_head(g_ref[rows, :], head)
        lanes = lanes_of(head)
        return q_head, g_head, dot_nt(k_ref[keys, lanes], q_head), dot_nt(v_ref[keys, lanes], g_head)

    ahead = products_of(units[0])
    for i, (rows, keys, head) in enumerate(units):
        q_head, g_head, scores, prob_grad = ahead
        if i + 1 < len(units):
            ahead = products_of(units[i + 1])
        lanes = lanes_of(head)
        probs = jnp.exp(scores + bias_ref[keys, rows] - lse_ref[head : head + 1, rows])
        inner = jnp.sum(probs * prob_grad, 0, keepdims=True)
        score_grad = (probs * (prob_grad - inner)).astype(BF16)
        dv_ref[keys, lanes] += dot_nn(probs.astype(BF16), g_head)
        dk_ref[keys, lanes] += dot_nn(score_grad, q_head)
        dq_ref[rows, lanes] += dot_tn(score_grad, only_head(k_ref[keys, :], head))


def fill_bias(bias_ref, key_seg, row_seg, causal):
    seen = key_seg == row_seg
    if causal:
        key = lax.broadcasted_iota(jnp.int32, bias_ref.shape, 0)
        row = lax.broadcasted_iota(jnp.int32, bias_ref.shape, 1)
        seen = seen & (key <= row)
    bias_ref[...] = jnp.where(seen, 0.0, HIDDEN_MASK)


def self_blocks(rows, causal):
    count = rows // PART
    parts = [slice(i * PART, (i + 1) * PART) for i in range(count)]
    return [(part, slice(0, part.stop if causal else rows)) for part in parts]


def note_active(bias, valid, active, rows):
    for h in range(2):
        best = jnp.max(bias[h], 0, keepdims=True)
        valid[h] = jnp.where(best > 0.5 * HIDDEN_MASK, 1.0, 0.0)
        for i in range(rows // PART):
            some = jnp.max(valid[h, :, i * PART : (i + 1) * PART])
            active[h, i] = (some > 0.0).astype(jnp.int32)


def self_forward(layer, x, seg_col, seg_row, gain, plan):
    rows, width = x.shape
    steps = len(plan.steps)

    def body(ins, wrefs, outs, bufs, sems, extra):
        x_ref, segc_ref, segr_ref, gain_ref = ins
        qkv_ref, lse_ref, hat_ref, inv_ref = outs
        acc, bias, mixed = extra
        step = pl.program_id(0)
        slot = advance(plan, wrefs, bufs, sems, layer, step)

        @pl.when(step == 0)
        def _():
            fill_bias(bias, segc_ref[...], segr_ref[...], layer == 1)
            acc[...] = x_ref[...].astype(F32)

        x_rows = x_ref[...]
        w = bufs[0].at[slot]
        q = dot_nn(x_rows, w[0]).astype(BF16)
        k = dot_nn(x_rows, w[1]).astype(BF16)
        v = dot_nn(x_rows, w[2]).astype(BF16)
        qkv_ref[0, 0] = q
        qkv_ref[0, 1] = k
        qkv_ref[0, 2] = v
        mixed[...] = jnp.zeros_like(mixed)
        attend(
            self_blocks(rows, layer == 1), qkv_ref.at[0, 0], qkv_ref.at[0, 1], qkv_ref.at[0, 2],
            bias, None, lse_ref.at[0], mixed,
        )
        acc[...] += dot_nn(mixed[...].astype(BF16), bufs[1][slot])

        @pl.when(step == steps - 1)
        def _():
            hat, inverse = normalized(acc[...])
            hat_ref[...] = hat.astype(BF16)
            inv_ref[...] = inverse

    return call(
        body,
        [x, seg_col, seg_row, gain],
        [whole(x.shape), whole(seg_col.shape), whole(seg_row.shape), whole(gain.shape)],
        plan,
        [
            shaped((steps, 3, rows, WIDE), BF16),
            shaped((steps, BUNCH, rows), F32),
            shaped((rows, width), BF16),
            shaped((rows, 1), F32),
        ],
        [
            per_step((3, rows, WIDE)),
            per_step((BUNCH, rows)),
            whole((rows, width)),
            whole((rows, 1)),
        ],
        [
            pltpu.VMEM((rows, width), F32),
            pltpu.VMEM((rows, rows), F32),
            pltpu.VMEM((rows, WIDE), F32),
        ],
        steps * (2 * rows * width * WIDE * 4 + 16 * rows * rows * WIDE),
    )


def self_backward(layer, grad, base, saved, lse, seg_col, seg_row, plan, first, count):
    rows, width = grad.shape
    steps = count
    plan = plan.part(first, count)

    def body(ins, wrefs, outs, bufs, sems, extra):
        g_ref, base_ref, saved_ref, lse_ref, segc_ref, segr_ref = ins
        (dx_ref,) = outs
        acc, bias, mixed_grad, dq, dk, dv = extra
        step = pl.program_id(0)
        slot = advance(plan, wrefs, bufs, sems, layer, step)

        @pl.when(step == 0)
        def _():
            fill_bias(bias, segc_ref[...], segr_ref[...], layer == 1)
            acc[...] = base_ref[...].astype(F32)

        mixed_grad[...] = dot_nt(g_ref[...], bufs[1][slot]).astype(BF16)
        for ref in (dq, dk, dv):
            ref[...] = jnp.zeros_like(ref)
        attend_slope(
            self_blocks(rows, layer == 1), saved_ref.at[0, 0], saved_ref.at[0, 1],
            saved_ref.at[0, 2], mixed_grad, bias, lse_ref.at[0], dq, dk, dv,
        )
        w = bufs[0].at[slot]
        acc[...] += (
            dot_nt((dq[...] * SCALE).astype(BF16), w[0])
            + dot_nt(dk[...].astype(BF16), w[1])
            + dot_nt(dv[...].astype(BF16), w[2])
        )

        @pl.when(step == steps - 1)
        def _():
            dx_ref[...] = acc[...].astype(BF16)

    return call(
        body,
        [grad, base, saved, lse, seg_col, seg_row],
        [
            whole(grad.shape),
            whole(grad.shape),
            per_step((3, rows, WIDE), -first),
            per_step((BUNCH, rows), -first),
            whole(seg_col.shape),
            whole(seg_row.shape),
        ],
        plan,
        [shaped((rows, width), BF16)],
        [whole((rows, width))],
        [
            pltpu.VMEM((rows, width), F32),
            pltpu.VMEM((rows, rows), F32),
            pltpu.VMEM((rows, WIDE), BF16),
            pltpu.VMEM((rows, WIDE), F32),
            pltpu.VMEM((rows, WIDE), F32),
            pltpu.VMEM((rows, WIDE), F32),
        ],
        steps * (2 * rows * width * WIDE * 4 + 40 * rows * rows * WIDE),
    )[0]


def cross_forward(hat, gain, kv_own, kv_away, keys_col, seg_row, plan):
    rows, width = hat.shape
    steps = len(plan.steps)

    def body(ins, wrefs, outs, bufs, sems, extra):
        hat_ref, gain_ref, own_ref, away_ref, keysc_ref, segr_ref = ins
        q_ref, lse_ref, nhat_ref, inv_ref = outs
        acc, low, bias, mixed, valid, active = extra
        step = pl.program_id(0)
        slot = advance(plan, wrefs, bufs, sems, 1, step)

        @pl.when(step == 0)
        def _():
            for h in range(2):
                fill_bias(bias.at[h], keysc_ref[h], segr_ref[...], False)
            note_active(bias, valid, active, rows)
            first = hat_ref[...].astype(F32) * gain_ref[...]
            acc[...] = first
            low[...] = first.astype(BF16)

        q = dot_nn(low[...], bufs[0][slot]).astype(BF16)
        q_ref[0] = q
        mixed[...] = jnp.zeros_like(mixed)
        for h, kv_ref in enumerate((own_ref, away_ref)):
            for i, pair in enumerate(self_blocks(rows, False)):

                @pl.when(active[h, i] > 0)
                def _():
                    attend(
                        [pair], q_ref.at[0], kv_ref.at[0, 0], kv_ref.at[0, 1],
                        bias.at[h], valid.at[h], lse_ref.at[0, h], mixed,
                    )

        acc[...] += dot_nt(mixed[...].astype(BF16), bufs[1][slot])

        @pl.when(step == steps - 1)
        def _():
            nhat, inverse = normalized(acc[...])
            nhat_ref[...] = nhat.astype(BF16)
            inv_ref[...] = inverse

    return call(
        body,
        [hat, gain, kv_own, kv_away, keys_col, seg_row],
        [
            whole(hat.shape),
            whole(gain.shape),
            per_step((2, rows, WIDE)),
            per_step((2, rows, WIDE)),
            whole(keys_col.shape),
            whole(seg_row.shape),
        ],
        plan,
        [
            shaped((steps, rows, WIDE), BF16),
            shaped((steps, 2, BUNCH, rows), F32),
            shaped((rows, width), BF16),
            shaped((rows, 1), F32),
        ],
        [
            per_step((rows, WIDE)),
            per_step((2, BUNCH, rows)),
            whole((rows, width)),
            whole((rows, 1)),
        ],
        [
            pltpu.VMEM((rows, width), F32),
            pltpu.VMEM((rows, width), BF16),
            pltpu.VMEM((2, rows, rows), F32),
            pltpu.VMEM((rows, WIDE), F32),
            pltpu.VMEM((2, 1, rows), F32),
            pltpu.SMEM((2, rows // PART), jnp.int32),
        ],
        steps * (2 * rows * width * WIDE * 2 + 32 * rows * rows * WIDE),
    )


def cross_backward(grad, hat, inv, gain, saved_q, lse, kv_own, kv_away, keys_col, seg_row, plan):
    rows, width = grad.shape
    steps = len(plan.steps)

    def body(ins, wrefs, outs, bufs, sems, extra):
        g_ref, hat_ref, inv_ref, gain_ref, q_ref, lse_ref, own_ref, away_ref, keysc_ref, segr_ref = ins
        dx_ref, own_grad_ref, away_grad_ref = outs
        acc, bias, mixed_grad, dq, dk, dv, valid, active = extra
        step = pl.program_id(0)
        slot = advance(plan, wrefs, bufs, sems, 1, step)

        @pl.when(step == 0)
        def _():
            for h in range(2):
                fill_bias(bias.at[h], keysc_ref[h], segr_ref[...], False)
            note_active(bias, valid, active, rows)
            acc[...] = g_ref[...].astype(F32)

        mixed_grad[...] = dot_nn(g_ref[...], bufs[1][slot]).astype(BF16)
        for ref in (dq, dk, dv):
            ref[...] = jnp.zeros_like(ref)
        for h, kv_ref in enumerate((own_ref, away_ref)):
            for i, pair in enumerate(self_blocks(rows, False)):

                @pl.when(active[h, i] > 0)
                def _():
                    attend_slope(
                        [pair], q_ref.at[0], kv_ref.at[0, 0], kv_ref.at[0, 1], mixed_grad,
                        bias.at[h], lse_ref.at[0, h], dq, dk.at[h], dv.at[h],
                    )

        for h, out_ref in enumerate((own_grad_ref, away_grad_ref)):
            out_ref[0, 0] = dk[h].astype(BF16)
            out_ref[0, 1] = dv[h].astype(BF16)
        acc[...] += dot_nt((dq[...] * SCALE).astype(BF16), bufs[0][slot])

        @pl.when(step == steps - 1)
        def _():
            dx_ref[...] = norm_slope(
                acc[...], hat_ref[...].astype(F32), inv_ref[...], gain_ref[...]
            ).astype(BF16)

    return call(
        body,
        [grad, hat, inv, gain, saved_q, lse, kv_own, kv_away, keys_col, seg_row],
        [
            whole(grad.shape),
            whole(hat.shape),
            whole(inv.shape),
            whole(gain.shape),
            per_step((rows, WIDE)),
            per_step((2, BUNCH, rows)),
            per_step((2, rows, WIDE)),
            per_step((2, rows, WIDE)),
            whole(keys_col.shape),
            whole(seg_row.shape),
        ],
        plan,
        [
            shaped((rows, width), BF16),
            shaped((steps, 2, rows, WIDE), BF16),
            shaped((steps, 2, rows, WIDE), BF16),
        ],
        [whole((rows, width)), per_step((2, rows, WIDE)), per_step((2, rows, WIDE))],
        [
            pltpu.VMEM((rows, width), F32),
            pltpu.VMEM((2, rows, rows), F32),
            pltpu.VMEM((rows, WIDE), BF16),
            pltpu.VMEM((rows, WIDE), F32),
            pltpu.VMEM((2, rows, WIDE), F32),
            pltpu.VMEM((2, rows, WIDE), F32),
            pltpu.VMEM((2, 1, rows), F32),
            pltpu.SMEM((2, rows // PART), jnp.int32),
        ],
        steps * (2 * rows * width * WIDE * 2 + 80 * rows * rows * WIDE),
    )


def keys_forward(y, plan):
    rows, width = y.shape
    steps = len(plan.steps)

    def body(ins, wrefs, outs, bufs, sems, extra):
        (kv_ref,) = outs
        slot = advance(plan, wrefs, bufs, sems, 0, pl.program_id(0))
        kv_ref[0, 0] = dot_nn(ins[0][...], bufs[0][slot]).astype(BF16)
        kv_ref[0, 1] = dot_nn(ins[0][...], bufs[1][slot]).astype(BF16)

    return call(
        body,
        [y],
        [whole(y.shape)],
        plan,
        [shaped((steps, 2, rows, WIDE), BF16)],
        [per_step((2, rows, WIDE))],
        [],
        steps * 4 * rows * width * WIDE,
    )[0]


def keys_backward(out_grad, kv_grad, kv_grad_away, plan):
    rows, width = out_grad.shape
    steps = len(plan.steps)

    def body(ins, wrefs, outs, bufs, sems, extra):
        g_ref, own_ref, away_ref = ins
        (sum_ref,) = outs
        (acc,) = extra
        step = pl.program_id(0)
        slot = advance(plan, wrefs, bufs, sems, 0, step)

        @pl.when(step == 0)
        def _():
            acc[...] = g_ref[...].astype(F32)

        both = (own_ref[0].astype(F32) + away_ref[0].astype(F32)).astype(BF16)
        acc[...] += dot_nt(both[0], bufs[0][slot]) + dot_nt(both[1], bufs[1][slot])

        @pl.when(step == steps - 1)
        def _():
            sum_ref[...] = acc[...].astype(BF16)

    return call(
        body,
        [out_grad, kv_grad, kv_grad_away],
        [whole(out_grad.shape), per_step((2, rows, WIDE)), per_step((2, rows, WIDE))],
        plan,
        [shaped((rows, width), BF16)],
        [whole((rows, width))],
        [pltpu.VMEM((rows, width), F32)],
        steps * 4 * rows * width * WIDE,
    )[0]


def branch_forward(layer, hat, gain, out_gain, down_bias, up_bias, plan):
    rows, width = hat.shape
    nb = 2
    na = len(plan.steps) - nb
    units = down_bias.shape[-1]
    steps = na + nb

    def body(ins, wrefs, outs, bufs, sems, extra):
        hat_ref, gain_ref, ogain_ref, dbias_ref, ubias_ref = ins
        slope_ref, aslope_ref, aact_ref, nhat_ref, inv_ref, y_ref = outs
        acc, low = extra
        step = pl.program_id(0)
        slot = advance(plan, wrefs, bufs, sems, layer, step)

        @pl.when(step == 0)
        def _():
            first = hat_ref[...].astype(F32) * gain_ref[...]
            low[...] = first.astype(BF16)
            acc[...] = first + 4.0 * ubias_ref[...]

        @pl.when(step < na)
        def _():
            for at in range(0, rows, 256):
                part = slice(at, at + 256)
                act, slope = gelu_pair(dot_nn(low[part, :], bufs[0][slot]))
                slope_ref[0, part, :] = slope.astype(BF16)
                acc[part, :] += dot_nn(act.astype(BF16), bufs[1][slot])

        @pl.when(step >= na)
        def _():
            act, slope = gelu_pair(dot_nn(low[...], bufs[2][slot]) + dbias_ref[0])
            low_act = act.astype(BF16)
            aslope_ref[0] = slope.astype(BF16)
            aact_ref[0] = low_act
            acc[...] += dot_nn(low_act * jnp.asarray(4.0, BF16), bufs[3][slot])

        @pl.when(step == steps - 1)
        def _():
            nhat, inverse = normalized(acc[...])
            nhat_ref[...] = nhat.astype(BF16)
            inv_ref[...] = inverse
            y_ref[...] = (nhat * ogain_ref[...]).astype(BF16)

    return call(
        body,
        [hat, gain, out_gain, down_bias, up_bias],
        [
            whole(hat.shape),
            whole(gain.shape),
            whole(out_gain.shape),
            per_step((1, units), na),
            whole(up_bias.shape),
        ],
        plan,
        [
            shaped((na, rows, CHUNK), BF16),
            shaped((nb, rows, units), BF16),
            shaped((nb, rows, units), BF16),
            shaped((rows, width), BF16),
            shaped((rows, 1), F32),
            shaped((rows, width), BF16),
        ],
        [
            per_step((rows, CHUNK), 0, na - 1),
            per_step((rows, units), na),
            per_step((rows, units), na),
            whole((rows, width)),
            whole((rows, 1)),
            whole((rows, width)),
        ],
        [pltpu.VMEM((rows, width), F32), pltpu.VMEM((rows, width), BF16)],
        4 * rows * width * (na * CHUNK + nb * units),
    )


def branch_backward(layer, out_grad, nhat, ninv, out_gain, hat, inv, gain, slope, aslope, aact, plan):
    rows, width = hat.shape
    nb = 2
    na = len(plan.steps) - nb
    units = aact.shape[-1]
    steps = na + nb

    def body(ins, wrefs, outs, bufs, sems, extra):
        g_ref, nhat_ref, ninv_ref, ogain_ref, hat_ref, inv_ref, gain_ref, slope_ref, aslope_ref, aact_ref = ins
        dx_ref, packed_ref = outs
        acc, low, rows_low, up_bias = extra
        step = pl.program_id(0)
        slot = advance(plan, wrefs, bufs, sems, layer, step)

        @pl.when(step == 0)
        def _():
            grad = norm_slope(
                g_ref[...].astype(F32), nhat_ref[...].astype(F32), ninv_ref[...], ogain_ref[...]
            )
            acc[...] = grad
            small = grad.astype(BF16)
            low[...] = small
            up_bias[...] = 4.0 * jnp.sum(small.astype(F32), 0, keepdims=True)
            rows_low[...] = (hat_ref[...].astype(F32) * gain_ref[...]).astype(BF16)

        @pl.when(step < na)
        def _():
            for at in range(0, rows, 256):
                part = slice(at, at + 256)
                hidden = dot_nt(low[part, :], bufs[1][slot]) * slope_ref[0, part, :].astype(F32)
                acc[part, :] += dot_nt(hidden.astype(BF16), bufs[0][slot])

        @pl.when(step >= na)
        def _():
            hidden = 4.0 * dot_nt(low[...], bufs[3][slot]) * aslope_ref[0].astype(F32)
            small = hidden.astype(BF16)
            acc[...] += dot_nt(small, bufs[2][slot])
            down = dot_tn(rows_low[...], small).astype(BF16)
            for n in range(width // units):
                cols = slice(n * units, (n + 1) * units)
                packed_ref[0, 0, :units, cols] = down[cols]
            packed_ref[0, 1, :units] = (4.0 * dot_tn(aact_ref[0], low[...])).astype(BF16)
            bias = jnp.sum(small.astype(F32), 0, keepdims=True)
            bias = jnp.concatenate([bias] + [jnp.zeros_like(bias)] * (width // units - 1), 1)
            row = lax.broadcasted_iota(jnp.int32, (EXTRA, width), 0)
            last = jnp.where(row == 0, bias, jnp.where(row == 1, up_bias[...], 0.0))
            packed_ref[0, 0, units:] = jnp.zeros((EXTRA, width), BF16)
            packed_ref[0, 1, units:] = last.astype(BF16)

        @pl.when(step == steps - 1)
        def _():
            dx_ref[...] = norm_slope(
                acc[...], hat_ref[...].astype(F32), inv_ref[...], gain_ref[...]
            ).astype(BF16)

    return call(
        body,
        [out_grad, nhat, ninv, out_gain, hat, inv, gain, slope, aslope, aact],
        [
            whole(out_grad.shape),
            whole(nhat.shape),
            whole(ninv.shape),
            whole(out_gain.shape),
            whole(hat.shape),
            whole(inv.shape),
            whole(gain.shape),
            per_step((rows, CHUNK), 0, na - 1),
            per_step((rows, units), na),
            per_step((rows, units), na),
        ],
        plan,
        [
            shaped((rows, width), BF16),
            shaped((nb, 2, units + EXTRA, width), BF16),
        ],
        [
            whole((rows, width)),
            per_step((2, units + EXTRA, width), na),
        ],
        [
            pltpu.VMEM((rows, width), F32),
            pltpu.VMEM((rows, width), BF16),
            pltpu.VMEM((rows, width), BF16),
            pltpu.VMEM((1, width), F32),
        ],
        4 * rows * width * (na * CHUNK + nb * units),
    )


class Lane:
    def __init__(self, depth):
        self.depth = depth
        self.sent = []

    def send(self, value, axes, route):
        if len(self.sent) >= self.depth:
            value, _ = lax.optimization_barrier((value, self.sent[-self.depth]))
        got = lax.ppermute(value, axes, route)
        self.sent.append(got)
        return got


MESH_AXES = ("section", "mp", "dp")


def route(axis, flip, core=None):
    sizes = [lax.axis_size(a) for a in MESH_AXES]
    pairs = []
    for s in range(sizes[0]):
        for m in range(sizes[1]):
            for d in range(sizes[2]):
                if core is not None and s != core:
                    continue
                to = [s, m, d]
                to[MESH_AXES.index(axis)] ^= flip
                number = lambda p: (p[0] * sizes[1] + p[1]) * sizes[2] + p[2]
                pairs.append((number((s, m, d)), number(to)))
    return pairs


def after(value, token):
    return lax.optimization_barrier((value, token))[0]


def swap(value, axis):
    return jax.tree.map(lambda a: lax.ppermute(a, axis, [(0, 1), (1, 0)]), value)


def rotated(pieces, start, count):
    return lax.dynamic_slice_in_dim(jnp.concatenate(pieces, 0), start, count, 0)


def per_device(
    inputs,
    segment_ids,
    cotangent,
    norm_gains,
    cross_gain,
    self_qkv,
    self_out,
    cross_kv,
    cross_vo,
    ffn_in,
    ffn_out,
    adapter_down,
    adapter_down_bias,
    adapter_up,
    adapter_up_bias,
):
    core = lax.axis_index("section")
    side = lax.axis_index("mp")
    first_core = core == 0
    seq = segment_ids.shape[2]
    half = seq // 2
    width = inputs.shape[3]
    units = adapter_down.shape[2]

    stride = max(lax.axis_size("dp") // 4, 1)
    lane_y, lane_x, lane_z = Lane(1), Lane(2), Lane(2)

    def over_y(value):
        return lane_y.send(value, MESH_AXES, route("mp", 1))

    def over_x(value):
        return lane_x.send(value, MESH_AXES, route("dp", 1))

    def over_z(value):
        return lane_z.send(value, MESH_AXES, route("dp", stride))

    def near_pairs(*arrays):
        return [(a, swap(a, "section")) for a in arrays]

    def share(j, size):
        return block(pl.multiple_of(share_of(j, stride) * size, size), size)

    def eighth(j, size):
        return block(pl.multiple_of(eighth_of(j, 0, stride) * size, size), size)

    def columns(n, size):
        return block(n * size, size)

    qkv = jnp.transpose(self_qkv[0], (1, 0, 2))
    near_self = near_pairs(qkv, self_out[0])

    def self_piece(j):
        moves = [(0, lambda: (ALL, ALL, share(j, QUARTER)), at((block(0, 3),)))]
        moves += [
            (1, lambda n=n: (share(j, QUARTER), columns(n, QUARTER)), at((3, columns(n, QUARTER))))
            for n in range(width // QUARTER)
        ]
        return cut_piece([(qkv,), (self_out[0],)], None, (4, width, QUARTER), moves)

    piece = width // 8

    def ffn_piece(layer, j):
        moves = [(0, lambda: (ALL, eighth(j, WIDE)), at((block(0, width), ALL)))]
        moves += [
            (1, lambda n=n: (eighth(j, WIDE), columns(n, WIDE)), at((block(width + n * WIDE, WIDE), ALL)))
            for n in range(width // WIDE)
        ]
        moves += [(2, lambda: (eighth(j, piece), ALL), at((block(2 * width, piece), ALL)))]
        moves += [
            (
                3,
                lambda n=n: (columns(n, piece), eighth(j, piece)),
                at((block(2 * width + piece, piece), columns(n, piece))),
            )
            for n in range(units // piece)
        ]
        return cut_piece(near_ffn, layer, (2 * width + 2 * piece, WIDE), moves)

    def cross_piece(j):
        moves = [(n, lambda: (ALL, share(j, QUARTER)), at((n,))) for n in range(2)]
        return cut_piece([(cross_kv[0],), (cross_vo[0],)], None, (2, width, QUARTER), moves)

    def swapped(value):
        return swap(value, "section")

    def quarters(pieces, swaps, base):
        return [((p, q), (p, q), base) for p, q in zip(pieces, swaps)]

    def eighths(pieces, swaps, base):
        return [((p, p, base), (q, q, base)) for p, q in zip(pieces, swaps)]

    def swapped_after(pieces, token):
        return [swapped(after(p, token)) for p in pieces]

    bias_near = adapter_down_bias[0][None]
    bias_far = over_y(bias_near)
    small = jnp.concatenate(
        [
            norm_gains[0],
            adapter_up_bias,
            jnp.concatenate([bias_near, bias_far, jnp.zeros((1, width - 2 * units), F32)], 1),
        ],
        0,
    )
    small_other = swap(small, "section")
    enc_small = jnp.where(first_core, small, small_other)
    dec_small = jnp.where(first_core, small_other, small)

    def small_of(s):
        down_bias = jnp.stack([s[3:4, :units], s[3:4, units : 2 * units]], 0)
        return s[0:1], s[1:2], s[2:3], down_bias

    enc_gain1, enc_gain2, enc_upb, enc_downb = small_of(enc_small)
    dec_gain1, dec_gain2, dec_upb, dec_downb = small_of(dec_small)
    mid_gain = cross_gain[None]

    segs = lax.dynamic_index_in_dim(segment_ids, side, 1, keepdims=False)
    docs = jnp.arange(seq)
    counts = jnp.sum(segs[:, :, None] == docs[None, None, :8], 1)
    largest = jnp.argmax(counts, 1)
    starts = jnp.sum(segs < largest[:, None], 1).astype(jnp.int32)

    def halves_of_seg(seg, start):
        twice = jnp.concatenate([seg, seg], 0)
        mine = lax.dynamic_slice_in_dim(twice, start + half * core, half, 0)
        away = lax.dynamic_slice_in_dim(twice, start + half * (1 - core), half, 0)
        return mine, away

    enc_seg, enc_seg_away = halves_of_seg(segs[0], starts[0])
    dec_seg, _ = halves_of_seg(segs[1], starts[1])
    own_start = jnp.where(first_core, starts[0], starts[1])

    def rows_sent(value, token=None):
        keep = lax.dynamic_index_in_dim(value[0], side, 0, keepdims=False)
        give = lax.dynamic_index_in_dim(value[0], 1 - side, 0, keepdims=False)
        return keep, over_y(give if token is None else after(give, token))

    def rows_here(keep, got):
        start = lax.rem(own_start + seq - half * side, seq)
        ring = (keep, got, keep, got)
        mine = rotated(ring, start + half * core, half)
        away = rotated(ring, lax.rem(start + half * (1 - core), seq), half)
        other = swap(away, "section")
        return jnp.where(first_core, mine, other), jnp.where(first_core, other, mine)

    def slices_back(big, rest, start):
        ring = (big, rest, big, rest)
        keep = rotated(ring, lax.rem(half * side + seq - start, seq), half)
        give = rotated(ring, lax.rem(half * (1 - side) + seq - start, seq), half)
        return keep, give

    def by_row(keep, got):
        return jnp.where(side == 0, jnp.stack([keep, got]), jnp.stack([got, keep]))

    def rows_back(enc, dec):
        mine = jnp.where(first_core, enc, dec)
        away = jnp.where(first_core, dec, enc)
        other = swap(away, "section")
        big = jnp.where(first_core, mine, other)
        rest = jnp.where(first_core, other, mine)
        keep, give = slices_back(big, rest, own_start)
        return by_row(keep, swap(give, "mp"))

    def layer_back(layer, value):
        other = lax.ppermute(value, MESH_AXES, route("section", 1, 1 - layer))
        big, rest = (value, other) if layer == 0 else (other, value)
        keep, give = slices_back(big, rest, starts[layer])
        return by_row(keep, lax.ppermute(give, MESH_AXES, route("mp", 1, layer)))

    x_keep, x_got = rows_sent(inputs)
    near_ffn = near_pairs(ffn_in[0], ffn_out[0], adapter_down[0], adapter_up[0])
    near_cross = near_pairs(cross_kv[0], cross_vo[0])
    near_other = [pair[1] for pair in near_self + near_ffn + near_cross]
    self_0 = over_y(after(self_piece(0), near_other))
    self_3 = over_y(self_piece(3))
    self_1, self_2 = over_x(self_0), over_z(self_0)
    self_swaps = [swapped(p) for p in (self_0, self_1, self_2)]
    self_swaps.append(swapped(after(self_3, (self_1, self_2))))
    cross_0 = over_y(after(cross_piece(0), (self_1, self_2)))
    enc_0 = over_y(ffn_piece(0, 0))
    lane_y.depth = 2
    x_enc, x_dec = rows_here(x_keep, x_got)
    w_self = self_plan(near_self, quarters((self_0, self_1, self_2, self_3), self_swaps, 2))

    enc_col, enc_row = enc_seg[:, None], enc_seg[None, :]
    dec_col, dec_row = dec_seg[:, None], dec_seg[None, :]
    all_keys = jnp.stack([enc_seg, enc_seg_away], 0)[:, :, None]

    e_qkv, e_lse, e_hat1, e_inv1 = self_forward(0, x_enc, enc_col, enc_row, enc_gain1, w_self)
    enc_1, enc_2 = over_x(after(enc_0, e_inv1)), over_z(after(enc_0, e_inv1))
    enc_3 = over_y(after(ffn_piece(0, 3), e_inv1))
    d_qkv, d_lse, d_hat1, d_inv1 = self_forward(
        1, after(x_dec, e_inv1), dec_col, dec_row, dec_gain1, w_self
    )
    enc = (enc_0, enc_1, enc_2, enc_3)
    w_enc = branch_plan(near_ffn, eighths(enc, swapped_after(enc, d_inv1), width), stride)
    cross_1, cross_2 = over_x(after(cross_0, d_inv1)), over_z(after(cross_0, d_inv1))
    cross_3 = over_y(after(cross_piece(3), d_inv1))
    dec_0 = over_y(after(ffn_piece(1, 0), d_inv1))
    e_slope, e_aslope, e_aact, e_hat2, e_inv2, y_enc = branch_forward(
        0, after(e_hat1, d_inv1), enc_gain1, enc_gain2, enc_downb, enc_upb, w_enc
    )
    crosses = (cross_0, cross_1, cross_2, cross_3)
    cross_swaps = swapped_after(crosses, e_inv2)
    w_cross = cross_plan(near_cross, quarters(crosses, cross_swaps, 1))
    dec_3 = over_y(after(ffn_piece(1, 3), e_inv2))
    kv = keys_forward(y_enc, w_cross)
    kv_away = swap(kv, "section")
    dec_1, dec_2 = over_x(after(dec_0, kv)), over_z(after(dec_0, kv))
    d_q, c_lse, d_hat2, d_inv2 = cross_forward(
        d_hat1, dec_gain1, kv, kv_away, all_keys, dec_row, w_cross
    )
    dec = (dec_0, dec_1, dec_2, dec_3)
    w_dec = branch_plan(near_ffn, eighths(dec, swapped_after(dec, d_inv2), width), stride)
    g_keep, g_got = rows_sent(cotangent, d_inv2)
    d_slope, d_aslope, d_aact, d_hat3, d_inv3, y_dec = branch_forward(
        1, d_hat2, mid_gain, dec_gain2, dec_downb, dec_upb, w_dec
    )
    g_enc, g_dec = rows_here(g_keep, g_got)

    def summed_here(grads):
        keep = lax.dynamic_index_in_dim(grads, core, 1, keepdims=False)
        give = lax.dynamic_index_in_dim(grads, 1 - core, 1, keepdims=False)
        return (keep.astype(F32) + swap(give, "section").astype(F32)).astype(BF16)

    def summed_side(both, token):
        got = after(swap(both[1], "mp"), token)
        return (both[0].astype(F32) + got.astype(F32)).astype(BF16)

    def summed_rows(value, over, token):
        for flip in over:
            got = after(lax.ppermute(value, MESH_AXES, route("dp", flip)), token)
            value = (value.astype(F32) + got.astype(F32)).astype(BF16)
        return value

    flips = [1 << i for i in range(lax.axis_size("dp").bit_length() - 1)]
    d_mid, d_grads = branch_backward(
        1, g_dec, d_hat3, d_inv3, dec_gain2, d_hat2, d_inv2, mid_gain,
        d_slope, d_aslope, d_aact, w_dec,
    )
    d_both = summed_here(d_grads)
    d_first, kv_grad, kv_grad_give = cross_backward(
        after(d_mid, d_both), d_hat1, d_inv1, dec_gain1, d_q, c_lse, kv, kv_away, all_keys, dec_row,
        w_cross,
    )
    d_total = summed_side(d_both, d_first)
    kv_grad_away = swap(kv_grad_give, "section")
    e_out = keys_backward(after(g_enc, d_total), kv_grad, kv_grad_away, w_cross)
    e_first, e_grads = branch_backward(
        0, e_out, e_hat2, e_inv2, enc_gain2, e_hat1, e_inv1, enc_gain1,
        e_slope, e_aslope, e_aact, w_enc,
    )
    e_both = summed_here(e_grads)
    d_total = summed_rows(d_total, flips[:1], e_first)
    d_first = after(d_first, e_both)
    bunches = len(w_self.steps) // 2

    def self_part(layer, grad, base, saved, lse, col, row, n):
        return self_backward(
            layer, grad, base, saved, lse, col, row, w_self, n * bunches, bunches
        )

    dx_dec = self_part(1, d_first, d_first, d_qkv, d_lse, dec_col, dec_row, 0)
    e_total = summed_side(e_both, dx_dec)
    d_total = summed_rows(d_total, flips[1:2], dx_dec)
    outputs = rows_back(y_enc, y_dec)
    dx_dec = self_part(1, d_first, after(dx_dec, (e_total, outputs)), d_qkv, d_lse, dec_col, dec_row, 1)
    e_total = summed_rows(e_total, flips[:1], dx_dec)
    d_total = summed_rows(d_total, flips[2:], dx_dec)
    e_first = after(e_first, (dx_dec, e_total))
    dx_enc = self_part(0, e_first, e_first, e_qkv, e_lse, enc_col, enc_row, 0)
    e_total = summed_rows(e_total, flips[1:2], dx_enc)
    dx_dec_back = layer_back(1, dx_dec)
    dx_enc = self_part(
        0, e_first, after(dx_enc, (e_total, d_total, dx_dec_back)), e_qkv, e_lse, enc_col, enc_row, 1
    )
    e_total = summed_rows(e_total, flips[2:], dx_enc)
    dx = jnp.where(first_core, layer_back(0, dx_enc), dx_dec_back)
    mine = jnp.where(first_core, e_total, d_total)
    other = swap(jnp.where(first_core, d_total, e_total), "section")
    down_total = jnp.where(first_core, mine, other)[:units].astype(F32)
    down_total = jnp.transpose(down_total.reshape(units, -1, units), (1, 0, 2)).reshape(width, units)
    up_total = jnp.where(first_core, other, mine).astype(F32)
    dx = jnp.where(first_core, layer_back(0, dx_enc), dx_dec_back)

    return (
        outputs[None],
        dx.astype(F32)[None],
        down_total[None],
        up_total[units : units + 1, :units],
        up_total[:units][None],
        up_total[units + 1 : units + 2],
    )


def solution(mesh):
    in_specs = (
        P("section", "dp", "mp", None),
        P(None, "dp", None),
        P("section", "dp", "mp", None),
        P("section", None, None),
        P(),
        P("section", None, None, "mp"),
        P("section", "mp", None),
        P("section", None, "mp"),
        P("section", None, "mp"),
        P("section", None, "mp"),
        P("section", "mp", None),
        P("section", None, "mp"),
        P("section", "mp"),
        P("section", "mp", None),
        P("section", None),
    )
    out_specs = (
        P("section", "dp", "mp", None),
        P("section", "dp", "mp", None),
        P("section", None, "mp"),
        P("section", "mp"),
        P("section", "mp", None),
        P("section", None),
    )
    return jax.shard_map(
        per_device, mesh=mesh, in_specs=in_specs, out_specs=out_specs, check_vma=False
    )
```

time: 860 us -> 625 us (0.73)
  waiting for transfers between devices: 436 us -> 182 us
  starting transfers between devices: 25.7 us -> 73.8 us
  local copies, waits for them, and re-layouts: 22.1 us -> 48.1 us
  blocking collectives: 22 us -> 0 us
  Pallas kernels: 291 us -> 276 us
  between operations: 18.2 us -> 7.97 us
    ppermute x44 -> x36, waiting for transfers between devices: 402 us -> 31.8 us  [swap(): lax.ppermute(a, axis, [(0, 1), (1, 0)])]
    ppermute x0 -> x29, waiting for transfers between devices: none -> 150 us  [the longest x19 112 us: send(): got = lax.ppermute(value, axes, route)]
    ppermute x0 -> x29, starting transfers between devices: none -> 49.4 us  [the longest x19 24.7 us: send(): got = lax.ppermute(value, axes, route)]
    psum x1 -> x0, waiting for transfers between devices: 33.4 us -> none  [over_dp(): return lax.psum(value.astype(BF16), 'dp').astype(F32)]
    psum x1 -> x0, blocking collectives: 22 us -> none  [over_dp(): return lax.psum(value.astype(BF16), 'dp').astype(F32)]
    pallas_call x12 -> x22, Pallas kernels: 291 us -> 276 us  [the longest x14 270 us: call(): pl.pallas_call(kernel, grid=(len(plan.steps),), in_specs=list(in_blocks)...]
    unnamed x75 -> x115, local copies, waits for them, and re-layouts: 9.03 us -> 20.7 us
    ppermute x44 -> x36, starting transfers between devices: 25.7 us -> 24.4 us  [swap(): lax.ppermute(a, axis, [(0, 1), (1, 0)])]
  transfers between devices with their start and end apart: 45 -> 65, of which waited for: 14 -> 26; matrix products, arithmetic and copies ran while one was open for 5% -> 8% of each run, Pallas kernels for 24% -> 35%
where the time goes in v2:
time: 625 us; the launch traced here: 620 us
  Pallas kernels  276 us (44%)
  waiting for transfers between devices  182 us (29%)
  starting transfers between devices  73.8 us (12%)
  local copies, waits for them, and re-layouts  48.1 us (8%)
  other arithmetic  32.2 us (5%)
  between operations  7.97 us (1%)
    pallas_call x14, Pallas kernels, call(): pl.pallas_call(kernel, grid=(len(plan.steps),), in_specs=list(in_blocks)...  270 us
    ppermute x19, waiting for transfers between devices, send(): got = lax.ppermute(value, axes, route)  112 us
    ppermute x36, waiting for transfers between devices, swap(): lax.ppermute(a, axis, [(0, 1), (1, 0)])  31.8 us
    ppermute x6, waiting for transfers between devices, summed_rows(): got = after(lax.ppermute(value, MESH_AXES, route('dp', flip)), token)  30.8 us
    ppermute x19, starting transfers between devices, send(): got = lax.ppermute(value, axes, route)  24.7 us
    ppermute x36, starting transfers between devices, swap(): lax.ppermute(a, axis, [(0, 1), (1, 0)])  24.4 us
    unnamed x115, local copies, waits for them, and re-layouts  20.7 us
    ppermute x6, starting transfers between devices, summed_rows(): got = after(lax.ppermute(value, MESH_AXES, route('dp', flip)), token)  15.7 us
  transfers between devices with their start and end apart: 65, of which 26 were waited for; matrix products, arithmetic and copies ran while one was open for 8% of the time, Pallas kernels for 35%

profile of v2, /device:TPU:0, one launch (start us, length us, event | category | flops | bytes accessed | tf_op | source)
XLA Modules:
  0.0 620.1 jit_solution(4810851179474112944)
XLA Ops:
  28.0 23.2 %collective-permute-done.1 = bf16[512,1024]{1,0:T(8,128)(2,1)S(1)} collective-permute-done((bf16[512,1024]{1,0:T(8,128)(2,1)S(1)}, bf16[512,1024]{1,0:T(8,128)(2,1)S(1)}, u32[]{:S(2)}, u32[]{:S(2)}) %collective-permute-start.1) | collective-permute-done | bytes 1048608 | tf_op jit(solution)/shard_map/ppermute | solution.py:922
  55.1 20.8 %collective-permute-done.12.refs_8_.refs_6_ = bf16[4,1024,128]{2,1,0:T(8,128)(2,1)} collective-permute-done((bf16[4,1024,128]{2,1,0:T(8,128)(2,1)S(1)}, bf16[4,1024,128]{2,1,0:T(8,128)(2,1)}, u32[]{:S(2)}, u32[]{:S(2)}) %collective-permute-start.12) | collective-permute-done | bytes 1048608 | tf_op jit(solution)/shard_map/ppermute | solution.py:922
  92.0 8.0 %collective-permute-done.18.refs_14_.refs_12_ = bf16[4,1024,128]{2,1,0:T(8,128)(2,1)} collective-permute-done((bf16[4,1024,128]{2,1,0:T(8,128)(2,1)}, bf16[4,1024,128]{2,1,0:T(8,128)(2,1)}, u32[]{:S(2)}, u32[]{:S(2)}) %collective-permute-start.18) | collective-permute-done | bytes 1048608 | tf_op jit(solution)/shard_map/ppermute | solution.py:922
  119.3 19.8 %shard_map.192 = (bf16[4,3,512,256]{3,2,1,0:T(8,128)(2,1)}, f32[4,4,512]{2,1,0:T(4,128)}, bf16[512,1024]{1,0:T(8,128)(2,1)}, f32[512,1]{1,0:T(8,128)}) custom-call(bf16[512,1024]{1,0:T(8,128)(2,1)} %get-tuple-element.180.refs_0_, s32[512,1]{1,0:T(8,128)} %copy.35.refs_1_.refs_4_, s32[1,512]{1,0:T(1,128)} %bitcast.152, ...), custom_call_target="tpu_custom_call" | custom-call | flops 25769803776 | bytes 42949672 | tf_op jit(solution)/shard_map/pallas_call | solution.py:134
  140.8 7.2 %collective-permute-done.21.refs_13_.refs_18_ = bf16[2304,256]{1,0:T(8,128)(2,1)} collective-permute-done((bf16[2304,256]{1,0:T(8,128)(2,1)}, bf16[2304,256]{1,0:T(8,128)(2,1)}, u32[]{:S(2)}, u32[]{:S(2)}) %collective-permute-start.21) | collective-permute-done | bytes 1179680 | tf_op jit(solution)/shard_map/ppermute | solution.py:922
  150.1 19.5 %shard_map.193 = (bf16[4,3,512,256]{3,2,1,0:T(8,128)(2,1)}, f32[4,4,512]{2,1,0:T(4,128)}, bf16[512,1024]{1,0:T(8,128)(2,1)}, f32[512,1]{1,0:T(8,128)}) custom-call(bf16[512,1024]{1,0:T(8,128)(2,1)} %get-tuple-element.99.refs_0_, s32[512,1]{1,0:T(8,128)} %copy.36.refs_1_.refs_4_, s32[1,512]{1,0:T(1,128)} %bitcast.159, ...), custom_call_target="tpu_custom_call" | custom-call | flops 25769803776 | bytes 42949672 | tf_op jit(solution)/shard_map/pallas_call | solution.py:134
  179.7 24.0 %shard_map.197 = (bf16[8,512,512]{2,1,0:T(8,128)(2,1)}, bf16[2,512,256]{2,1,0:T(8,128)(2,1)}, bf16[2,512,256]{2,1,0:T(8,128)(2,1)}, bf16[512,1024]{1,0:T(8,128)(...) custom-call(bf16[512,1024]{1,0:T(8,128)(2,1)} %get-tuple-element.101.refs_0_.refs_4_, ...), custom_call_target="tpu_custom_call" | custom-call | flops 28991029248 | bytes 48318384 | tf_op jit(solution)/shard_map/pallas_call | solution.py:134
  233.4 19.5 %collective-permute-done.37.refs_13_.refs_18_ = bf16[2304,256]{1,0:T(8,128)(2,1)} collective-permute-done((bf16[2304,256]{1,0:T(8,128)(2,1)}, bf16[2304,256]{1,0:T(8,128)(2,1)}, u32[]{:S(2)}, u32[]{:S(2)}) %collective-permute-start.37) | collective-permute-done | bytes 1179680 | tf_op jit(solution)/shard_map/ppermute | solution.py:922
  255.5 23.2 %shard_map.200 = (bf16[4,512,256]{2,1,0:T(8,128)(2,1)}, f32[4,2,4,512]{3,2,1,0:T(4,128)}, bf16[512,1024]{1,0:T(8,128)(2,1)}, f32[512,1]{1,0:T(8,128)}) custom-call(bf16[512,1024]{1,0:T(8,128)(2,1)} %get-tuple-element.113.refs_0_.refs_1_, f32[1,1024]{1,0:T(1,128)} %get-tuple-element.198.refs_3_.refs_1_, bf16[4,2,512,256]{3,2,1,0:T(8,128)(2,1)} %shard_map.199.refs_2_.refs_6_, ...), custom_call_target="tpu_custom_call" | custom-call | flops 32212254720 | bytes 53687092 | tf_op jit(solution)/shard_map/pallas_call | solution.py:134
  284.3 18.5 %collective-permute-done.47 = bf16[512,1024]{1,0:T(8,128)(2,1)} collective-permute-done((bf16[512,1024]{1,0:T(8,128)(2,1)S(1)}, bf16[512,1024]{1,0:T(8,128)(2,1)}, u32[]{:S(2)}, u32[]{:S(2)}) %collective-permute-start.47) | collective-permute-done | bytes 1048608 | tf_op jit(solution)/shard_map/ppermute | solution.py:922
  309.0 24.3 %shard_map.203 = (bf16[8,512,512]{2,1,0:T(8,128)(2,1)}, bf16[2,512,256]{2,1,0:T(8,128)(2,1)}, bf16[2,512,256]{2,1,0:T(8,128)(2,1)}, bf16[512,1024]{1,0:T(8,128)(...) custom-call(bf16[512,1024]{1,0:T(8,128)(2,1)} %get-tuple-element.124.refs_0_.refs_4_, f32[1,1024]{1,0:T(1,128)} %bitcast.165, ...), custom_call_target="tpu_custom_call" | custom-call | flops 28991029248 | bytes 48318384 | tf_op jit(solution)/shard_map/pallas_call | solution.py:134
  336.5 25.2 %shard_map.204 = (bf16[512,1024]{1,0:T(8,128)(2,1)}, bf16[2,2,272,1024]{3,2,1,0:T(8,128)(2,1)}) custom-call(bf16[512,1024]{1,0:T(8,128)(2,1)} %get-tuple-element.178.refs_0_, bf16[512,1024]{1,0:T(8,128)(2,1)} %get-tuple-element.140.refs_1_, f32[512,1]{1,0:T(8,128)} %get-tuple-element.141.refs_2_, f32[1,1024]{1,0:T(1,128)} %get-tuple-element.197.refs_2_.refs_3_, ...), custom_call_target="tpu_custom_call" | custom-call | flops 28991029248 | bytes 48318384 | tf_op jit(solution)/shard_map/pallas_call | solution.py:134
  369.1 29.1 %shard_map.205 = (bf16[512,1024]{1,0:T(8,128)(2,1)}, bf16[4,2,512,256]{3,2,1,0:T(8,128)(2,1)}, bf16[4,2,512,256]{3,2,1,0:T(8,128)(2,1)}) custom-call(bf16[512,1024]{1,0:T(8,128)(2,1)} %get-tuple-element.147.refs_0_, bf16[512,1024]{1,0:T(8,128)(2,1)} %get-tuple-element.113.refs_0_.refs_1_, f32[512,1]{1,0:T(8,128)} %get-tuple-element.100.refs_2_, ...), custom_call_target="tpu_custom_call" | custom-call | flops 70866960384 | bytes 118111600 | tf_op jit(solution)/shard_map/pallas_call | solution.py:134
  398.1 9.0 %collective-permute-start.51 = (bf16[4,2,512,256]{3,2,1,0:T(8,128)(2,1)}, bf16[4,2,512,256]{3,2,1,0:T(8,128)(2,1)}, u32[]{:S(2)}, u32[]{:S(2)}) collective-permute-start(bf16[4,2,512,256]{3,2,1,0:T(8,128)(2,1)} %get-tuple-element.154), channel_id=1, source_target_pairs={{0,16},{16,0},{1,17},{17,1},{2,18},{18,2},{3,19},{19,3},{4,20},{20... | collective-permute-start | bytes 6291464 | tf_op jit(solution)/shard_map/ppermute | solution.py:950
  409.8 12.0 %collective-permute-done.50 = bf16[272,1024]{1,0:T(8,128)(2,1)S(1)} collective-permute-done((bf16[272,1024]{1,0:T(8,128)(2,1)S(1)}, bf16[272,1024]{1,0:T(8,128)(2,1)S(1)}, u32[]{:S(2)}, u32[]{:S(2)}) %collective-permute-start.50) | collective-permute-done | bytes 557088 | tf_op jit(solution)/shard_map/ppermute | solution.py:950
  422.0 8.5 %shard_map.206.refs_0_ = bf16[512,1024]{1,0:T(8,128)(2,1)} custom-call(bf16[512,1024]{1,0:T(8,128)(2,1)} %get-tuple-element.152.refs_0_, bf16[4,2,512,256]{3,2,1,0:T(8,128)(2,1)} %get-tuple-element.153.refs_1_, bf16[4,2,512,256]{3,2,1,0:T(8,128)(2,1)} %collective-permute-done.51.refs_2_, bf16[1024,512]{1,0:T(8,128)(2,1)} %bitcast.135, ...), custom_call_target="tpu_custom_call" | custom-call | flops 6442450944 | bytes 10737418 | tf_op jit(solution)/shard_map/pallas_call | solution.py:134
  430.5 25.3 %shard_map.207 = (bf16[512,1024]{1,0:T(8,128)(2,1)}, bf16[2,2,272,1024]{3,2,1,0:T(8,128)(2,1)}) custom-call(bf16[512,1024]{1,0:T(8,128)(2,1)} %shard_map.206.refs_0_, bf16[512,1024]{1,0:T(8,128)(2,1)} %get-tuple-element.155.refs_1_, f32[512,1]{1,0:T(8,128)} %get-tuple-element.114.refs_2_, f32[1,1024]{1,0:T(1,128)} %get-tuple-element.202.refs_2_.refs_3_, ...), custom_call_target="tpu_custom_call" | custom-call | flops 28991029248 | bytes 48318384 | tf_op jit(solution)/shard_map/pallas_call | solution.py:134
  464.5 8.8 %collective-permute-done.56 = bf16[272,1024]{1,0:T(8,128)(2,1)} collective-permute-done((bf16[272,1024]{1,0:T(8,128)(2,1)S(1)}, bf16[272,1024]{1,0:T(8,128)(2,1)}, u32[]{:S(2)}, u32[]{:S(2)}) %collective-permute-start.56) | collective-permute-done | bytes 557088 | tf_op jit(solution)/shard_map/ppermute | solution.py:1189
  478.7 15.4 %shard_map.208.refs_1_ = bf16[512,1024]{1,0:T(8,128)(2,1)} custom-call(bf16[512,1024]{1,0:T(8,128)(2,1)} %get-tuple-element.161.refs_0_.refs_1_, bf16[512,1024]{1,0:T(8,128)(2,1)} %get-tuple-element.161.refs_0_.refs_1_, bf16[4,3,512,256]{3,2,1,0:T(8,128)(2,1)} %get-tuple-element.162.refs_2_, f32[4,4,512]{2,1,0:T(4,128)} %get-tuple-element.163.refs_3_, ...), custom_call_target="tpu_custom_call" | custom-call | flops 22548578304 | bytes 37580964 | tf_op jit(solution)/shard_map/pallas_call | solution.py:134
  494.3 9.0 %collective-permute-start.58 = (bf16[272,1024]{1,0:T(8,128)(2,1)S(1)}, bf16[272,1024]{1,0:T(8,128)(2,1)S(1)}, u32[]{:S(2)}, u32[]{:S(2)}) collective-permute-start(bf16[272,1024]{1,0:T(8,128)(2,1)S(1)} %add_convert_fusion.2), channel_id=1, source_target_pairs={{0,4},{1,5},{2,6},{3,7},{4,0},{5,1},{6,2},{7,3},{8,12},{9,13},{10,... | collective-permute-start | bytes 1671176 | tf_op jit(solution)/shard_map/ppermute | solution.py:1189
  505.3 15.1 %shard_map.209 = bf16[512,1024]{1,0:T(8,128)(2,1)} custom-call(bf16[512,1024]{1,0:T(8,128)(2,1)} %get-tuple-element.161.refs_0_.refs_1_, bf16[512,1024]{1,0:T(8,128)(2,1)} %shard_map.208.refs_1_, bf16[4,3,512,256]{3,2,1,0:T(8,128)(2,1)} %get-tuple-element.162.refs_2_, f32[4,4,512]{2,1,0:T(4,128)} %get-tuple-element.163.refs_3_, ...), custom_call_target="tpu_custom_call" | custom-call | flops 22548578304 | bytes 37580964 | tf_op jit(solution)/shard_map/pallas_call | solution.py:134
  527.7 16.5 %shard_map.210.refs_1_ = bf16[512,1024]{1,0:T(8,128)(2,1)} custom-call(bf16[512,1024]{1,0:T(8,128)(2,1)} %get-tuple-element.167.refs_0_.refs_1_, bf16[512,1024]{1,0:T(8,128)(2,1)} %get-tuple-element.167.refs_0_.refs_1_, bf16[4,3,512,256]{3,2,1,0:T(8,128)(2,1)} %get-tuple-element.168.refs_2_, f32[4,4,512]{2,1,0:T(4,128)} %get-tuple-element.169.refs_3_, ...), custom_call_target="tpu_custom_call" | custom-call | flops 22548578304 | bytes 37580964 | tf_op jit(solution)/shard_map/pallas_call | solution.py:134
  544.5 16.6 %shard_map.211 = bf16[512,1024]{1,0:T(8,128)(2,1)} custom-call(bf16[512,1024]{1,0:T(8,128)(2,1)} %get-tuple-element.167.refs_0_.refs_1_, bf16[512,1024]{1,0:T(8,128)(2,1)} %shard_map.210.refs_1_, bf16[4,3,512,256]{3,2,1,0:T(8,128)(2,1)} %get-tuple-element.168.refs_2_, f32[4,4,512]{2,1,0:T(4,128)} %get-tuple-element.169.refs_3_, ...), custom_call_target="tpu_custom_call" | custom-call | flops 22548578304 | bytes 37580964 | tf_op jit(solution)/shard_map/pallas_call | solution.py:134
  573.8 17.5 %collective-permute-done.63 = bf16[272,1024]{1,0:T(8,128)(2,1)S(1)} collective-permute-done((bf16[272,1024]{1,0:T(8,128)(2,1)S(1)}, bf16[272,1024]{1,0:T(8,128)(2,1)S(1)}, u32[]{:S(2)}, u32[]{:S(2)}) %collective-permute-start.63) | collective-permute-done | bytes 557088 | tf_op jit(solution)/shard_map/ppermute | solution.py:1189
  (304 shorter events, 196.2 us)
Async XLA Ops:
  0.6 27.3 %collective-permute-start.6 = (bf16[1024,2048]{1,0:T(8,128)(2,1)}, bf16[1024,2048]{1,0:T(8,128)(2,1)}, u32[]{:S(2)}, u32[]{:S(2)}) collective-permute-start(bf16[1024,2048]{1,0:T(8,128)(2,1)} %bitcast.81), channel_id=1, source_target_pairs={{0,16},{16,0},{1,17},{17,1},{2,18},{18,2},{3,19},{19,3},{4,20},{20... | collective-permute-start | bytes 12582920 | tf_op jit(solution)/shard_map/ppermute | solution.py:950
  1.1 26.8 %collective-permute-start.7 = (bf16[2048,1024]{1,0:T(8,128)(2,1)}, bf16[2048,1024]{1,0:T(8,128)(2,1)}, u32[]{:S(2)}, u32[]{:S(2)}) collective-permute-start(bf16[2048,1024]{1,0:T(8,128)(2,1)} %bitcast.90), channel_id=1, source_target_pairs={{0,16},{16,0},{1,17},{17,1},{2,18},{18,2},{3,19},{19,3},{4,20},{20... | collective-permute-start | bytes 12582920 | tf_op jit(solution)/shard_map/ppermute | solution.py:950
  1.2 26.7 %collective-permute-start.4 = (bf16[3,1024,512]{2,1,0:T(8,128)(2,1)}, bf16[3,1024,512]{2,1,0:T(8,128)(2,1)}, u32[]{:S(2)}, u32[]{:S(2)}) collective-permute-start(bf16[3,1024,512]{2,1,0:T(8,128)(2,1)} %bitcast.99), channel_id=1, source_target_pairs={{0,16},{16,0},{1,17},{17,1},{2,18},{18,2},{3,19},{19,3},{4,20},{20... | collective-permute-start | bytes 9437192 | tf_op jit(solution)/shard_map/ppermute | solution.py:950
  24.8 26.3 %collective-permute-start.1 = (bf16[512,1024]{1,0:T(8,128)(2,1)S(1)}, bf16[512,1024]{1,0:T(8,128)(2,1)S(1)}, u32[]{:S(2)}, u32[]{:S(2)}) collective-permute-start(bf16[512,1024]{1,0:T(8,128)(2,1)S(1)} %get-tuple-element.91), channel_id=1, source_target_pairs={{0,8},{1,9},{2,10},{3,11},{4,12},{5,13},{6,14},{7,15},{8,0},{9,1},... | collective-permute-start | bytes 3145736 | tf_op jit(solution)/shard_map/ppermute | solution.py:922
  118.8 29.2 %collective-permute-start.21 = (bf16[2304,256]{1,0:T(8,128)(2,1)}, bf16[2304,256]{1,0:T(8,128)(2,1)}, u32[]{:S(2)}, u32[]{:S(2)}) collective-permute-start(bf16[2304,256]{1,0:T(8,128)(2,1)} %shard_map.194), channel_id=1, source_target_pairs={{0,8},{1,9},{2,10},{3,11},{4,12},{5,13},{6,14},{7,15},{8,0},{9,1},... | collective-permute-start | bytes 3538952 | tf_op jit(solution)/shard_map/ppermute | solution.py:922
  139.2 32.8 %collective-permute-start.27 = (bf16[2304,256]{1,0:T(8,128)(2,1)S(1)}, bf16[2304,256]{1,0:T(8,128)(2,1)}, u32[]{:S(2)}, u32[]{:S(2)}) collective-permute-start(bf16[2304,256]{1,0:T(8,128)(2,1)S(1)} %copy-done.22), channel_id=1, source_target_pairs={{0,8},{1,9},{2,10},{3,11},{4,12},{5,13},{6,14},{7,15},{8,0},{9,1},... | collective-permute-start | bytes 3538952 | tf_op jit(solution)/shard_map/ppermute | solution.py:922
  175.7 28.1 %collective-permute-start.32 = (bf16[2,1024,128]{2,1,0:T(8,128)(2,1)}, bf16[2,1024,128]{2,1,0:T(8,128)(2,1)S(1)}, u32[]{:S(2)}, u32[]{:S(2)}) collective-permute-start(bf16[2,1024,128]{2,1,0:T(8,128)(2,1)} %collective-permute-done.20.refs_5_.refs_10_.refs_14_.refs_7_), channel_id=1, source_target_pairs={{0,2},{1,3},{2,0},{3,1},{4,6},{5,7},{6,4},{7,5},{8,10},{9,11},{10,... | collective-permute-start | bytes 1572872 | tf_op jit(solution)/shard_map/ppermute | solution.py:922
  176.5 27.8 %collective-permute-start.30 = (bf16[2,1024,128]{2,1,0:T(8,128)(2,1)}, bf16[2,1024,128]{2,1,0:T(8,128)(2,1)S(1)}, u32[]{:S(2)}, u32[]{:S(2)}) collective-permute-start(bf16[2,1024,128]{2,1,0:T(8,128)(2,1)} %collective-permute-done.20.refs_5_.refs_10_.refs_14_.refs_7_), channel_id=1, source_target_pairs={{0,1},{1,0},{2,3},{3,2},{4,5},{5,4},{6,7},{7,6},{8,9},{9,8},{10,11... | collective-permute-start | bytes 1572872 | tf_op jit(solution)/shard_map/ppermute | solution.py:922
  177.1 26.7 %collective-permute-start.34 = (bf16[2,1024,128]{2,1,0:T(8,128)(2,1)S(1)}, bf16[2,1024,128]{2,1,0:T(8,128)(2,1)S(1)}, u32[]{:S(2)}, u32[]{:S(2)}) collective-permute-start(bf16[2,1024,128]{2,1,0:T(8,128)(2,1)S(1)} %shard_map.198), channel_id=1, source_target_pairs={{0,8},{1,9},{2,10},{3,11},{4,12},{5,13},{6,14},{7,15},{8,0},{9,1},... | collective-permute-start | bytes 1572872 | tf_op jit(solution)/shard_map/ppermute | solution.py:922
  216.8 38.8 %collective-permute-start.36 = (bf16[4,2,512,256]{3,2,1,0:T(8,128)(2,1)}, bf16[4,2,512,256]{3,2,1,0:T(8,128)(2,1)}, u32[]{:S(2)}, u32[]{:S(2)}) collective-permute-start(bf16[4,2,512,256]{3,2,1,0:T(8,128)(2,1)} %shard_map.199.refs_2_.refs_6_), channel_id=1, source_target_pairs={{0,16},{16,0},{1,17},{17,1},{2,18},{18,2},{3,19},{19,3},{4,20},{20... | collective-permute-start | bytes 6291464 | tf_op jit(solution)/shard_map/ppermute | solution.py:950
  223.6 29.3 %collective-permute-start.37 = (bf16[2304,256]{1,0:T(8,128)(2,1)}, bf16[2304,256]{1,0:T(8,128)(2,1)}, u32[]{:S(2)}, u32[]{:S(2)}) collective-permute-start(bf16[2304,256]{1,0:T(8,128)(2,1)} %shard_map.201), channel_id=1, source_target_pairs={{0,8},{1,9},{2,10},{3,11},{4,12},{5,13},{6,14},{7,15},{8,0},{9,1},... | collective-permute-start | bytes 3538952 | tf_op jit(solution)/shard_map/ppermute | solution.py:922
  232.7 47.7 %collective-permute-start.43 = (bf16[2304,256]{1,0:T(8,128)(2,1)S(1)}, bf16[2304,256]{1,0:T(8,128)(2,1)}, u32[]{:S(2)}, u32[]{:S(2)}) collective-permute-start(bf16[2304,256]{1,0:T(8,128)(2,1)S(1)} %shard_map.202), channel_id=1, source_target_pairs={{0,8},{1,9},{2,10},{3,11},{4,12},{5,13},{6,14},{7,15},{8,0},{9,1},... | collective-permute-start | bytes 3538952 | tf_op jit(solution)/shard_map/ppermute | solution.py:922
  252.9 30.3 %collective-permute-start.41 = (bf16[2304,256]{1,0:T(8,128)(2,1)}, bf16[2304,256]{1,0:T(8,128)(2,1)}, u32[]{:S(2)}, u32[]{:S(2)}) collective-permute-start(bf16[2304,256]{1,0:T(8,128)(2,1)} %collective-permute-done.37.refs_13_.refs_18_), channel_id=1, source_target_pairs={{0,2},{1,3},{2,0},{3,1},{4,6},{5,7},{6,4},{7,5},{8,10},{9,11},{10,... | collective-permute-start | bytes 3538952 | tf_op jit(solution)/shard_map/ppermute | solution.py:922
  254.2 29.0 %collective-permute-start.39 = (bf16[2304,256]{1,0:T(8,128)(2,1)}, bf16[2304,256]{1,0:T(8,128)(2,1)}, u32[]{:S(2)}, u32[]{:S(2)}) collective-permute-start(bf16[2304,256]{1,0:T(8,128)(2,1)} %collective-permute-done.37.refs_13_.refs_18_), channel_id=1, source_target_pairs={{0,1},{1,0},{2,3},{3,2},{4,5},{5,4},{6,7},{7,6},{8,9},{9,8},{10,11... | collective-permute-start | bytes 3538952 | tf_op jit(solution)/shard_map/ppermute | solution.py:922
  280.4 28.7 %collective-permute-start.44 = (bf16[2304,256]{1,0:T(8,128)(2,1)}, bf16[2304,256]{1,0:T(8,128)(2,1)}, u32[]{:S(2)}, u32[]{:S(2)}) collective-permute-start(bf16[2304,256]{1,0:T(8,128)(2,1)} %collective-permute-done.43.refs_19_.refs_24_), channel_id=1, source_target_pairs={{0,16},{16,0},{1,17},{17,1},{2,18},{18,2},{3,19},{19,3},{4,20},{20... | collective-permute-start | bytes 3538952 | tf_op jit(solution)/shard_map/ppermute | solution.py:950
  306.9 26.4 %collective-permute-start.48 = (bf16[512,1024]{1,0:T(8,128)(2,1)S(1)}, bf16[512,1024]{1,0:T(8,128)(2,1)S(1)}, u32[]{:S(2)}, u32[]{:S(2)}) collective-permute-start(bf16[512,1024]{1,0:T(8,128)(2,1)S(1)} %constant_dynamic-slice_fusion.4), channel_id=1, source_target_pairs={{0,16},{16,0},{1,17},{17,1},{2,18},{18,2},{3,19},{19,3},{4,20},{20... | collective-permute-start | bytes 3145736 | tf_op jit(solution)/shard_map/ppermute | solution.py:950
  409.8 51.8 %collective-permute-start.45 = (bf16[512,1024]{1,0:T(8,128)(2,1)}, bf16[512,1024]{1,0:T(8,128)(2,1)}, u32[]{:S(2)}, u32[]{:S(2)}) collective-permute-start(bf16[512,1024]{1,0:T(8,128)(2,1)} %broadcast_select_fusion.4), channel_id=1, source_target_pairs={{0,16},{16,0},{1,17},{17,1},{2,18},{18,2},{3,19},{19,3},{4,20},{20... | collective-permute-start | bytes 3145736 | tf_op jit(solution)/shard_map/ppermute | solution.py:950
  477.1 26.2 %collective-permute-start.53 = (bf16[272,1024]{1,0:T(8,128)(2,1)S(1)}, bf16[272,1024]{1,0:T(8,128)(2,1)S(1)}, u32[]{:S(2)}, u32[]{:S(2)}) collective-permute-start(bf16[272,1024]{1,0:T(8,128)(2,1)S(1)} %slice_bitcast_fusion.1), channel_id=1, source_target_pairs={{0,8},{8,0},{1,9},{9,1},{2,10},{10,2},{3,11},{11,3},{4,12},{12,4},... | collective-permute-start | bytes 1671176 | tf_op jit(solution)/shard_map/ppermute | solution.py:950
  494.3 32.9 %collective-permute-start.58 = (bf16[272,1024]{1,0:T(8,128)(2,1)S(1)}, bf16[272,1024]{1,0:T(8,128)(2,1)S(1)}, u32[]{:S(2)}, u32[]{:S(2)}) collective-permute-start(bf16[272,1024]{1,0:T(8,128)(2,1)S(1)} %add_convert_fusion.2), channel_id=1, source_target_pairs={{0,4},{1,5},{2,6},{3,7},{4,0},{5,1},{6,2},{7,3},{8,12},{9,13},{10,... | collective-permute-start | bytes 1671176 | tf_op jit(solution)/shard_map/ppermute | solution.py:1189
  520.4 48.2 %collective-permute-start.61 = (bf16[512,1024]{1,0:T(8,128)(2,1)}, bf16[512,1024]{1,0:T(8,128)(2,1)}, u32[]{:S(2)}, u32[]{:S(2)}) collective-permute-start(bf16[512,1024]{1,0:T(8,128)(2,1)} %shard_map.209), channel_id=1, source_target_pairs={{0,16},{1,17},{2,18},{3,19},{4,20},{5,21},{6,22},{7,23},{8,24},{9,... | collective-permute-start | bytes 3145736 | tf_op jit(solution)/shard_map/ppermute | solution.py:1122
  561.0 30.9 %collective-permute-start.59 = (bf16[512,1024]{1,0:T(8,128)(2,1)}, bf16[512,1024]{1,0:T(8,128)(2,1)S(1)}, u32[]{:S(2)}, u32[]{:S(2)}) collective-permute-start(bf16[512,1024]{1,0:T(8,128)(2,1)} %shard_map.211), channel_id=1, source_target_pairs={{16,0},{17,1},{18,2},{19,3},{20,4},{21,5},{22,6},{23,7},{24,8},{25... | collective-permute-start | bytes 3145736 | tf_op jit(solution)/shard_map/ppermute | solution.py:1122
  563.1 28.2 %collective-permute-start.63 = (bf16[272,1024]{1,0:T(8,128)(2,1)S(1)}, bf16[272,1024]{1,0:T(8,128)(2,1)S(1)}, u32[]{:S(2)}, u32[]{:S(2)}) collective-permute-start(bf16[272,1024]{1,0:T(8,128)(2,1)S(1)} %add_convert_fusion.4), channel_id=1, source_target_pairs={{0,4},{1,5},{2,6},{3,7},{4,0},{5,1},{6,2},{7,3},{8,12},{9,13},{10,... | collective-permute-start | bytes 1671176 | tf_op jit(solution)/shard_map/ppermute | solution.py:1189
  566.9 31.1 %collective-permute-start.46 = (bf16[512,1024]{1,0:T(8,128)(2,1)S(1)}, bf16[512,1024]{1,0:T(8,128)(2,1)S(1)}, u32[]{:S(2)}, u32[]{:S(2)}) collective-permute-start(bf16[512,1024]{1,0:T(8,128)(2,1)S(1)} %get-tuple-element.187), channel_id=1, source_target_pairs={{0,8},{8,0},{1,9},{9,1},{2,10},{10,2},{3,11},{11,3},{4,12},{12,4},... | collective-permute-start | bytes 3145736 | tf_op jit(solution)/shard_map/ppermute | solution.py:950
  572.0 36.4 %collective-permute-start.62 = (bf16[512,1024]{1,0:T(8,128)(2,1)}, bf16[512,1024]{1,0:T(8,128)(2,1)}, u32[]{:S(2)}, u32[]{:S(2)}) collective-permute-start(bf16[512,1024]{1,0:T(8,128)(2,1)} %get-tuple-element.183), channel_id=1, source_target_pairs={{16,24},{17,25},{18,26},{19,27},{20,28},{21,29},{22,30},{23,31},{2... | collective-permute-start | bytes 3145736 | tf_op jit(solution)/shard_map/ppermute | solution.py:1125
  (98 other events, 1168.1 us)

commit v3 on v2

--- a/solution.py
+++ b/solution.py
@@ -10,7 +10,7 @@
 HEADDIM = 64
 BUNCH = 4
 WIDE = BUNCH * HEADDIM
-CHUNK = 512
+CHUNK = 1024
 SCALE = HEADDIM**-0.5
 LANES = 128
 PART = 256
@@ -206,11 +206,12 @@
         cols = block(g * CHUNK, CHUNK)
         plan.steps.append([(up, at((ALL, cols)), 0, at(())), (down, at((cols, ALL)), 1, at(()))])
     adapter = []
+    each = CHUNK // (2 * WIDE)
     for j, both in enumerate(far):
-        copies = []
+        copies = [] if j % each == 0 else copies
         for k, (first, second, base) in enumerate(both):
             a, b = plan.add(first), plan.add(second)
-            cols = block(k * WIDE, WIDE)
+            cols = block((j % each * 2 + k) * WIDE, WIDE)
             copies.append((a, at((block(0, width), ALL)), 0, at((ALL, cols))))
             for n in range(width // WIDE):
                 rows = block(base + n * WIDE, WIDE)
@@ -227,7 +228,8 @@
                 adapter.append(
                     (b, at((rows, here)), 3, lambda spot=spot, here=here: (here, spot()))
                 )
-        plan.steps.append(copies)
+        if j % each == each - 1:
+            plan.steps.append(copies)
     plan.steps.append([(adown, at(()), 2, at(())), (aup, at(()), 3, at(()))])
     plan.steps.append(adapter)
     return plan
@@ -398,9 +400,15 @@
 
 
 def self_blocks(rows, causal):
+    if not causal:
+        return [(slice(0, rows), slice(0, rows))]
     count = rows // PART
     parts = [slice(i * PART, (i + 1) * PART) for i in range(count)]
-    return [(part, slice(0, part.stop if causal else rows)) for part in parts]
+    return [(part, slice(0, part.stop)) for part in parts]
+
+
+def cross_blocks(rows):
+    return [(slice(i, i + PART), slice(0, rows)) for i in range(0, rows, PART)]
 
 
 def note_active(bias, valid, active, rows):
@@ -560,7 +568,7 @@
         q_ref[0] = q
         mixed[...] = jnp.zeros_like(mixed)
         for h, kv_ref in enumerate((own_ref, away_ref)):
-            for i, pair in enumerate(self_blocks(rows, False)):
+            for i, pair in enumerate(cross_blocks(rows)):
 
                 @pl.when(active[h, i] > 0)
                 def _():
@@ -635,7 +643,7 @@
         for ref in (dq, dk, dv):
             ref[...] = jnp.zeros_like(ref)
         for h, kv_ref in enumerate((own_ref, away_ref)):
-            for i, pair in enumerate(self_blocks(rows, False)):
+            for i, pair in enumerate(cross_blocks(rows)):
 
                 @pl.when(active[h, i] > 0)
                 def _():
@@ -769,8 +777,8 @@
 
         @pl.when(step < na)
         def _():
-            for at in range(0, rows, 256):
-                part = slice(at, at + 256)
+            for at in range(0, rows, 512):
+                part = slice(at, at + 512)
                 act, slope = gelu_pair(dot_nn(low[part, :], bufs[0][slot]))
                 slope_ref[0, part, :] = slope.astype(BF16)
                 acc[part, :] += dot_nn(act.astype(BF16), bufs[1][slot])
@@ -849,8 +857,8 @@
 
         @pl.when(step < na)
         def _():
-            for at in range(0, rows, 256):
-                part = slice(at, at + 256)
+            for at in range(0, rows, 512):
+                part = slice(at, at + 512)
                 hidden = dot_nt(low[part, :], bufs[1][slot]) * slope_ref[0, part, :].astype(F32)
                 acc[part, :] += dot_nt(hidden.astype(BF16), bufs[0][slot])
 
@@ -980,7 +988,7 @@
     units = adapter_down.shape[2]
 
     stride = max(lax.axis_size("dp") // 4, 1)
-    lane_y, lane_x, lane_z = Lane(1), Lane(2), Lane(2)
+    lane_y, lane_x, lane_z, lane_core = Lane(1), Lane(2), Lane(2), Lane(3)
 
     def over_y(value):
         return lane_y.send(value, MESH_AXES, route("mp", 1))
@@ -992,7 +1000,7 @@
         return lane_z.send(value, MESH_AXES, route("dp", stride))
 
     def near_pairs(*arrays):
-        return [(a, swap(a, "section")) for a in arrays]
+        return [(a, lane_core.send(a, MESH_AXES, route("section", 1))) for a in arrays]
 
     def share(j, size):
         return block(pl.multiple_of(share_of(j, stride) * size, size), size)
@@ -1161,7 +1169,7 @@
     cross_swaps = swapped_after(crosses, e_inv2)
     w_cross = cross_plan(near_cross, quarters(crosses, cross_swaps, 1))
     dec_3 = over_y(after(ffn_piece(1, 3), e_inv2))
-    kv = keys_forward(y_enc, w_cross)
+    kv = keys_forward(after(y_enc, dec_0), w_cross)
     kv_away = swap(kv, "section")
     dec_1, dec_2 = over_x(after(dec_0, kv)), over_z(after(dec_0, kv))
     d_q, c_lse, d_hat2, d_inv2 = cross_forward(
@@ -1191,6 +1199,7 @@
         return value
 
     flips = [1 << i for i in range(lax.axis_size("dp").bit_length() - 1)]
+    flips = flips[2:3] + flips[:2] + flips[3:]
     d_mid, d_grads = branch_backward(
         1, g_dec, d_hat3, d_inv3, dec_gain2, d_hat2, d_inv2, mid_gain,
         d_slope, d_aslope, d_aact, w_dec,

time: 625 us -> 608 us (0.973)
  waiting for transfers between devices: 182 us -> 161 us
  starting transfers between devices: 73.8 us -> 94.5 us
  Pallas kernels: 276 us -> 262 us
    ppermute x36 -> x28, starting transfers between devices: 24.4 us -> 45.9 us  [swap(): lax.ppermute(a, axis, [(0, 1), (1, 0)])]
    pallas_call x14, Pallas kernels: 270 us -> 256 us  [call(): pl.pallas_call(kernel, grid=(len(plan.steps),), in_specs=list(in_blocks)...]
    ppermute x19 -> x27, waiting for transfers between devices: 112 us -> 99.2 us  [send(): got = lax.ppermute(value, axes, route)]
    ppermute x36 -> x28, waiting for transfers between devices: 31.8 us -> 21.7 us  [swap(): lax.ppermute(a, axis, [(0, 1), (1, 0)])]
    ppermute x19 -> x27, starting transfers between devices: 24.7 us -> 27.4 us  [send(): got = lax.ppermute(value, axes, route)]
    unnamed x115 -> x107, local copies, waits for them, and re-layouts: 20.7 us -> 21.6 us
  transfers between devices with their start and end apart: 65 -> 65, of which waited for: 26 -> 23; matrix products, arithmetic and copies ran while one was open for 8% -> 8% of each run, Pallas kernels for 35% -> 33%
where the time goes in v3:
time: 608 us; the launch traced here: 606 us
  Pallas kernels  262 us (43%)
  waiting for transfers between devices  161 us (26%)
  starting transfers between devices  94.5 us (16%)
  local copies, waits for them, and re-layouts  48.7 us (8%)
  other arithmetic  32.2 us (5%)
  between operations  7.85 us (1%)
    pallas_call x14, Pallas kernels, call(): pl.pallas_call(kernel, grid=(len(plan.steps),), in_specs=list(in_blocks)...  256 us
    ppermute x27, waiting for transfers between devices, send(): got = lax.ppermute(value, axes, route)  99.2 us
    ppermute x28, starting transfers between devices, swap(): lax.ppermute(a, axis, [(0, 1), (1, 0)])  45.9 us
    ppermute x6, waiting for transfers between devices, summed_rows(): got = after(lax.ppermute(value, MESH_AXES, route('dp', flip)), token)  28.2 us
    ppermute x27, starting transfers between devices, send(): got = lax.ppermute(value, axes, route)  27.4 us
    ppermute x28, waiting for transfers between devices, swap(): lax.ppermute(a, axis, [(0, 1), (1, 0)])  21.7 us
    unnamed x107, local copies, waits for them, and re-layouts  21.6 us
    ppermute x6, starting transfers between devices, summed_rows(): got = after(lax.ppermute(value, MESH_AXES, route('dp', flip)), token)  12.8 us
  transfers between devices with their start and end apart: 65, of which 23 were waited for; matrix products, arithmetic and copies ran while one was open for 8% of the time, Pallas kernels for 33%

profile of v3, /device:TPU:0, one launch (start us, length us, event | category | flops | bytes accessed | tf_op | source)
XLA Modules:
  0.0 606.3 jit_solution(7811612483521958263)
XLA Ops:
  7.5 8.6 %collective-permute-done.5.refs_7_.refs_9_ = bf16[512,1024]{1,0:T(8,128)(2,1)S(1)} collective-permute-done((bf16[512,1024]{1,0:T(8,128)(2,1)}, bf16[512,1024]{1,0:T(8,128)(2,1)S(1)}, u32[]{:S(2)}, u32[]{:S(2)}) %collective-permute-start.5) | collective-permute-done | bytes 1048608 | tf_op jit(solution)/shard_map/ppermute | solution.py:930
  28.5 20.7 %collective-permute-done.1 = bf16[512,1024]{1,0:T(8,128)(2,1)S(1)} collective-permute-done((bf16[512,1024]{1,0:T(8,128)(2,1)S(1)}, bf16[512,1024]{1,0:T(8,128)(2,1)S(1)}, u32[]{:S(2)}, u32[]{:S(2)}) %collective-permute-start.1) | collective-permute-done | bytes 1048608 | tf_op jit(solution)/shard_map/ppermute | solution.py:930
  53.3 20.8 %collective-permute-done.12.refs_8_.refs_6_ = bf16[4,1024,128]{2,1,0:T(8,128)(2,1)} collective-permute-done((bf16[4,1024,128]{2,1,0:T(8,128)(2,1)S(1)}, bf16[4,1024,128]{2,1,0:T(8,128)(2,1)}, u32[]{:S(2)}, u32[]{:S(2)}) %collective-permute-start.12) | collective-permute-done | bytes 1048608 | tf_op jit(solution)/shard_map/ppermute | solution.py:930
  89.2 9.8 %collective-permute-done.14.refs_10_.refs_8_ = bf16[4,1024,128]{2,1,0:T(8,128)(2,1)} collective-permute-done((bf16[4,1024,128]{2,1,0:T(8,128)(2,1)}, bf16[4,1024,128]{2,1,0:T(8,128)(2,1)}, u32[]{:S(2)}, u32[]{:S(2)}) %collective-permute-start.14) | collective-permute-done | bytes 1048608 | tf_op jit(solution)/shard_map/ppermute | solution.py:930
  117.3 19.8 %shard_map.192 = (bf16[4,3,512,256]{3,2,1,0:T(8,128)(2,1)}, f32[4,4,512]{2,1,0:T(4,128)}, bf16[512,1024]{1,0:T(8,128)(2,1)}, f32[512,1]{1,0:T(8,128)}) custom-call(bf16[512,1024]{1,0:T(8,128)(2,1)} %get-tuple-element.192.refs_0_, s32[512,1]{1,0:T(8,128)} %copy.35.refs_1_.refs_4_, s32[1,512]{1,0:T(1,128)} %bitcast.152, ...), custom_call_target="tpu_custom_call" | custom-call | flops 25769803776 | bytes 42949672 | tf_op jit(solution)/shard_map/pallas_call | solution.py:134
  148.1 19.5 %shard_map.193 = (bf16[4,3,512,256]{3,2,1,0:T(8,128)(2,1)}, f32[4,4,512]{2,1,0:T(4,128)}, bf16[512,1024]{1,0:T(8,128)(2,1)}, f32[512,1]{1,0:T(8,128)}) custom-call(bf16[512,1024]{1,0:T(8,128)(2,1)} %get-tuple-element.110.refs_0_, s32[512,1]{1,0:T(8,128)} %copy.36.refs_1_.refs_4_, s32[1,512]{1,0:T(1,128)} %bitcast.159, ...), custom_call_target="tpu_custom_call" | custom-call | flops 25769803776 | bytes 42949672 | tf_op jit(solution)/shard_map/pallas_call | solution.py:134
  184.5 20.8 %shard_map.197 = (bf16[4,512,1024]{2,1,0:T(8,128)(2,1)}, bf16[2,512,256]{2,1,0:T(8,128)(2,1)}, bf16[2,512,256]{2,1,0:T(8,128)(2,1)}, bf16[512,1024]{1,0:T(8,128)...) custom-call(bf16[512,1024]{1,0:T(8,128)(2,1)} %get-tuple-element.112.refs_0_.refs_4_, ...), custom_call_target="tpu_custom_call" | custom-call | flops 28991029248 | bytes 48318384 | tf_op jit(solution)/shard_map/pallas_call | solution.py:134
  206.4 13.4 %collective-permute-done.29.refs_13_.refs_18_ = bf16[2304,256]{1,0:T(8,128)(2,1)} collective-permute-done((bf16[2304,256]{1,0:T(8,128)(2,1)S(1)}, bf16[2304,256]{1,0:T(8,128)(2,1)}, u32[]{:S(2)}, u32[]{:S(2)}) %collective-permute-start.29) | collective-permute-done | bytes 1179680 | tf_op jit(solution)/shard_map/ppermute | solution.py:930
  239.8 22.9 %shard_map.201 = (bf16[4,512,256]{2,1,0:T(8,128)(2,1)}, f32[4,2,4,512]{3,2,1,0:T(4,128)}, bf16[512,1024]{1,0:T(8,128)(2,1)}, f32[512,1]{1,0:T(8,128)}) custom-call(bf16[512,1024]{1,0:T(8,128)(2,1)} %get-tuple-element.124.refs_0_.refs_1_, f32[1,1024]{1,0:T(1,128)} %get-tuple-element.210.refs_3_.refs_1_, bf16[4,2,512,256]{3,2,1,0:T(8,128)(2,1)} %shard_map.200.refs_2_.refs_6_, ...), custom_call_target="tpu_custom_call" | custom-call | flops 32212254720 | bytes 53687092 | tf_op jit(solution)/shard_map/pallas_call | solution.py:134
  264.3 11.2 %collective-permute-start.44 = (bf16[2304,256]{1,0:T(8,128)(2,1)}, bf16[2304,256]{1,0:T(8,128)(2,1)}, u32[]{:S(2)}, u32[]{:S(2)}) collective-permute-start(bf16[2304,256]{1,0:T(8,128)(2,1)} %collective-permute-done.43.refs_19_.refs_24_), channel_id=1, source_target_pairs={{0,16},{16,0},{1,17},{17,1},{2,18},{18,2},{3,19},{19,3},{4,20},{20... | collective-permute-start | bytes 3538952 | tf_op jit(solution)/shard_map/ppermute | solution.py:958
  281.9 11.5 %collective-permute-start.48 = (bf16[512,1024]{1,0:T(8,128)(2,1)S(1)}, bf16[512,1024]{1,0:T(8,128)(2,1)S(1)}, u32[]{:S(2)}, u32[]{:S(2)}) collective-permute-start(bf16[512,1024]{1,0:T(8,128)(2,1)S(1)} %constant_dynamic-slice_fusion.4), channel_id=1, source_target_pairs={{0,16},{16,0},{1,17},{17,1},{2,18},{18,2},{3,19},{19,3},{4,20},{20... | collective-permute-start | bytes 3145736 | tf_op jit(solution)/shard_map/ppermute | solution.py:958
  293.4 21.0 %shard_map.203 = (bf16[4,512,1024]{2,1,0:T(8,128)(2,1)}, bf16[2,512,256]{2,1,0:T(8,128)(2,1)}, bf16[2,512,256]{2,1,0:T(8,128)(2,1)}, bf16[512,1024]{1,0:T(8,128)...) custom-call(bf16[512,1024]{1,0:T(8,128)(2,1)} %get-tuple-element.138.refs_0_.refs_4_, f32[1,1024]{1,0:T(1,128)} %bitcast.165, ...), custom_call_target="tpu_custom_call" | custom-call | flops 28991029248 | bytes 48318384 | tf_op jit(solution)/shard_map/pallas_call | solution.py:134
  317.6 23.4 %shard_map.204 = (bf16[512,1024]{1,0:T(8,128)(2,1)}, bf16[2,2,272,1024]{3,2,1,0:T(8,128)(2,1)}) custom-call(bf16[512,1024]{1,0:T(8,128)(2,1)} %get-tuple-element.190.refs_0_, bf16[512,1024]{1,0:T(8,128)(2,1)} %get-tuple-element.152.refs_1_, f32[512,1]{1,0:T(8,128)} %get-tuple-element.153.refs_2_, f32[1,1024]{1,0:T(1,128)} %get-tuple-element.209.refs_2_.refs_3_, ...), custom_call_target="tpu_custom_call" | custom-call | flops 28991029248 | bytes 48318384 | tf_op jit(solution)/shard_map/pallas_call | solution.py:134
  348.3 29.2 %shard_map.205 = (bf16[512,1024]{1,0:T(8,128)(2,1)}, bf16[4,2,512,256]{3,2,1,0:T(8,128)(2,1)}, bf16[4,2,512,256]{3,2,1,0:T(8,128)(2,1)}) custom-call(bf16[512,1024]{1,0:T(8,128)(2,1)} %get-tuple-element.159.refs_0_, bf16[512,1024]{1,0:T(8,128)(2,1)} %get-tuple-element.124.refs_0_.refs_1_, f32[512,1]{1,0:T(8,128)} %get-tuple-element.111.refs_2_, ...), custom_call_target="tpu_custom_call" | custom-call | flops 70866960384 | bytes 118111600 | tf_op jit(solution)/shard_map/pallas_call | solution.py:134
  377.5 17.8 %collective-permute-start.51 = (bf16[4,2,512,256]{3,2,1,0:T(8,128)(2,1)}, bf16[4,2,512,256]{3,2,1,0:T(8,128)(2,1)}, u32[]{:S(2)}, u32[]{:S(2)}) collective-permute-start(bf16[4,2,512,256]{3,2,1,0:T(8,128)(2,1)} %get-tuple-element.166), channel_id=1, source_target_pairs={{0,16},{16,0},{1,17},{17,1},{2,18},{18,2},{3,19},{19,3},{4,20},{20... | collective-permute-start | bytes 6291464 | tf_op jit(solution)/shard_map/ppermute | solution.py:958
  396.5 13.4 %collective-permute-done.50 = bf16[272,1024]{1,0:T(8,128)(2,1)S(1)} collective-permute-done((bf16[272,1024]{1,0:T(8,128)(2,1)S(1)}, bf16[272,1024]{1,0:T(8,128)(2,1)S(1)}, u32[]{:S(2)}, u32[]{:S(2)}) %collective-permute-start.50) | collective-permute-done | bytes 557088 | tf_op jit(solution)/shard_map/ppermute | solution.py:958
  418.7 23.5 %shard_map.207 = (bf16[512,1024]{1,0:T(8,128)(2,1)}, bf16[2,2,272,1024]{3,2,1,0:T(8,128)(2,1)}) custom-call(bf16[512,1024]{1,0:T(8,128)(2,1)} %shard_map.206.refs_0_, bf16[512,1024]{1,0:T(8,128)(2,1)} %get-tuple-element.167.refs_1_, f32[512,1]{1,0:T(8,128)} %get-tuple-element.128.refs_2_, f32[1,1024]{1,0:T(1,128)} %get-tuple-element.214.refs_2_.refs_3_, ...), custom_call_target="tpu_custom_call" | custom-call | flops 28991029248 | bytes 48318384 | tf_op jit(solution)/shard_map/pallas_call | solution.py:134
  450.0 13.1 %collective-permute-done.56 = bf16[272,1024]{1,0:T(8,128)(2,1)} collective-permute-done((bf16[272,1024]{1,0:T(8,128)(2,1)S(1)}, bf16[272,1024]{1,0:T(8,128)(2,1)}, u32[]{:S(2)}, u32[]{:S(2)}) %collective-permute-start.56) | collective-permute-done | bytes 557088 | tf_op jit(solution)/shard_map/ppermute | solution.py:1197
  464.4 9.7 %collective-permute-start.57 = (bf16[272,1024]{1,0:T(8,128)(2,1)S(1)}, bf16[272,1024]{1,0:T(8,128)(2,1)S(1)}, u32[]{:S(2)}, u32[]{:S(2)}) collective-permute-start(bf16[272,1024]{1,0:T(8,128)(2,1)S(1)} %add_convert_fusion.3), channel_id=1, source_target_pairs={{0,1},{1,0},{2,3},{3,2},{4,5},{5,4},{6,7},{7,6},{8,9},{9,8},{10,11... | collective-permute-start | bytes 1671176 | tf_op jit(solution)/shard_map/ppermute | solution.py:1197
  476.8 15.3 %shard_map.208.refs_1_ = bf16[512,1024]{1,0:T(8,128)(2,1)} custom-call(bf16[512,1024]{1,0:T(8,128)(2,1)} %get-tuple-element.173.refs_0_.refs_1_, bf16[512,1024]{1,0:T(8,128)(2,1)} %get-tuple-element.173.refs_0_.refs_1_, bf16[4,3,512,256]{3,2,1,0:T(8,128)(2,1)} %get-tuple-element.174.refs_2_, f32[4,4,512]{2,1,0:T(4,128)} %get-tuple-element.175.refs_3_, ...), custom_call_target="tpu_custom_call" | custom-call | flops 22548578304 | bytes 37580964 | tf_op jit(solution)/shard_map/pallas_call | solution.py:134
  495.2 15.1 %shard_map.209 = bf16[512,1024]{1,0:T(8,128)(2,1)} custom-call(bf16[512,1024]{1,0:T(8,128)(2,1)} %get-tuple-element.173.refs_0_.refs_1_, bf16[512,1024]{1,0:T(8,128)(2,1)} %shard_map.208.refs_1_, bf16[4,3,512,256]{3,2,1,0:T(8,128)(2,1)} %get-tuple-element.174.refs_2_, f32[4,4,512]{2,1,0:T(4,128)} %get-tuple-element.175.refs_3_, ...), custom_call_target="tpu_custom_call" | custom-call | flops 22548578304 | bytes 37580964 | tf_op jit(solution)/shard_map/pallas_call | solution.py:134
  520.2 15.1 %shard_map.210.refs_1_ = bf16[512,1024]{1,0:T(8,128)(2,1)} custom-call(bf16[512,1024]{1,0:T(8,128)(2,1)} %get-tuple-element.179.refs_0_.refs_1_, bf16[512,1024]{1,0:T(8,128)(2,1)} %get-tuple-element.179.refs_0_.refs_1_, bf16[4,3,512,256]{3,2,1,0:T(8,128)(2,1)} %get-tuple-element.180.refs_2_, f32[4,4,512]{2,1,0:T(4,128)} %get-tuple-element.181.refs_3_, ...), custom_call_target="tpu_custom_call" | custom-call | flops 22548578304 | bytes 37580964 | tf_op jit(solution)/shard_map/pallas_call | solution.py:134
  535.6 15.0 %shard_map.211 = bf16[512,1024]{1,0:T(8,128)(2,1)} custom-call(bf16[512,1024]{1,0:T(8,128)(2,1)} %get-tuple-element.179.refs_0_.refs_1_, bf16[512,1024]{1,0:T(8,128)(2,1)} %shard_map.210.refs_1_, bf16[4,3,512,256]{3,2,1,0:T(8,128)(2,1)} %get-tuple-element.180.refs_2_, f32[4,4,512]{2,1,0:T(4,128)} %get-tuple-element.181.refs_3_, ...), custom_call_target="tpu_custom_call" | custom-call | flops 22548578304 | bytes 37580964 | tf_op jit(solution)/shard_map/pallas_call | solution.py:134
  589.4 12.1 %collective-permute-done.60 = bf16[512,1024]{1,0:T(8,128)(2,1)} collective-permute-done((bf16[512,1024]{1,0:T(8,128)(2,1)}, bf16[512,1024]{1,0:T(8,128)(2,1)}, u32[]{:S(2)}, u32[]{:S(2)}) %collective-permute-start.60) | collective-permute-done | bytes 1048608 | tf_op jit(solution)/shard_map/ppermute | solution.py:1133
  (296 shorter events, 195.8 us)
Async XLA Ops:
  22.9 26.3 %collective-permute-start.1 = (bf16[512,1024]{1,0:T(8,128)(2,1)S(1)}, bf16[512,1024]{1,0:T(8,128)(2,1)S(1)}, u32[]{:S(2)}, u32[]{:S(2)}) collective-permute-start(bf16[512,1024]{1,0:T(8,128)(2,1)S(1)} %get-tuple-element.97), channel_id=1, source_target_pairs={{0,8},{1,9},{2,10},{3,11},{4,12},{5,13},{6,14},{7,15},{8,0},{9,1},... | collective-permute-start | bytes 3145736 | tf_op jit(solution)/shard_map/ppermute | solution.py:930
  49.3 24.8 %collective-permute-start.12 = (bf16[4,1024,128]{2,1,0:T(8,128)(2,1)S(1)}, bf16[4,1024,128]{2,1,0:T(8,128)(2,1)}, u32[]{:S(2)}, u32[]{:S(2)}) collective-permute-start(bf16[4,1024,128]{2,1,0:T(8,128)(2,1)S(1)} %shard_map.190), channel_id=1, source_target_pairs={{0,8},{1,9},{2,10},{3,11},{4,12},{5,13},{6,14},{7,15},{8,0},{9,1},... | collective-permute-start | bytes 3145736 | tf_op jit(solution)/shard_map/ppermute | solution.py:930
  74.1 26.1 %collective-permute-start.18 = (bf16[4,1024,128]{2,1,0:T(8,128)(2,1)}, bf16[4,1024,128]{2,1,0:T(8,128)(2,1)}, u32[]{:S(2)}, u32[]{:S(2)}) collective-permute-start(bf16[4,1024,128]{2,1,0:T(8,128)(2,1)} %shard_map.191), channel_id=1, source_target_pairs={{0,8},{1,9},{2,10},{3,11},{4,12},{5,13},{6,14},{7,15},{8,0},{9,1},... | collective-permute-start | bytes 3145736 | tf_op jit(solution)/shard_map/ppermute | solution.py:930
  116.7 29.2 %collective-permute-start.21 = (bf16[2304,256]{1,0:T(8,128)(2,1)}, bf16[2304,256]{1,0:T(8,128)(2,1)}, u32[]{:S(2)}, u32[]{:S(2)}) collective-permute-start(bf16[2304,256]{1,0:T(8,128)(2,1)} %shard_map.194), channel_id=1, source_target_pairs={{0,8},{1,9},{2,10},{3,11},{4,12},{5,13},{6,14},{7,15},{8,0},{9,1},... | collective-permute-start | bytes 3538952 | tf_op jit(solution)/shard_map/ppermute | solution.py:930
  137.1 32.8 %collective-permute-start.27 = (bf16[2304,256]{1,0:T(8,128)(2,1)}, bf16[2304,256]{1,0:T(8,128)(2,1)}, u32[]{:S(2)}, u32[]{:S(2)}) collective-permute-start(bf16[2304,256]{1,0:T(8,128)(2,1)} %copy-done.19), channel_id=1, source_target_pairs={{0,8},{1,9},{2,10},{3,11},{4,12},{5,13},{6,14},{7,15},{8,0},{9,1},... | collective-permute-start | bytes 3538952 | tf_op jit(solution)/shard_map/ppermute | solution.py:930
  145.9 25.8 %collective-permute-start.25 = (bf16[2304,256]{1,0:T(8,128)(2,1)}, bf16[2304,256]{1,0:T(8,128)(2,1)}, u32[]{:S(2)}, u32[]{:S(2)}) collective-permute-start(bf16[2304,256]{1,0:T(8,128)(2,1)} %collective-permute-done.21.refs_13_.refs_18_), channel_id=1, source_target_pairs={{0,2},{1,3},{2,0},{3,1},{4,6},{5,7},{6,4},{7,5},{8,10},{9,11},{10,... | collective-permute-start | bytes 3538952 | tf_op jit(solution)/shard_map/ppermute | solution.py:930
  147.5 25.5 %collective-permute-start.23 = (bf16[2304,256]{1,0:T(8,128)(2,1)}, bf16[2304,256]{1,0:T(8,128)(2,1)}, u32[]{:S(2)}, u32[]{:S(2)}) collective-permute-start(bf16[2304,256]{1,0:T(8,128)(2,1)} %collective-permute-done.21.refs_13_.refs_18_), channel_id=1, source_target_pairs={{0,1},{1,0},{2,3},{3,2},{4,5},{5,4},{6,7},{7,6},{8,9},{9,8},{10,11... | collective-permute-start | bytes 3538952 | tf_op jit(solution)/shard_map/ppermute | solution.py:930
  180.5 24.9 %collective-permute-start.33 = (bf16[2,1024,128]{2,1,0:T(8,128)(2,1)}, bf16[2,1024,128]{2,1,0:T(8,128)(2,1)S(1)}, u32[]{:S(2)}, u32[]{:S(2)}) collective-permute-start(bf16[2,1024,128]{2,1,0:T(8,128)(2,1)} %collective-permute-done.20.refs_5_.refs_10_.refs_14_.refs_7_), channel_id=1, source_target_pairs={{0,2},{1,3},{2,0},{3,1},{4,6},{5,7},{6,4},{7,5},{8,10},{9,11},{10,... | collective-permute-start | bytes 1572872 | tf_op jit(solution)/shard_map/ppermute | solution.py:930
  182.5 37.3 %collective-permute-start.29 = (bf16[2304,256]{1,0:T(8,128)(2,1)S(1)}, bf16[2304,256]{1,0:T(8,128)(2,1)}, u32[]{:S(2)}, u32[]{:S(2)}) collective-permute-start(bf16[2304,256]{1,0:T(8,128)(2,1)S(1)} %shard_map.198), channel_id=1, source_target_pairs={{0,8},{1,9},{2,10},{3,11},{4,12},{5,13},{6,14},{7,15},{8,0},{9,1},... | collective-permute-start | bytes 3538952 | tf_op jit(solution)/shard_map/ppermute | solution.py:930
  236.0 28.3 %collective-permute-start.43 = (bf16[2304,256]{1,0:T(8,128)(2,1)S(1)}, bf16[2304,256]{1,0:T(8,128)(2,1)}, u32[]{:S(2)}, u32[]{:S(2)}) collective-permute-start(bf16[2304,256]{1,0:T(8,128)(2,1)S(1)} %shard_map.202), channel_id=1, source_target_pairs={{0,8},{1,9},{2,10},{3,11},{4,12},{5,13},{6,14},{7,15},{8,0},{9,1},... | collective-permute-start | bytes 3538952 | tf_op jit(solution)/shard_map/ppermute | solution.py:930
  237.2 38.3 %collective-permute-start.41 = (bf16[2304,256]{1,0:T(8,128)(2,1)}, bf16[2304,256]{1,0:T(8,128)(2,1)}, u32[]{:S(2)}, u32[]{:S(2)}) collective-permute-start(bf16[2304,256]{1,0:T(8,128)(2,1)} %collective-permute-done.29.refs_13_.refs_18_), channel_id=1, source_target_pairs={{0,2},{1,3},{2,0},{3,1},{4,6},{5,7},{6,4},{7,5},{8,10},{9,11},{10,... | collective-permute-start | bytes 3538952 | tf_op jit(solution)/shard_map/ppermute | solution.py:930
  238.2 37.4 %collective-permute-start.39 = (bf16[2304,256]{1,0:T(8,128)(2,1)}, bf16[2304,256]{1,0:T(8,128)(2,1)}, u32[]{:S(2)}, u32[]{:S(2)}) collective-permute-start(bf16[2304,256]{1,0:T(8,128)(2,1)} %collective-permute-done.29.refs_13_.refs_18_), channel_id=1, source_target_pairs={{0,1},{1,0},{2,3},{3,2},{4,5},{5,4},{6,7},{7,6},{8,9},{9,8},{10,11... | collective-permute-start | bytes 3538952 | tf_op jit(solution)/shard_map/ppermute | solution.py:930
  264.3 29.0 %collective-permute-start.44 = (bf16[2304,256]{1,0:T(8,128)(2,1)}, bf16[2304,256]{1,0:T(8,128)(2,1)}, u32[]{:S(2)}, u32[]{:S(2)}) collective-permute-start(bf16[2304,256]{1,0:T(8,128)(2,1)} %collective-permute-done.43.refs_19_.refs_24_), channel_id=1, source_target_pairs={{0,16},{16,0},{1,17},{17,1},{2,18},{18,2},{3,19},{19,3},{4,20},{20... | collective-permute-start | bytes 3538952 | tf_op jit(solution)/shard_map/ppermute | solution.py:958
  281.9 32.5 %collective-permute-start.48 = (bf16[512,1024]{1,0:T(8,128)(2,1)S(1)}, bf16[512,1024]{1,0:T(8,128)(2,1)S(1)}, u32[]{:S(2)}, u32[]{:S(2)}) collective-permute-start(bf16[512,1024]{1,0:T(8,128)(2,1)S(1)} %constant_dynamic-slice_fusion.4), channel_id=1, source_target_pairs={{0,16},{16,0},{1,17},{17,1},{2,18},{18,2},{3,19},{19,3},{4,20},{20... | collective-permute-start | bytes 3145736 | tf_op jit(solution)/shard_map/ppermute | solution.py:958
  377.5 32.7 %collective-permute-start.51 = (bf16[4,2,512,256]{3,2,1,0:T(8,128)(2,1)}, bf16[4,2,512,256]{3,2,1,0:T(8,128)(2,1)}, u32[]{:S(2)}, u32[]{:S(2)}) collective-permute-start(bf16[4,2,512,256]{3,2,1,0:T(8,128)(2,1)} %get-tuple-element.166), channel_id=1, source_target_pairs={{0,16},{16,0},{1,17},{17,1},{2,18},{18,2},{3,19},{19,3},{4,20},{20... | collective-permute-start | bytes 6291464 | tf_op jit(solution)/shard_map/ppermute | solution.py:958
  396.5 50.7 %collective-permute-start.45 = (bf16[512,1024]{1,0:T(8,128)(2,1)}, bf16[512,1024]{1,0:T(8,128)(2,1)}, u32[]{:S(2)}, u32[]{:S(2)}) collective-permute-start(bf16[512,1024]{1,0:T(8,128)(2,1)} %broadcast_select_fusion.4), channel_id=1, source_target_pairs={{0,16},{16,0},{1,17},{17,1},{2,18},{18,2},{3,19},{19,3},{4,20},{20... | collective-permute-start | bytes 3145736 | tf_op jit(solution)/shard_map/ppermute | solution.py:958
  444.5 29.6 %collective-permute-start.52 = (bf16[2,272,1024]{2,1,0:T(8,128)(2,1)}, bf16[2,272,1024]{2,1,0:T(8,128)(2,1)}, u32[]{:S(2)}, u32[]{:S(2)}) collective-permute-start(bf16[2,272,1024]{2,1,0:T(8,128)(2,1)} %dynamic-slice_bitcast_fusion), channel_id=1, source_target_pairs={{0,16},{16,0},{1,17},{17,1},{2,18},{18,2},{3,19},{19,3},{4,20},{20... | collective-permute-start | bytes 3342344 | tf_op jit(solution)/shard_map/ppermute | solution.py:958
  464.4 27.7 %collective-permute-start.57 = (bf16[272,1024]{1,0:T(8,128)(2,1)S(1)}, bf16[272,1024]{1,0:T(8,128)(2,1)S(1)}, u32[]{:S(2)}, u32[]{:S(2)}) collective-permute-start(bf16[272,1024]{1,0:T(8,128)(2,1)S(1)} %add_convert_fusion.3), channel_id=1, source_target_pairs={{0,1},{1,0},{2,3},{3,2},{4,5},{5,4},{6,7},{7,6},{8,9},{9,8},{10,11... | collective-permute-start | bytes 1671176 | tf_op jit(solution)/shard_map/ppermute | solution.py:1197
  492.3 24.8 %collective-permute-start.58 = (bf16[272,1024]{1,0:T(8,128)(2,1)S(1)}, bf16[272,1024]{1,0:T(8,128)(2,1)S(1)}, u32[]{:S(2)}, u32[]{:S(2)}) collective-permute-start(bf16[272,1024]{1,0:T(8,128)(2,1)S(1)} %add_convert_fusion.2), channel_id=1, source_target_pairs={{0,2},{1,3},{2,0},{3,1},{4,6},{5,7},{6,4},{7,5},{8,10},{9,11},{10,... | collective-permute-start | bytes 1671176 | tf_op jit(solution)/shard_map/ppermute | solution.py:1197
  492.6 27.0 %collective-permute-start.54 = (bf16[272,1024]{1,0:T(8,128)(2,1)S(1)}, bf16[272,1024]{1,0:T(8,128)(2,1)S(1)}, u32[]{:S(2)}, u32[]{:S(2)}) collective-permute-start(bf16[272,1024]{1,0:T(8,128)(2,1)S(1)} %fusion.4), channel_id=1, source_target_pairs={{0,4},{1,5},{2,6},{3,7},{4,0},{5,1},{6,2},{7,3},{8,12},{9,13},{10,... | collective-permute-start | bytes 1671176 | tf_op jit(solution)/shard_map/ppermute | solution.py:1197
  510.3 43.8 %collective-permute-start.61 = (bf16[512,1024]{1,0:T(8,128)(2,1)}, bf16[512,1024]{1,0:T(8,128)(2,1)}, u32[]{:S(2)}, u32[]{:S(2)}) collective-permute-start(bf16[512,1024]{1,0:T(8,128)(2,1)} %shard_map.209), channel_id=1, source_target_pairs={{0,16},{1,17},{2,18},{3,19},{4,20},{5,21},{6,22},{7,23},{8,24},{9,... | collective-permute-start | bytes 3145736 | tf_op jit(solution)/shard_map/ppermute | solution.py:1130
  553.1 25.9 %collective-permute-start.46 = (bf16[512,1024]{1,0:T(8,128)(2,1)S(1)}, bf16[512,1024]{1,0:T(8,128)(2,1)S(1)}, u32[]{:S(2)}, u32[]{:S(2)}) collective-permute-start(bf16[512,1024]{1,0:T(8,128)(2,1)S(1)} %get-tuple-element.199), channel_id=1, source_target_pairs={{0,8},{8,0},{1,9},{9,1},{2,10},{10,2},{3,11},{11,3},{4,12},{12,4},... | collective-permute-start | bytes 3145736 | tf_op jit(solution)/shard_map/ppermute | solution.py:958
  557.5 31.9 %collective-permute-start.62 = (bf16[512,1024]{1,0:T(8,128)(2,1)}, bf16[512,1024]{1,0:T(8,128)(2,1)}, u32[]{:S(2)}, u32[]{:S(2)}) collective-permute-start(bf16[512,1024]{1,0:T(8,128)(2,1)} %get-tuple-element.195), channel_id=1, source_target_pairs={{16,24},{17,25},{18,26},{19,27},{20,28},{21,29},{22,30},{23,31},{2... | collective-permute-start | bytes 3145736 | tf_op jit(solution)/shard_map/ppermute | solution.py:1133
  570.9 30.6 %collective-permute-start.60 = (bf16[512,1024]{1,0:T(8,128)(2,1)}, bf16[512,1024]{1,0:T(8,128)(2,1)}, u32[]{:S(2)}, u32[]{:S(2)}) collective-permute-start(bf16[512,1024]{1,0:T(8,128)(2,1)} %get-tuple-element.197), channel_id=1, source_target_pairs={{0,8},{1,9},{2,10},{3,11},{4,12},{5,13},{6,14},{7,15},{8,0},{9,1},... | collective-permute-start | bytes 3145736 | tf_op jit(solution)/shard_map/ppermute | solution.py:1133
  (94 other events, 1101.0 us)

commit v4 on v3

--- a/solution.py
+++ b/solution.py
@@ -1136,9 +1136,9 @@
     near_ffn = near_pairs(ffn_in[0], ffn_out[0], adapter_down[0], adapter_up[0])
     near_cross = near_pairs(cross_kv[0], cross_vo[0])
     near_other = [pair[1] for pair in near_self + near_ffn + near_cross]
-    self_0 = over_y(after(self_piece(0), near_other))
+    self_0 = over_y(self_piece(0))
     self_3 = over_y(self_piece(3))
-    self_1, self_2 = over_x(self_0), over_z(self_0)
+    self_1, self_2 = over_x(after(self_0, near_other)), over_z(after(self_0, near_other))
     self_swaps = [swapped(p) for p in (self_0, self_1, self_2)]
     self_swaps.append(swapped(after(self_3, (self_1, self_2))))
     cross_0 = over_y(after(cross_piece(0), (self_1, self_2)))
@@ -1177,7 +1177,7 @@
     )
     dec = (dec_0, dec_1, dec_2, dec_3)
     w_dec = branch_plan(near_ffn, eighths(dec, swapped_after(dec, d_inv2), width), stride)
-    g_keep, g_got = rows_sent(cotangent, d_inv2)
+    g_keep, g_got = rows_sent(cotangent, kv)
     d_slope, d_aslope, d_aact, d_hat3, d_inv3, y_dec = branch_forward(
         1, d_hat2, mid_gain, dec_gain2, dec_downb, dec_upb, w_dec
     )
@@ -1209,15 +1209,14 @@
         after(d_mid, d_both), d_hat1, d_inv1, dec_gain1, d_q, c_lse, kv, kv_away, all_keys, dec_row,
         w_cross,
     )
-    d_total = summed_side(d_both, d_first)
     kv_grad_away = swap(kv_grad_give, "section")
-    e_out = keys_backward(after(g_enc, d_total), kv_grad, kv_grad_away, w_cross)
+    e_out = keys_backward(g_enc, kv_grad, kv_grad_away, w_cross)
     e_first, e_grads = branch_backward(
         0, e_out, e_hat2, e_inv2, enc_gain2, e_hat1, e_inv1, enc_gain1,
         e_slope, e_aslope, e_aact, w_enc,
     )
     e_both = summed_here(e_grads)
-    d_total = summed_rows(d_total, flips[:1], e_first)
+    d_total = summed_side(d_both, e_first)
     d_first = after(d_first, e_both)
     bunches = len(w_self.steps) // 2
 
@@ -1228,14 +1227,15 @@
 
     dx_dec = self_part(1, d_first, d_first, d_qkv, d_lse, dec_col, dec_row, 0)
     e_total = summed_side(e_both, dx_dec)
-    d_total = summed_rows(d_total, flips[1:2], dx_dec)
+    d_total = summed_rows(d_total, flips[:1], dx_dec)
     outputs = rows_back(y_enc, y_dec)
     dx_dec = self_part(1, d_first, after(dx_dec, (e_total, outputs)), d_qkv, d_lse, dec_col, dec_row, 1)
     e_total = summed_rows(e_total, flips[:1], dx_dec)
-    d_total = summed_rows(d_total, flips[2:], dx_dec)
+    d_total = summed_rows(d_total, flips[1:2], dx_dec)
     e_first = after(e_first, (dx_dec, e_total))
     dx_enc = self_part(0, e_first, e_first, e_qkv, e_lse, enc_col, enc_row, 0)
     e_total = summed_rows(e_total, flips[1:2], dx_enc)
+    d_total = summed_rows(d_total, flips[2:], dx_enc)
     dx_dec_back = layer_back(1, dx_dec)
     dx_enc = self_part(
         0, e_first, after(dx_enc, (e_total, d_total, dx_dec_back)), e_qkv, e_lse, enc_col, enc_row, 1

time: 608 us -> 591 us (0.972)
  waiting for transfers between devices: 161 us -> 150 us
  starting transfers between devices: 94.5 us -> 84.3 us
    ppermute x28, starting transfers between devices: 45.9 us -> 24.9 us  [swap(): lax.ppermute(a, axis, [(0, 1), (1, 0)])]
    ppermute x6, starting transfers between devices: 12.8 us -> 26.6 us  [summed_rows(): got = after(lax.ppermute(value, MESH_AXES, route('dp', flip)), token)]
    ppermute x6, waiting for transfers between devices: 28.2 us -> 15.1 us  [summed_rows(): got = after(lax.ppermute(value, MESH_AXES, route('dp', flip)), token)]
    unnamed x107 -> x117, local copies, waits for them, and re-layouts: 21.6 us -> 20.2 us
  transfers between devices with their start and end apart: 65 -> 65, of which waited for: 23 -> 24; matrix products, arithmetic and copies ran while one was open for 8% -> 10% of each run, Pallas kernels for 33% -> 31%
where the time goes in v4:
time: 591 us; the launch traced here: 593 us
  Pallas kernels  262 us (44%)
  waiting for transfers between devices  150 us (25%)
  starting transfers between devices  84.3 us (14%)
  local copies, waits for them, and re-layouts  51.1 us (9%)
  other arithmetic  37 us (6%)
  between operations  8.06 us (1%)
    pallas_call x14, Pallas kernels, call(): pl.pallas_call(kernel, grid=(len(plan.steps),), in_specs=list(in_blocks)...  256 us
    ppermute x27, waiting for transfers between devices, send(): got = lax.ppermute(value, axes, route)  101 us
    ppermute x6, starting transfers between devices, summed_rows(): got = after(lax.ppermute(value, MESH_AXES, route('dp', flip)), token)  26.6 us
    ppermute x27, starting transfers between devices, send(): got = lax.ppermute(value, axes, route)  25 us
    ppermute x28, starting transfers between devices, swap(): lax.ppermute(a, axis, [(0, 1), (1, 0)])  24.9 us
    ppermute x28, waiting for transfers between devices, swap(): lax.ppermute(a, axis, [(0, 1), (1, 0)])  22.3 us
    unnamed x117, local copies, waits for them, and re-layouts  20.2 us
    ppermute x6, waiting for transfers between devices, summed_rows(): got = after(lax.ppermute(value, MESH_AXES, route('dp', flip)), token)  15.1 us
  transfers between devices with their start and end apart: 65, of which 24 were waited for; matrix products, arithmetic and copies ran while one was open for 10% of the time, Pallas kernels for 31%

profile of v4, /device:TPU:0, one launch (start us, length us, event | category | flops | bytes accessed | tf_op | source)
XLA Modules:
  0.0 592.8 jit_solution(17134934682280174311)
XLA Ops:
  23.5 15.8 %collective-permute-done.1 = bf16[512,1024]{1,0:T(8,128)(2,1)S(1)} collective-permute-done((bf16[512,1024]{1,0:T(8,128)(2,1)S(1)}, bf16[512,1024]{1,0:T(8,128)(2,1)S(1)}, u32[]{:S(2)}, u32[]{:S(2)}) %collective-permute-start.1) | collective-permute-done | bytes 1048608 | tf_op jit(solution)/shard_map/ppermute | solution.py:930
  42.7 21.1 %collective-permute-done.6.refs_8_.refs_6_ = bf16[4,1024,128]{2,1,0:T(8,128)(2,1)} collective-permute-done((bf16[4,1024,128]{2,1,0:T(8,128)(2,1)S(1)}, bf16[4,1024,128]{2,1,0:T(8,128)(2,1)}, u32[]{:S(2)}, u32[]{:S(2)}) %collective-permute-start.6) | collective-permute-done | bytes 1048608 | tf_op jit(solution)/shard_map/ppermute | solution.py:930
  108.2 19.8 %shard_map.192 = (bf16[4,3,512,256]{3,2,1,0:T(8,128)(2,1)}, f32[4,4,512]{2,1,0:T(4,128)}, bf16[512,1024]{1,0:T(8,128)(2,1)}, f32[512,1]{1,0:T(8,128)}) custom-call(bf16[512,1024]{1,0:T(8,128)(2,1)} %get-tuple-element.190.refs_0_, s32[512,1]{1,0:T(8,128)} %copy.35.refs_1_.refs_4_, s32[1,512]{1,0:T(1,128)} %bitcast.152, ...), custom_call_target="tpu_custom_call" | custom-call | flops 25769803776 | bytes 42949672 | tf_op jit(solution)/shard_map/pallas_call | solution.py:134
  128.3 7.2 %collective-permute-done.21.refs_13_.refs_18_ = bf16[2304,256]{1,0:T(8,128)(2,1)} collective-permute-done((bf16[2304,256]{1,0:T(8,128)(2,1)}, bf16[2304,256]{1,0:T(8,128)(2,1)}, u32[]{:S(2)}, u32[]{:S(2)}) %collective-permute-start.21) | collective-permute-done | bytes 1179680 | tf_op jit(solution)/shard_map/ppermute | solution.py:930
  138.4 19.5 %shard_map.193 = (bf16[4,3,512,256]{3,2,1,0:T(8,128)(2,1)}, f32[4,4,512]{2,1,0:T(4,128)}, bf16[512,1024]{1,0:T(8,128)(2,1)}, f32[512,1]{1,0:T(8,128)}) custom-call(bf16[512,1024]{1,0:T(8,128)(2,1)} %get-tuple-element.109.refs_0_, s32[512,1]{1,0:T(8,128)} %copy.36.refs_1_.refs_4_, s32[1,512]{1,0:T(1,128)} %bitcast.159, ...), custom_call_target="tpu_custom_call" | custom-call | flops 25769803776 | bytes 42949672 | tf_op jit(solution)/shard_map/pallas_call | solution.py:134
  175.5 20.8 %shard_map.197 = (bf16[4,512,1024]{2,1,0:T(8,128)(2,1)}, bf16[2,512,256]{2,1,0:T(8,128)(2,1)}, bf16[2,512,256]{2,1,0:T(8,128)(2,1)}, bf16[512,1024]{1,0:T(8,128)...) custom-call(bf16[512,1024]{1,0:T(8,128)(2,1)} %get-tuple-element.111.refs_0_.refs_4_, ...), custom_call_target="tpu_custom_call" | custom-call | flops 28991029248 | bytes 48318384 | tf_op jit(solution)/shard_map/pallas_call | solution.py:134
  197.5 12.9 %collective-permute-done.29.refs_13_.refs_18_ = bf16[2304,256]{1,0:T(8,128)(2,1)} collective-permute-done((bf16[2304,256]{1,0:T(8,128)(2,1)S(1)}, bf16[2304,256]{1,0:T(8,128)(2,1)}, u32[]{:S(2)}, u32[]{:S(2)}) %collective-permute-start.29) | collective-permute-done | bytes 1179680 | tf_op jit(solution)/shard_map/ppermute | solution.py:930
  233.0 15.1 %collective-permute-done.47 = bf16[512,1024]{1,0:T(8,128)(2,1)} collective-permute-done((bf16[512,1024]{1,0:T(8,128)(2,1)}, bf16[512,1024]{1,0:T(8,128)(2,1)}, u32[]{:S(2)}, u32[]{:S(2)}) %collective-permute-start.47) | collective-permute-done | bytes 1048608 | tf_op jit(solution)/shard_map/ppermute | solution.py:930
  253.2 22.9 %shard_map.201 = (bf16[4,512,256]{2,1,0:T(8,128)(2,1)}, f32[4,2,4,512]{3,2,1,0:T(4,128)}, bf16[512,1024]{1,0:T(8,128)(2,1)}, f32[512,1]{1,0:T(8,128)}) custom-call(bf16[512,1024]{1,0:T(8,128)(2,1)} %get-tuple-element.123.refs_0_.refs_1_, f32[1,1024]{1,0:T(1,128)} %get-tuple-element.208.refs_3_.refs_1_, bf16[4,2,512,256]{3,2,1,0:T(8,128)(2,1)} %shard_map.200.refs_2_.refs_6_, ...), custom_call_target="tpu_custom_call" | custom-call | flops 32212254720 | bytes 53687092 | tf_op jit(solution)/shard_map/pallas_call | solution.py:134
  276.0 7.2 %collective-permute-start.44 = (bf16[2304,256]{1,0:T(8,128)(2,1)}, bf16[2304,256]{1,0:T(8,128)(2,1)S(1)}, u32[]{:S(2)}, u32[]{:S(2)}) collective-permute-start(bf16[2304,256]{1,0:T(8,128)(2,1)} %collective-permute-done.43.refs_19_.refs_24_), channel_id=1, source_target_pairs={{0,16},{16,0},{1,17},{17,1},{2,18},{18,2},{3,19},{19,3},{4,20},{20... | collective-permute-start | bytes 3538952 | tf_op jit(solution)/shard_map/ppermute | solution.py:958
  291.2 21.0 %shard_map.203 = (bf16[4,512,1024]{2,1,0:T(8,128)(2,1)}, bf16[2,512,256]{2,1,0:T(8,128)(2,1)}, bf16[2,512,256]{2,1,0:T(8,128)(2,1)}, bf16[512,1024]{1,0:T(8,128)...) custom-call(bf16[512,1024]{1,0:T(8,128)(2,1)} %get-tuple-element.137.refs_0_.refs_4_, f32[1,1024]{1,0:T(1,128)} %bitcast.165, ...), custom_call_target="tpu_custom_call" | custom-call | flops 28991029248 | bytes 48318384 | tf_op jit(solution)/shard_map/pallas_call | solution.py:134
  312.2 23.6 %shard_map.204 = (bf16[512,1024]{1,0:T(8,128)(2,1)}, bf16[2,2,272,1024]{3,2,1,0:T(8,128)(2,1)}) custom-call(bf16[512,1024]{1,0:T(8,128)(2,1)} %get-tuple-element.188.refs_0_, bf16[512,1024]{1,0:T(8,128)(2,1)} %get-tuple-element.151.refs_1_, f32[512,1]{1,0:T(8,128)} %get-tuple-element.152.refs_2_, f32[1,1024]{1,0:T(1,128)} %get-tuple-element.207.refs_2_.refs_3_, ...), custom_call_target="tpu_custom_call" | custom-call | flops 28991029248 | bytes 48318384 | tf_op jit(solution)/shard_map/pallas_call | solution.py:134
  341.9 29.2 %shard_map.205 = (bf16[512,1024]{1,0:T(8,128)(2,1)}, bf16[4,2,512,256]{3,2,1,0:T(8,128)(2,1)}, bf16[4,2,512,256]{3,2,1,0:T(8,128)(2,1)}) custom-call(bf16[512,1024]{1,0:T(8,128)(2,1)} %get-tuple-element.158.refs_0_, bf16[512,1024]{1,0:T(8,128)(2,1)} %get-tuple-element.123.refs_0_.refs_1_, f32[512,1]{1,0:T(8,128)} %get-tuple-element.110.refs_2_, ...), custom_call_target="tpu_custom_call" | custom-call | flops 70866960384 | bytes 118111600 | tf_op jit(solution)/shard_map/pallas_call | solution.py:134
  371.2 9.2 %collective-permute-start.50 = (bf16[4,2,512,256]{3,2,1,0:T(8,128)(2,1)}, bf16[4,2,512,256]{3,2,1,0:T(8,128)(2,1)}, u32[]{:S(2)}, u32[]{:S(2)}) collective-permute-start(bf16[4,2,512,256]{3,2,1,0:T(8,128)(2,1)} %get-tuple-element.162), channel_id=1, source_target_pairs={{0,16},{16,0},{1,17},{17,1},{2,18},{18,2},{3,19},{19,3},{4,20},{20... | collective-permute-start | bytes 6291464 | tf_op jit(solution)/shard_map/ppermute | solution.py:958
  384.5 8.1 %shard_map.206.refs_0_ = bf16[512,1024]{1,0:T(8,128)(2,1)} custom-call(bf16[512,1024]{1,0:T(8,128)(2,1)} %get-tuple-element.189.refs_0_, bf16[4,2,512,256]{3,2,1,0:T(8,128)(2,1)} %get-tuple-element.161.refs_1_, bf16[4,2,512,256]{3,2,1,0:T(8,128)(2,1)} %collective-permute-done.50.refs_2_, bf16[1024,512]{1,0:T(8,128)(2,1)} %bitcast.134, ...), custom_call_target="tpu_custom_call" | custom-call | flops 6442450944 | bytes 10737418 | tf_op jit(solution)/shard_map/pallas_call | solution.py:134
  392.6 23.9 %shard_map.207 = (bf16[512,1024]{1,0:T(8,128)(2,1)}, bf16[2,2,272,1024]{3,2,1,0:T(8,128)(2,1)}) custom-call(bf16[512,1024]{1,0:T(8,128)(2,1)} %shard_map.206.refs_0_, bf16[512,1024]{1,0:T(8,128)(2,1)} %get-tuple-element.163.refs_1_, f32[512,1]{1,0:T(8,128)} %get-tuple-element.127.refs_2_, f32[1,1024]{1,0:T(1,128)} %get-tuple-element.212.refs_2_.refs_3_, ...), custom_call_target="tpu_custom_call" | custom-call | flops 28991029248 | bytes 48318384 | tf_op jit(solution)/shard_map/pallas_call | solution.py:134
  427.4 7.7 %collective-permute-done.55 = bf16[272,1024]{1,0:T(8,128)(2,1)} collective-permute-done((bf16[272,1024]{1,0:T(8,128)(2,1)}, bf16[272,1024]{1,0:T(8,128)(2,1)}, u32[]{:S(2)}, u32[]{:S(2)}) %collective-permute-start.55) | collective-permute-done | bytes 557088 | tf_op jit(solution)/shard_map/ppermute | solution.py:958
  442.5 15.3 %shard_map.208.refs_1_ = bf16[512,1024]{1,0:T(8,128)(2,1)} custom-call(bf16[512,1024]{1,0:T(8,128)(2,1)} %get-tuple-element.170.refs_0_.refs_1_, bf16[512,1024]{1,0:T(8,128)(2,1)} %get-tuple-element.170.refs_0_.refs_1_, bf16[4,3,512,256]{3,2,1,0:T(8,128)(2,1)} %get-tuple-element.171.refs_2_, f32[4,4,512]{2,1,0:T(4,128)} %get-tuple-element.172.refs_3_, ...), custom_call_target="tpu_custom_call" | custom-call | flops 22548578304 | bytes 37580964 | tf_op jit(solution)/shard_map/pallas_call | solution.py:134
  458.1 21.6 %collective-permute-start.57 = (bf16[272,1024]{1,0:T(8,128)(2,1)S(1)}, bf16[272,1024]{1,0:T(8,128)(2,1)S(1)}, u32[]{:S(2)}, u32[]{:S(2)}) collective-permute-start(bf16[272,1024]{1,0:T(8,128)(2,1)S(1)} %add_convert_fusion.3), channel_id=1, source_target_pairs={{0,1},{1,0},{2,3},{3,2},{4,5},{5,4},{6,7},{7,6},{8,9},{9,8},{10,11... | collective-permute-start | bytes 1671176 | tf_op jit(solution)/shard_map/ppermute | solution.py:1197
  480.0 15.1 %shard_map.209 = bf16[512,1024]{1,0:T(8,128)(2,1)} custom-call(bf16[512,1024]{1,0:T(8,128)(2,1)} %get-tuple-element.170.refs_0_.refs_1_, bf16[512,1024]{1,0:T(8,128)(2,1)} %shard_map.208.refs_1_, bf16[4,3,512,256]{3,2,1,0:T(8,128)(2,1)} %get-tuple-element.171.refs_2_, f32[4,4,512]{2,1,0:T(4,128)} %get-tuple-element.172.refs_3_, ...), custom_call_target="tpu_custom_call" | custom-call | flops 22548578304 | bytes 37580964 | tf_op jit(solution)/shard_map/pallas_call | solution.py:134
  506.3 15.1 %shard_map.210.refs_1_ = bf16[512,1024]{1,0:T(8,128)(2,1)} custom-call(bf16[512,1024]{1,0:T(8,128)(2,1)} %get-tuple-element.176.refs_0_.refs_1_, bf16[512,1024]{1,0:T(8,128)(2,1)} %get-tuple-element.176.refs_0_.refs_1_, bf16[4,3,512,256]{3,2,1,0:T(8,128)(2,1)} %get-tuple-element.177.refs_2_, f32[4,4,512]{2,1,0:T(4,128)} %get-tuple-element.178.refs_3_, ...), custom_call_target="tpu_custom_call" | custom-call | flops 22548578304 | bytes 37580964 | tf_op jit(solution)/shard_map/pallas_call | solution.py:134
  521.9 15.0 %shard_map.211 = bf16[512,1024]{1,0:T(8,128)(2,1)} custom-call(bf16[512,1024]{1,0:T(8,128)(2,1)} %get-tuple-element.176.refs_0_.refs_1_, bf16[512,1024]{1,0:T(8,128)(2,1)} %shard_map.210.refs_1_, bf16[4,3,512,256]{3,2,1,0:T(8,128)(2,1)} %get-tuple-element.177.refs_2_, f32[4,4,512]{2,1,0:T(4,128)} %get-tuple-element.178.refs_3_, ...), custom_call_target="tpu_custom_call" | custom-call | flops 22548578304 | bytes 37580964 | tf_op jit(solution)/shard_map/pallas_call | solution.py:134
  545.5 8.8 %collective-permute-done.63 = bf16[272,1024]{1,0:T(8,128)(2,1)S(1)} collective-permute-done((bf16[272,1024]{1,0:T(8,128)(2,1)S(1)}, bf16[272,1024]{1,0:T(8,128)(2,1)S(1)}, u32[]{:S(2)}, u32[]{:S(2)}) %collective-permute-start.63) | collective-permute-done | bytes 557088 | tf_op jit(solution)/shard_map/ppermute | solution.py:1197
  576.1 12.0 %collective-permute-done.60 = bf16[512,1024]{1,0:T(8,128)(2,1)} collective-permute-done((bf16[512,1024]{1,0:T(8,128)(2,1)}, bf16[512,1024]{1,0:T(8,128)(2,1)}, u32[]{:S(2)}, u32[]{:S(2)}) %collective-permute-start.60) | collective-permute-done | bytes 1048608 | tf_op jit(solution)/shard_map/ppermute | solution.py:1133
  (306 shorter events, 196.7 us)
Async XLA Ops:
  6.6 33.0 %collective-permute-start.9 = (bf16[2048,1024]{1,0:T(8,128)(2,1)}, bf16[2048,1024]{1,0:T(8,128)(2,1)}, u32[]{:S(2)}, u32[]{:S(2)}) collective-permute-start(bf16[2048,1024]{1,0:T(8,128)(2,1)} %bitcast.90), channel_id=1, source_target_pairs={{0,16},{1,17},{2,18},{3,19},{4,20},{5,21},{6,22},{7,23},{8,24},{9,... | collective-permute-start | bytes 12582920 | tf_op jit(solution)/shard_map/ppermute | solution.py:930
  7.0 34.5 %collective-permute-start.8 = (bf16[1024,2048]{1,0:T(8,128)(2,1)}, bf16[1024,2048]{1,0:T(8,128)(2,1)}, u32[]{:S(2)}, u32[]{:S(2)}) collective-permute-start(bf16[1024,2048]{1,0:T(8,128)(2,1)} %bitcast.81), channel_id=1, source_target_pairs={{0,16},{1,17},{2,18},{3,19},{4,20},{5,21},{6,22},{7,23},{8,24},{9,... | collective-permute-start | bytes 12582920 | tf_op jit(solution)/shard_map/ppermute | solution.py:930
  14.2 25.1 %collective-permute-start.1 = (bf16[512,1024]{1,0:T(8,128)(2,1)S(1)}, bf16[512,1024]{1,0:T(8,128)(2,1)S(1)}, u32[]{:S(2)}, u32[]{:S(2)}) collective-permute-start(bf16[512,1024]{1,0:T(8,128)(2,1)S(1)} %get-tuple-element.96), channel_id=1, source_target_pairs={{0,8},{1,9},{2,10},{3,11},{4,12},{5,13},{6,14},{7,15},{8,0},{9,1},... | collective-permute-start | bytes 3145736 | tf_op jit(solution)/shard_map/ppermute | solution.py:930
  106.4 29.2 %collective-permute-start.21 = (bf16[2304,256]{1,0:T(8,128)(2,1)}, bf16[2304,256]{1,0:T(8,128)(2,1)}, u32[]{:S(2)}, u32[]{:S(2)}) collective-permute-start(bf16[2304,256]{1,0:T(8,128)(2,1)} %shard_map.194), channel_id=1, source_target_pairs={{0,8},{1,9},{2,10},{3,11},{4,12},{5,13},{6,14},{7,15},{8,0},{9,1},... | collective-permute-start | bytes 3538952 | tf_op jit(solution)/shard_map/ppermute | solution.py:930
  128.0 31.6 %collective-permute-start.27 = (bf16[2304,256]{1,0:T(8,128)(2,1)}, bf16[2304,256]{1,0:T(8,128)(2,1)}, u32[]{:S(2)}, u32[]{:S(2)}) collective-permute-start(bf16[2304,256]{1,0:T(8,128)(2,1)} %copy-done.24), channel_id=1, source_target_pairs={{0,8},{1,9},{2,10},{3,11},{4,12},{5,13},{6,14},{7,15},{8,0},{9,1},... | collective-permute-start | bytes 3538952 | tf_op jit(solution)/shard_map/ppermute | solution.py:930
  135.6 25.8 %collective-permute-start.25 = (bf16[2304,256]{1,0:T(8,128)(2,1)}, bf16[2304,256]{1,0:T(8,128)(2,1)}, u32[]{:S(2)}, u32[]{:S(2)}) collective-permute-start(bf16[2304,256]{1,0:T(8,128)(2,1)} %collective-permute-done.21.refs_13_.refs_18_), channel_id=1, source_target_pairs={{0,2},{1,3},{2,0},{3,1},{4,6},{5,7},{6,4},{7,5},{8,10},{9,11},{10,... | collective-permute-start | bytes 3538952 | tf_op jit(solution)/shard_map/ppermute | solution.py:930
  137.2 25.5 %collective-permute-start.23 = (bf16[2304,256]{1,0:T(8,128)(2,1)}, bf16[2304,256]{1,0:T(8,128)(2,1)}, u32[]{:S(2)}, u32[]{:S(2)}) collective-permute-start(bf16[2304,256]{1,0:T(8,128)(2,1)} %collective-permute-done.21.refs_13_.refs_18_), channel_id=1, source_target_pairs={{0,1},{1,0},{2,3},{3,2},{4,5},{5,4},{6,7},{7,6},{8,9},{9,8},{10,11... | collective-permute-start | bytes 3538952 | tf_op jit(solution)/shard_map/ppermute | solution.py:930
  170.2 26.3 %collective-permute-start.33 = (bf16[2,1024,128]{2,1,0:T(8,128)(2,1)}, bf16[2,1024,128]{2,1,0:T(8,128)(2,1)S(1)}, u32[]{:S(2)}, u32[]{:S(2)}) collective-permute-start(bf16[2,1024,128]{2,1,0:T(8,128)(2,1)} %collective-permute-done.20.refs_5_.refs_10_.refs_14_.refs_7_), channel_id=1, source_target_pairs={{0,2},{1,3},{2,0},{3,1},{4,6},{5,7},{6,4},{7,5},{8,10},{9,11},{10,... | collective-permute-start | bytes 1572872 | tf_op jit(solution)/shard_map/ppermute | solution.py:930
  171.0 26.0 %collective-permute-start.31 = (bf16[2,1024,128]{2,1,0:T(8,128)(2,1)}, bf16[2,1024,128]{2,1,0:T(8,128)(2,1)S(1)}, u32[]{:S(2)}, u32[]{:S(2)}) collective-permute-start(bf16[2,1024,128]{2,1,0:T(8,128)(2,1)} %collective-permute-done.20.refs_5_.refs_10_.refs_14_.refs_7_), channel_id=1, source_target_pairs={{0,1},{1,0},{2,3},{3,2},{4,5},{5,4},{6,7},{7,6},{8,9},{9,8},{10,11... | collective-permute-start | bytes 1572872 | tf_op jit(solution)/shard_map/ppermute | solution.py:930
  174.0 36.3 %collective-permute-start.29 = (bf16[2304,256]{1,0:T(8,128)(2,1)S(1)}, bf16[2304,256]{1,0:T(8,128)(2,1)}, u32[]{:S(2)}, u32[]{:S(2)}) collective-permute-start(bf16[2304,256]{1,0:T(8,128)(2,1)S(1)} %shard_map.198), channel_id=1, source_target_pairs={{0,8},{1,9},{2,10},{3,11},{4,12},{5,13},{6,14},{7,15},{8,0},{9,1},... | collective-permute-start | bytes 3538952 | tf_op jit(solution)/shard_map/ppermute | solution.py:930
  218.5 34.6 %collective-permute-start.37 = (bf16[4,2,512,256]{3,2,1,0:T(8,128)(2,1)}, bf16[4,2,512,256]{3,2,1,0:T(8,128)(2,1)}, u32[]{:S(2)}, u32[]{:S(2)}) collective-permute-start(bf16[4,2,512,256]{3,2,1,0:T(8,128)(2,1)} %shard_map.200.refs_2_.refs_6_), channel_id=1, source_target_pairs={{0,16},{16,0},{1,17},{17,1},{2,18},{18,2},{3,19},{19,3},{4,20},{20... | collective-permute-start | bytes 6291464 | tf_op jit(solution)/shard_map/ppermute | solution.py:958
  221.8 26.3 %collective-permute-start.47 = (bf16[512,1024]{1,0:T(8,128)(2,1)}, bf16[512,1024]{1,0:T(8,128)(2,1)}, u32[]{:S(2)}, u32[]{:S(2)}) collective-permute-start(bf16[512,1024]{1,0:T(8,128)(2,1)} %get-tuple-element.150), channel_id=1, source_target_pairs={{0,8},{1,9},{2,10},{3,11},{4,12},{5,13},{6,14},{7,15},{8,0},{9,1},... | collective-permute-start | bytes 3145736 | tf_op jit(solution)/shard_map/ppermute | solution.py:930
  230.3 45.7 %collective-permute-start.43 = (bf16[2304,256]{1,0:T(8,128)(2,1)S(1)}, bf16[2304,256]{1,0:T(8,128)(2,1)}, u32[]{:S(2)}, u32[]{:S(2)}) collective-permute-start(bf16[2304,256]{1,0:T(8,128)(2,1)S(1)} %shard_map.202), channel_id=1, source_target_pairs={{0,8},{1,9},{2,10},{3,11},{4,12},{5,13},{6,14},{7,15},{8,0},{9,1},... | collective-permute-start | bytes 3538952 | tf_op jit(solution)/shard_map/ppermute | solution.py:930
  230.7 52.6 %collective-permute-start.41 = (bf16[2304,256]{1,0:T(8,128)(2,1)}, bf16[2304,256]{1,0:T(8,128)(2,1)}, u32[]{:S(2)}, u32[]{:S(2)}) collective-permute-start(bf16[2304,256]{1,0:T(8,128)(2,1)} %collective-permute-done.29.refs_13_.refs_18_), channel_id=1, source_target_pairs={{0,2},{1,3},{2,0},{3,1},{4,6},{5,7},{6,4},{7,5},{8,10},{9,11},{10,... | collective-permute-start | bytes 3538952 | tf_op jit(solution)/shard_map/ppermute | solution.py:930
  232.3 51.1 %collective-permute-start.39 = (bf16[2304,256]{1,0:T(8,128)(2,1)}, bf16[2304,256]{1,0:T(8,128)(2,1)}, u32[]{:S(2)}, u32[]{:S(2)}) collective-permute-start(bf16[2304,256]{1,0:T(8,128)(2,1)} %collective-permute-done.29.refs_13_.refs_18_), channel_id=1, source_target_pairs={{0,1},{1,0},{2,3},{3,2},{4,5},{5,4},{6,7},{7,6},{8,9},{9,8},{10,11... | collective-permute-start | bytes 3538952 | tf_op jit(solution)/shard_map/ppermute | solution.py:930
  253.1 31.4 %collective-permute-start.48 = (bf16[512,1024]{1,0:T(8,128)(2,1)S(1)}, bf16[512,1024]{1,0:T(8,128)(2,1)S(1)}, u32[]{:S(2)}, u32[]{:S(2)}) collective-permute-start(bf16[512,1024]{1,0:T(8,128)(2,1)S(1)} %constant_dynamic-slice_fusion.4), channel_id=1, source_target_pairs={{0,16},{16,0},{1,17},{17,1},{2,18},{18,2},{3,19},{19,3},{4,20},{20... | collective-permute-start | bytes 3145736 | tf_op jit(solution)/shard_map/ppermute | solution.py:958
  381.5 43.0 %collective-permute-start.45 = (bf16[512,1024]{1,0:T(8,128)(2,1)}, bf16[512,1024]{1,0:T(8,128)(2,1)}, u32[]{:S(2)}, u32[]{:S(2)}) collective-permute-start(bf16[512,1024]{1,0:T(8,128)(2,1)} %broadcast_select_fusion.4), channel_id=1, source_target_pairs={{0,16},{16,0},{1,17},{17,1},{2,18},{18,2},{3,19},{19,3},{4,20},{20... | collective-permute-start | bytes 3145736 | tf_op jit(solution)/shard_map/ppermute | solution.py:958
  440.7 39.0 %collective-permute-start.52 = (bf16[272,1024]{1,0:T(8,128)(2,1)S(1)}, bf16[272,1024]{1,0:T(8,128)(2,1)S(1)}, u32[]{:S(2)}, u32[]{:S(2)}) collective-permute-start(bf16[272,1024]{1,0:T(8,128)(2,1)S(1)} %slice_bitcast_fusion.3), channel_id=1, source_target_pairs={{0,8},{8,0},{1,9},{9,1},{2,10},{10,2},{3,11},{11,3},{4,12},{12,4},... | collective-permute-start | bytes 1671176 | tf_op jit(solution)/shard_map/ppermute | solution.py:958
  458.1 39.3 %collective-permute-start.57 = (bf16[272,1024]{1,0:T(8,128)(2,1)S(1)}, bf16[272,1024]{1,0:T(8,128)(2,1)S(1)}, u32[]{:S(2)}, u32[]{:S(2)}) collective-permute-start(bf16[272,1024]{1,0:T(8,128)(2,1)S(1)} %add_convert_fusion.3), channel_id=1, source_target_pairs={{0,1},{1,0},{2,3},{3,2},{4,5},{5,4},{6,7},{7,6},{8,9},{9,8},{10,11... | collective-permute-start | bytes 1671176 | tf_op jit(solution)/shard_map/ppermute | solution.py:1197
  479.9 25.8 %collective-permute-start.53 = (bf16[272,1024]{1,0:T(8,128)(2,1)S(1)}, bf16[272,1024]{1,0:T(8,128)(2,1)S(1)}, u32[]{:S(2)}, u32[]{:S(2)}) collective-permute-start(bf16[272,1024]{1,0:T(8,128)(2,1)S(1)} %fusion.5), channel_id=1, source_target_pairs={{0,4},{1,5},{2,6},{3,7},{4,0},{5,1},{6,2},{7,3},{8,12},{9,13},{10,... | collective-permute-start | bytes 1671176 | tf_op jit(solution)/shard_map/ppermute | solution.py:1197
  495.0 45.3 %collective-permute-start.61 = (bf16[512,1024]{1,0:T(8,128)(2,1)}, bf16[512,1024]{1,0:T(8,128)(2,1)}, u32[]{:S(2)}, u32[]{:S(2)}) collective-permute-start(bf16[512,1024]{1,0:T(8,128)(2,1)} %shard_map.209), channel_id=1, source_target_pairs={{0,16},{1,17},{2,18},{3,19},{4,20},{5,21},{6,22},{7,23},{8,24},{9,... | collective-permute-start | bytes 3145736 | tf_op jit(solution)/shard_map/ppermute | solution.py:1130
  539.7 25.9 %collective-permute-start.46 = (bf16[512,1024]{1,0:T(8,128)(2,1)S(1)}, bf16[512,1024]{1,0:T(8,128)(2,1)S(1)}, u32[]{:S(2)}, u32[]{:S(2)}) collective-permute-start(bf16[512,1024]{1,0:T(8,128)(2,1)S(1)} %get-tuple-element.197), channel_id=1, source_target_pairs={{0,8},{8,0},{1,9},{9,1},{2,10},{10,2},{3,11},{11,3},{4,12},{12,4},... | collective-permute-start | bytes 3145736 | tf_op jit(solution)/shard_map/ppermute | solution.py:958
  543.7 32.3 %collective-permute-start.62 = (bf16[512,1024]{1,0:T(8,128)(2,1)}, bf16[512,1024]{1,0:T(8,128)(2,1)}, u32[]{:S(2)}, u32[]{:S(2)}) collective-permute-start(bf16[512,1024]{1,0:T(8,128)(2,1)} %get-tuple-element.193), channel_id=1, source_target_pairs={{16,24},{17,25},{18,26},{19,27},{20,28},{21,29},{22,30},{23,31},{2... | collective-permute-start | bytes 3145736 | tf_op jit(solution)/shard_map/ppermute | solution.py:1133
  557.5 30.7 %collective-permute-start.60 = (bf16[512,1024]{1,0:T(8,128)(2,1)}, bf16[512,1024]{1,0:T(8,128)(2,1)}, u32[]{:S(2)}, u32[]{:S(2)}) collective-permute-start(bf16[512,1024]{1,0:T(8,128)(2,1)} %get-tuple-element.195), channel_id=1, source_target_pairs={{0,8},{1,9},{2,10},{3,11},{4,12},{5,13},{6,14},{7,15},{8,0},{9,1},... | collective-permute-start | bytes 3145736 | tf_op jit(solution)/shard_map/ppermute | solution.py:1133
  (99 other events, 1190.8 us)

commit v5 on v4

--- a/solution.py
+++ b/solution.py
@@ -1218,28 +1218,26 @@
     e_both = summed_here(e_grads)
     d_total = summed_side(d_both, e_first)
     d_first = after(d_first, e_both)
-    bunches = len(w_self.steps) // 2
-
-    def self_part(layer, grad, base, saved, lse, col, row, n):
-        return self_backward(
-            layer, grad, base, saved, lse, col, row, w_self, n * bunches, bunches
-        )
-
-    dx_dec = self_part(1, d_first, d_first, d_qkv, d_lse, dec_col, dec_row, 0)
+    bunches = len(w_self.steps)
+
+    def self_part(layer, grad, base, saved, lse, col, row, first, count):
+        return self_backward(layer, grad, base, saved, lse, col, row, w_self, first, count)
+
+    outputs = rows_back(y_enc, y_dec)
+    dx_dec = self_part(1, d_first, d_first, d_qkv, d_lse, dec_col, dec_row, 0, bunches)
     e_total = summed_side(e_both, dx_dec)
     d_total = summed_rows(d_total, flips[:1], dx_dec)
-    outputs = rows_back(y_enc, y_dec)
-    dx_dec = self_part(1, d_first, after(dx_dec, (e_total, outputs)), d_qkv, d_lse, dec_col, dec_row, 1)
-    e_total = summed_rows(e_total, flips[:1], dx_dec)
-    d_total = summed_rows(d_total, flips[1:2], dx_dec)
-    e_first = after(e_first, (dx_dec, e_total))
-    dx_enc = self_part(0, e_first, e_first, e_qkv, e_lse, enc_col, enc_row, 0)
+    e_first = after(e_first, (dx_dec, e_total, outputs))
+    dx_enc = self_part(0, e_first, e_first, e_qkv, e_lse, enc_col, enc_row, 0, bunches // 2)
+    e_total = summed_rows(e_total, flips[:1], dx_enc)
+    d_total = summed_rows(d_total, flips[1:2], dx_enc)
+    dx_dec_back = layer_back(1, dx_dec)
+    dx_enc = self_part(
+        0, e_first, after(dx_enc, (e_total, d_total, dx_dec_back)), e_qkv, e_lse, enc_col, enc_row,
+        bunches // 2, bunches // 2,
+    )
     e_total = summed_rows(e_total, flips[1:2], dx_enc)
     d_total = summed_rows(d_total, flips[2:], dx_enc)
-    dx_dec_back = layer_back(1, dx_dec)
-    dx_enc = self_part(
-        0, e_first, after(dx_enc, (e_total, d_total, dx_dec_back)), e_qkv, e_lse, enc_col, enc_row, 1
-    )
     e_total = summed_rows(e_total, flips[2:], dx_enc)
     dx = jnp.where(first_core, layer_back(0, dx_enc), dx_dec_back)
     mine = jnp.where(first_core, e_total, d_total)

time: 591 us -> 577 us (0.976); the launches traced: 593 us -> 571 us
  waiting for transfers between devices: 150 us -> 142 us
    ppermute x6, waiting for transfers between devices: 15.1 us -> 3.7 us  [summed_rows(): got = after(lax.ppermute(value, MESH_AXES, route('dp', flip)), token)]
    pallas_call x14 -> x13, Pallas kernels: 256 us -> 252 us  [call(): pl.pallas_call(kernel, grid=(len(plan.steps),), in_specs=list(in_blocks)...]
  transfers between devices with their start and end apart: 65 -> 65, of which waited for: 24 -> 23; matrix products, arithmetic and copies ran while one was open for 10% -> 10% of each run, Pallas kernels for 31% -> 31%
where the time goes in v5:
time: 577 us; the launch traced here: 571 us
  Pallas kernels  258 us (45%)
  waiting for transfers between devices  142 us (25%)
  starting transfers between devices  78.5 us (14%)
  local copies, waits for them, and re-layouts  51.2 us (9%)
  other arithmetic  33.8 us (6%)
  between operations  8.02 us (1%)
    pallas_call x13, Pallas kernels, call(): pl.pallas_call(kernel, grid=(len(plan.steps),), in_specs=list(in_blocks)...  252 us
    ppermute x27, waiting for transfers between devices, send(): got = lax.ppermute(value, axes, route)  100 us
    ppermute x28, waiting for transfers between devices, swap(): lax.ppermute(a, axis, [(0, 1), (1, 0)])  25.7 us
    ppermute x27, starting transfers between devices, send(): got = lax.ppermute(value, axes, route)  25 us
    ppermute x28, starting transfers between devices, swap(): lax.ppermute(a, axis, [(0, 1), (1, 0)])  23.1 us
    unnamed x117, local copies, waits for them, and re-layouts  22.2 us
    ppermute x6, starting transfers between devices, summed_rows(): got = after(lax.ppermute(value, MESH_AXES, route('dp', flip)), token)  21.4 us
    ppermute x2, waiting for transfers between devices, layer_back(): return by_row(keep, lax.ppermute(give, MESH_AXES, route('mp', 1, layer)))  12 us
  transfers between devices with their start and end apart: 65, of which 23 were waited for; matrix products, arithmetic and copies ran while one was open for 10% of the time, Pallas kernels for 31%

profile of v5, /device:TPU:0, one launch (start us, length us, event | category | flops | bytes accessed | tf_op | source)
XLA Modules:
  0.0 571.0 jit_solution(16711740680166641770)
XLA Ops:
  23.5 15.8 %collective-permute-done.1 = bf16[512,1024]{1,0:T(8,128)(2,1)S(1)} collective-permute-done((bf16[512,1024]{1,0:T(8,128)(2,1)S(1)}, bf16[512,1024]{1,0:T(8,128)(2,1)S(1)}, u32[]{:S(2)}, u32[]{:S(2)}) %collective-permute-start.1) | collective-permute-done | bytes 1048608 | tf_op jit(solution)/shard_map/ppermute | solution.py:930
  42.7 21.1 %collective-permute-done.6.refs_8_.refs_10_.refs_6_ = bf16[4,1024,128]{2,1,0:T(8,128)(2,1)} collective-permute-done((bf16[4,1024,128]{2,1,0:T(8,128)(2,1)S(1)}, bf16[4,1024,128]{2,1,0:T(8,128)(2,1)}, u32[]{:S(2)}, u32[]{:S(2)}) %collective-permute-start.6) | collective-permute-done | bytes 1048608 | tf_op jit(solution)/shard_map/ppermute | solution.py:930
  108.2 19.8 %shard_map.192 = (bf16[4,3,512,256]{3,2,1,0:T(8,128)(2,1)}, f32[4,4,512]{2,1,0:T(4,128)}, bf16[512,1024]{1,0:T(8,128)(2,1)}, f32[512,1]{1,0:T(8,128)}) custom-call(bf16[512,1024]{1,0:T(8,128)(2,1)} %get-tuple-element.188.refs_0_, s32[512,1]{1,0:T(8,128)} %copy.34.refs_1_.refs_4_, s32[1,512]{1,0:T(1,128)} %bitcast.152, ...), custom_call_target="tpu_custom_call" | custom-call | flops 25769803776 | bytes 42949672 | tf_op jit(solution)/shard_map/pallas_call | solution.py:134
  128.3 7.2 %collective-permute-done.21.refs_13_.refs_18_ = bf16[2304,256]{1,0:T(8,128)(2,1)} collective-permute-done((bf16[2304,256]{1,0:T(8,128)(2,1)}, bf16[2304,256]{1,0:T(8,128)(2,1)}, u32[]{:S(2)}, u32[]{:S(2)}) %collective-permute-start.21) | collective-permute-done | bytes 1179680 | tf_op jit(solution)/shard_map/ppermute | solution.py:930
  138.4 19.5 %shard_map.193 = (bf16[4,3,512,256]{3,2,1,0:T(8,128)(2,1)}, f32[4,4,512]{2,1,0:T(4,128)}, bf16[512,1024]{1,0:T(8,128)(2,1)}, f32[512,1]{1,0:T(8,128)}) custom-call(bf16[512,1024]{1,0:T(8,128)(2,1)} %get-tuple-element.108.refs_0_, s32[512,1]{1,0:T(8,128)} %copy.35.refs_1_.refs_4_, s32[1,512]{1,0:T(1,128)} %bitcast.159, ...), custom_call_target="tpu_custom_call" | custom-call | flops 25769803776 | bytes 42949672 | tf_op jit(solution)/shard_map/pallas_call | solution.py:134
  175.5 20.8 %shard_map.197 = (bf16[4,512,1024]{2,1,0:T(8,128)(2,1)}, bf16[2,512,256]{2,1,0:T(8,128)(2,1)}, bf16[2,512,256]{2,1,0:T(8,128)(2,1)}, bf16[512,1024]{1,0:T(8,128)...) custom-call(bf16[512,1024]{1,0:T(8,128)(2,1)} %get-tuple-element.110.refs_0_.refs_4_, ...), custom_call_target="tpu_custom_call" | custom-call | flops 28991029248 | bytes 48318384 | tf_op jit(solution)/shard_map/pallas_call | solution.py:134
  197.5 12.8 %collective-permute-done.29.refs_13_.refs_18_ = bf16[2304,256]{1,0:T(8,128)(2,1)} collective-permute-done((bf16[2304,256]{1,0:T(8,128)(2,1)S(1)}, bf16[2304,256]{1,0:T(8,128)(2,1)}, u32[]{:S(2)}, u32[]{:S(2)}) %collective-permute-start.29) | collective-permute-done | bytes 1179680 | tf_op jit(solution)/shard_map/ppermute | solution.py:930
  211.5 6.9 %shard_map.200.refs_2_.refs_6_ = bf16[4,2,512,256]{3,2,1,0:T(8,128)(2,1)} custom-call(bf16[512,1024]{1,0:T(8,128)(2,1)} %get-tuple-element.125.refs_0_, bf16[1024,512]{1,0:T(8,128)(2,1)} %bitcast.131, bf16[1024,512]{1,0:T(8,128)(2,1)} %copy-done.51, bf16[1024,512]{1,0:T(8,128)(2,1)} %bitcast.138, bf16[1024,512]{1,0:T(8,128)(2,1)} %copy-done.50, ...), custom_call_target="tpu_custom_call" | custom-call | flops 6442450944 | bytes 10737418 | tf_op jit(solution)/shard_map/pallas_call | solution.py:134
  233.0 15.1 %collective-permute-done.47 = bf16[512,1024]{1,0:T(8,128)(2,1)} collective-permute-done((bf16[512,1024]{1,0:T(8,128)(2,1)}, bf16[512,1024]{1,0:T(8,128)(2,1)}, u32[]{:S(2)}, u32[]{:S(2)}) %collective-permute-start.47) | collective-permute-done | bytes 1048608 | tf_op jit(solution)/shard_map/ppermute | solution.py:930
  252.6 22.9 %shard_map.201 = (bf16[4,512,256]{2,1,0:T(8,128)(2,1)}, f32[4,2,4,512]{3,2,1,0:T(4,128)}, bf16[512,1024]{1,0:T(8,128)(2,1)}, f32[512,1]{1,0:T(8,128)}) custom-call(bf16[512,1024]{1,0:T(8,128)(2,1)} %get-tuple-element.122.refs_0_.refs_1_, f32[1,1024]{1,0:T(1,128)} %get-tuple-element.206.refs_3_.refs_1_, bf16[4,2,512,256]{3,2,1,0:T(8,128)(2,1)} %shard_map.200.refs_2_.refs_6_, ...), custom_call_target="tpu_custom_call" | custom-call | flops 32212254720 | bytes 53687092 | tf_op jit(solution)/shard_map/pallas_call | solution.py:134
  275.5 7.3 %collective-permute-start.44 = (bf16[2304,256]{1,0:T(8,128)(2,1)}, bf16[2304,256]{1,0:T(8,128)(2,1)S(1)}, u32[]{:S(2)}, u32[]{:S(2)}) collective-permute-start(bf16[2304,256]{1,0:T(8,128)(2,1)} %collective-permute-done.43.refs_19_.refs_24_), channel_id=1, source_target_pairs={{0,16},{16,0},{1,17},{17,1},{2,18},{18,2},{3,19},{19,3},{4,20},{20... | collective-permute-start | bytes 3538952 | tf_op jit(solution)/shard_map/ppermute | solution.py:958
  290.6 21.2 %shard_map.203 = (bf16[4,512,1024]{2,1,0:T(8,128)(2,1)}, bf16[2,512,256]{2,1,0:T(8,128)(2,1)}, bf16[2,512,256]{2,1,0:T(8,128)(2,1)}, bf16[512,1024]{1,0:T(8,128)...) custom-call(bf16[512,1024]{1,0:T(8,128)(2,1)} %get-tuple-element.136.refs_0_.refs_4_, f32[1,1024]{1,0:T(1,128)} %bitcast.164, ...), custom_call_target="tpu_custom_call" | custom-call | flops 28991029248 | bytes 48318384 | tf_op jit(solution)/shard_map/pallas_call | solution.py:134
  311.8 23.6 %shard_map.204 = (bf16[512,1024]{1,0:T(8,128)(2,1)}, bf16[2,2,272,1024]{3,2,1,0:T(8,128)(2,1)}) custom-call(bf16[512,1024]{1,0:T(8,128)(2,1)} %get-tuple-element.186.refs_0_, bf16[512,1024]{1,0:T(8,128)(2,1)} %get-tuple-element.150.refs_1_, f32[512,1]{1,0:T(8,128)} %get-tuple-element.151.refs_2_, f32[1,1024]{1,0:T(1,128)} %get-tuple-element.205.refs_2_.refs_3_, ...), custom_call_target="tpu_custom_call" | custom-call | flops 28991029248 | bytes 48318384 | tf_op jit(solution)/shard_map/pallas_call | solution.py:134
  341.6 29.1 %shard_map.205 = (bf16[512,1024]{1,0:T(8,128)(2,1)}, bf16[4,2,512,256]{3,2,1,0:T(8,128)(2,1)}, bf16[4,2,512,256]{3,2,1,0:T(8,128)(2,1)}) custom-call(bf16[512,1024]{1,0:T(8,128)(2,1)} %get-tuple-element.157.refs_0_, bf16[512,1024]{1,0:T(8,128)(2,1)} %get-tuple-element.122.refs_0_.refs_1_, f32[512,1]{1,0:T(8,128)} %get-tuple-element.109.refs_2_, ...), custom_call_target="tpu_custom_call" | custom-call | flops 70866960384 | bytes 118111600 | tf_op jit(solution)/shard_map/pallas_call | solution.py:134
  370.7 9.2 %collective-permute-start.50 = (bf16[4,2,512,256]{3,2,1,0:T(8,128)(2,1)}, bf16[4,2,512,256]{3,2,1,0:T(8,128)(2,1)}, u32[]{:S(2)}, u32[]{:S(2)}) collective-permute-start(bf16[4,2,512,256]{3,2,1,0:T(8,128)(2,1)} %get-tuple-element.161), channel_id=1, source_target_pairs={{0,16},{16,0},{1,17},{17,1},{2,18},{18,2},{3,19},{19,3},{4,20},{20... | collective-permute-start | bytes 6291464 | tf_op jit(solution)/shard_map/ppermute | solution.py:958
  384.1 8.1 %shard_map.206.refs_0_ = bf16[512,1024]{1,0:T(8,128)(2,1)} custom-call(bf16[512,1024]{1,0:T(8,128)(2,1)} %get-tuple-element.187.refs_0_, bf16[4,2,512,256]{3,2,1,0:T(8,128)(2,1)} %get-tuple-element.160.refs_1_, bf16[4,2,512,256]{3,2,1,0:T(8,128)(2,1)} %collective-permute-done.50.refs_2_, bf16[1024,512]{1,0:T(8,128)(2,1)} %bitcast.134, ...), custom_call_target="tpu_custom_call" | custom-call | flops 6442450944 | bytes 10737418 | tf_op jit(solution)/shard_map/pallas_call | solution.py:134
  392.1 24.0 %shard_map.207 = (bf16[512,1024]{1,0:T(8,128)(2,1)}, bf16[2,2,272,1024]{3,2,1,0:T(8,128)(2,1)}) custom-call(bf16[512,1024]{1,0:T(8,128)(2,1)} %shard_map.206.refs_0_, bf16[512,1024]{1,0:T(8,128)(2,1)} %get-tuple-element.162.refs_1_, f32[512,1]{1,0:T(8,128)} %get-tuple-element.126.refs_2_, f32[1,1024]{1,0:T(1,128)} %get-tuple-element.210.refs_2_.refs_3_, ...), custom_call_target="tpu_custom_call" | custom-call | flops 28991029248 | bytes 48318384 | tf_op jit(solution)/shard_map/pallas_call | solution.py:134
  421.8 10.9 %collective-permute-done.54 = bf16[272,1024]{1,0:T(8,128)(2,1)S(1)} collective-permute-done((bf16[272,1024]{1,0:T(8,128)(2,1)S(1)}, bf16[272,1024]{1,0:T(8,128)(2,1)S(1)}, u32[]{:S(2)}, u32[]{:S(2)}) %collective-permute-start.54) | collective-permute-done | bytes 557088 | tf_op jit(solution)/shard_map/ppermute | solution.py:958
  433.9 25.6 %shard_map.208 = bf16[512,1024]{1,0:T(8,128)(2,1)} custom-call(bf16[512,1024]{1,0:T(8,128)(2,1)} %get-tuple-element.169.refs_0_.refs_1_, bf16[512,1024]{1,0:T(8,128)(2,1)} %get-tuple-element.169.refs_0_.refs_1_, bf16[4,3,512,256]{3,2,1,0:T(8,128)(2,1)} %get-tuple-element.170.refs_2_, f32[4,4,512]{2,1,0:T(4,128)} %get-tuple-element.171.refs_3_, ...), custom_call_target="tpu_custom_call" | custom-call | flops 45097156608 | bytes 75161928 | tf_op jit(solution)/shard_map/pallas_call | solution.py:134
  462.0 19.0 %collective-permute-start.56 = (bf16[272,1024]{1,0:T(8,128)(2,1)S(1)}, bf16[272,1024]{1,0:T(8,128)(2,1)S(1)}, u32[]{:S(2)}, u32[]{:S(2)}) collective-permute-start(bf16[272,1024]{1,0:T(8,128)(2,1)S(1)} %add_convert_fusion.4), channel_id=1, source_target_pairs={{0,1},{1,0},{2,3},{3,2},{4,5},{5,4},{6,7},{7,6},{8,9},{9,8},{10,11... | collective-permute-start | bytes 1671176 | tf_op jit(solution)/shard_map/ppermute | solution.py:1197
  481.3 15.2 %shard_map.209.refs_1_ = bf16[512,1024]{1,0:T(8,128)(2,1)} custom-call(bf16[512,1024]{1,0:T(8,128)(2,1)} %get-tuple-element.173.refs_0_.refs_1_, bf16[512,1024]{1,0:T(8,128)(2,1)} %get-tuple-element.173.refs_0_.refs_1_, bf16[4,3,512,256]{3,2,1,0:T(8,128)(2,1)} %get-tuple-element.174.refs_2_, f32[4,4,512]{2,1,0:T(4,128)} %get-tuple-element.175.refs_3_, ...), custom_call_target="tpu_custom_call" | custom-call | flops 22548578304 | bytes 37580964 | tf_op jit(solution)/shard_map/pallas_call | solution.py:134
  497.1 14.8 %shard_map.210 = bf16[512,1024]{1,0:T(8,128)(2,1)} custom-call(bf16[512,1024]{1,0:T(8,128)(2,1)} %get-tuple-element.173.refs_0_.refs_1_, bf16[512,1024]{1,0:T(8,128)(2,1)} %shard_map.209.refs_1_, bf16[4,3,512,256]{3,2,1,0:T(8,128)(2,1)} %get-tuple-element.174.refs_2_, f32[4,4,512]{2,1,0:T(4,128)} %get-tuple-element.175.refs_3_, ...), custom_call_target="tpu_custom_call" | custom-call | flops 22548578304 | bytes 37580964 | tf_op jit(solution)/shard_map/pallas_call | solution.py:134
  535.4 8.4 %collective-permute-done.46 = bf16[512,1024]{1,0:T(8,128)(2,1)S(1)} collective-permute-done((bf16[512,1024]{1,0:T(8,128)(2,1)S(1)}, bf16[512,1024]{1,0:T(8,128)(2,1)S(1)}, u32[]{:S(2)}, u32[]{:S(2)}) %collective-permute-start.46) | collective-permute-done | bytes 1048608 | tf_op jit(solution)/shard_map/ppermute | solution.py:958
  554.3 12.0 %collective-permute-done.58 = bf16[512,1024]{1,0:T(8,128)(2,1)} collective-permute-done((bf16[512,1024]{1,0:T(8,128)(2,1)}, bf16[512,1024]{1,0:T(8,128)(2,1)}, u32[]{:S(2)}, u32[]{:S(2)}) %collective-permute-start.58) | collective-permute-done | bytes 1048608 | tf_op jit(solution)/shard_map/ppermute | solution.py:1133
  (304 shorter events, 172.5 us)
Async XLA Ops:
  6.6 33.0 %collective-permute-start.9 = (bf16[2048,1024]{1,0:T(8,128)(2,1)}, bf16[2048,1024]{1,0:T(8,128)(2,1)}, u32[]{:S(2)}, u32[]{:S(2)}) collective-permute-start(bf16[2048,1024]{1,0:T(8,128)(2,1)} %bitcast.90), channel_id=1, source_target_pairs={{0,16},{1,17},{2,18},{3,19},{4,20},{5,21},{6,22},{7,23},{8,24},{9,... | collective-permute-start | bytes 12582920 | tf_op jit(solution)/shard_map/ppermute | solution.py:930
  7.0 34.5 %collective-permute-start.8 = (bf16[1024,2048]{1,0:T(8,128)(2,1)}, bf16[1024,2048]{1,0:T(8,128)(2,1)}, u32[]{:S(2)}, u32[]{:S(2)}) collective-permute-start(bf16[1024,2048]{1,0:T(8,128)(2,1)} %bitcast.81), channel_id=1, source_target_pairs={{0,16},{1,17},{2,18},{3,19},{4,20},{5,21},{6,22},{7,23},{8,24},{9,... | collective-permute-start | bytes 12582920 | tf_op jit(solution)/shard_map/ppermute | solution.py:930
  106.4 29.2 %collective-permute-start.21 = (bf16[2304,256]{1,0:T(8,128)(2,1)}, bf16[2304,256]{1,0:T(8,128)(2,1)}, u32[]{:S(2)}, u32[]{:S(2)}) collective-permute-start(bf16[2304,256]{1,0:T(8,128)(2,1)} %shard_map.194), channel_id=1, source_target_pairs={{0,8},{1,9},{2,10},{3,11},{4,12},{5,13},{6,14},{7,15},{8,0},{9,1},... | collective-permute-start | bytes 3538952 | tf_op jit(solution)/shard_map/ppermute | solution.py:930
  128.0 31.6 %collective-permute-start.27 = (bf16[2304,256]{1,0:T(8,128)(2,1)}, bf16[2304,256]{1,0:T(8,128)(2,1)}, u32[]{:S(2)}, u32[]{:S(2)}) collective-permute-start(bf16[2304,256]{1,0:T(8,128)(2,1)} %copy-done.24), channel_id=1, source_target_pairs={{0,8},{1,9},{2,10},{3,11},{4,12},{5,13},{6,14},{7,15},{8,0},{9,1},... | collective-permute-start | bytes 3538952 | tf_op jit(solution)/shard_map/ppermute | solution.py:930
  135.6 25.8 %collective-permute-start.25 = (bf16[2304,256]{1,0:T(8,128)(2,1)}, bf16[2304,256]{1,0:T(8,128)(2,1)}, u32[]{:S(2)}, u32[]{:S(2)}) collective-permute-start(bf16[2304,256]{1,0:T(8,128)(2,1)} %collective-permute-done.21.refs_13_.refs_18_), channel_id=1, source_target_pairs={{0,2},{1,3},{2,0},{3,1},{4,6},{5,7},{6,4},{7,5},{8,10},{9,11},{10,... | collective-permute-start | bytes 3538952 | tf_op jit(solution)/shard_map/ppermute | solution.py:930
  137.2 25.5 %collective-permute-start.23 = (bf16[2304,256]{1,0:T(8,128)(2,1)}, bf16[2304,256]{1,0:T(8,128)(2,1)}, u32[]{:S(2)}, u32[]{:S(2)}) collective-permute-start(bf16[2304,256]{1,0:T(8,128)(2,1)} %collective-permute-done.21.refs_13_.refs_18_), channel_id=1, source_target_pairs={{0,1},{1,0},{2,3},{3,2},{4,5},{5,4},{6,7},{7,6},{8,9},{9,8},{10,11... | collective-permute-start | bytes 3538952 | tf_op jit(solution)/shard_map/ppermute | solution.py:930
  170.2 26.3 %collective-permute-start.33 = (bf16[2,1024,128]{2,1,0:T(8,128)(2,1)}, bf16[2,1024,128]{2,1,0:T(8,128)(2,1)S(1)}, u32[]{:S(2)}, u32[]{:S(2)}) collective-permute-start(bf16[2,1024,128]{2,1,0:T(8,128)(2,1)} %collective-permute-done.20.refs_5_.refs_10_.refs_14_.refs_7_), channel_id=1, source_target_pairs={{0,2},{1,3},{2,0},{3,1},{4,6},{5,7},{6,4},{7,5},{8,10},{9,11},{10,... | collective-permute-start | bytes 1572872 | tf_op jit(solution)/shard_map/ppermute | solution.py:930
  171.0 26.0 %collective-permute-start.31 = (bf16[2,1024,128]{2,1,0:T(8,128)(2,1)}, bf16[2,1024,128]{2,1,0:T(8,128)(2,1)S(1)}, u32[]{:S(2)}, u32[]{:S(2)}) collective-permute-start(bf16[2,1024,128]{2,1,0:T(8,128)(2,1)} %collective-permute-done.20.refs_5_.refs_10_.refs_14_.refs_7_), channel_id=1, source_target_pairs={{0,1},{1,0},{2,3},{3,2},{4,5},{5,4},{6,7},{7,6},{8,9},{9,8},{10,11... | collective-permute-start | bytes 1572872 | tf_op jit(solution)/shard_map/ppermute | solution.py:930
  174.0 36.3 %collective-permute-start.29 = (bf16[2304,256]{1,0:T(8,128)(2,1)S(1)}, bf16[2304,256]{1,0:T(8,128)(2,1)}, u32[]{:S(2)}, u32[]{:S(2)}) collective-permute-start(bf16[2304,256]{1,0:T(8,128)(2,1)S(1)} %shard_map.198), channel_id=1, source_target_pairs={{0,8},{1,9},{2,10},{3,11},{4,12},{5,13},{6,14},{7,15},{8,0},{9,1},... | collective-permute-start | bytes 3538952 | tf_op jit(solution)/shard_map/ppermute | solution.py:930
  218.5 34.1 %collective-permute-start.37 = (bf16[4,2,512,256]{3,2,1,0:T(8,128)(2,1)}, bf16[4,2,512,256]{3,2,1,0:T(8,128)(2,1)}, u32[]{:S(2)}, u32[]{:S(2)}) collective-permute-start(bf16[4,2,512,256]{3,2,1,0:T(8,128)(2,1)} %shard_map.200.refs_2_.refs_6_), channel_id=1, source_target_pairs={{0,16},{16,0},{1,17},{17,1},{2,18},{18,2},{3,19},{19,3},{4,20},{20... | collective-permute-start | bytes 6291464 | tf_op jit(solution)/shard_map/ppermute | solution.py:958
  221.8 26.3 %collective-permute-start.47 = (bf16[512,1024]{1,0:T(8,128)(2,1)}, bf16[512,1024]{1,0:T(8,128)(2,1)}, u32[]{:S(2)}, u32[]{:S(2)}) collective-permute-start(bf16[512,1024]{1,0:T(8,128)(2,1)} %get-tuple-element.149), channel_id=1, source_target_pairs={{0,8},{1,9},{2,10},{3,11},{4,12},{5,13},{6,14},{7,15},{8,0},{9,1},... | collective-permute-start | bytes 3145736 | tf_op jit(solution)/shard_map/ppermute | solution.py:930
  230.3 45.1 %collective-permute-start.43 = (bf16[2304,256]{1,0:T(8,128)(2,1)S(1)}, bf16[2304,256]{1,0:T(8,128)(2,1)}, u32[]{:S(2)}, u32[]{:S(2)}) collective-permute-start(bf16[2304,256]{1,0:T(8,128)(2,1)S(1)} %shard_map.202), channel_id=1, source_target_pairs={{0,8},{1,9},{2,10},{3,11},{4,12},{5,13},{6,14},{7,15},{8,0},{9,1},... | collective-permute-start | bytes 3538952 | tf_op jit(solution)/shard_map/ppermute | solution.py:930
  230.7 52.1 %collective-permute-start.41 = (bf16[2304,256]{1,0:T(8,128)(2,1)}, bf16[2304,256]{1,0:T(8,128)(2,1)}, u32[]{:S(2)}, u32[]{:S(2)}) collective-permute-start(bf16[2304,256]{1,0:T(8,128)(2,1)} %collective-permute-done.29.refs_13_.refs_18_), channel_id=1, source_target_pairs={{0,2},{1,3},{2,0},{3,1},{4,6},{5,7},{6,4},{7,5},{8,10},{9,11},{10,... | collective-permute-start | bytes 3538952 | tf_op jit(solution)/shard_map/ppermute | solution.py:930
  232.2 50.6 %collective-permute-start.39 = (bf16[2304,256]{1,0:T(8,128)(2,1)}, bf16[2304,256]{1,0:T(8,128)(2,1)}, u32[]{:S(2)}, u32[]{:S(2)}) collective-permute-start(bf16[2304,256]{1,0:T(8,128)(2,1)} %collective-permute-done.29.refs_13_.refs_18_), channel_id=1, source_target_pairs={{0,1},{1,0},{2,3},{3,2},{4,5},{5,4},{6,7},{7,6},{8,9},{9,8},{10,11... | collective-permute-start | bytes 3538952 | tf_op jit(solution)/shard_map/ppermute | solution.py:930
  252.5 31.4 %collective-permute-start.48 = (bf16[512,1024]{1,0:T(8,128)(2,1)S(1)}, bf16[512,1024]{1,0:T(8,128)(2,1)S(1)}, u32[]{:S(2)}, u32[]{:S(2)}) collective-permute-start(bf16[512,1024]{1,0:T(8,128)(2,1)S(1)} %constant_dynamic-slice_fusion.4), channel_id=1, source_target_pairs={{0,16},{16,0},{1,17},{17,1},{2,18},{18,2},{3,19},{19,3},{4,20},{20... | collective-permute-start | bytes 3145736 | tf_op jit(solution)/shard_map/ppermute | solution.py:958
  383.7 34.4 %collective-permute-start.45 = (bf16[512,1024]{1,0:T(8,128)(2,1)}, bf16[512,1024]{1,0:T(8,128)(2,1)}, u32[]{:S(2)}, u32[]{:S(2)}) collective-permute-start(bf16[512,1024]{1,0:T(8,128)(2,1)} %broadcast_select_fusion.4), channel_id=1, source_target_pairs={{0,16},{16,0},{1,17},{17,1},{2,18},{18,2},{3,19},{19,3},{4,20},{20... | collective-permute-start | bytes 3145736 | tf_op jit(solution)/shard_map/ppermute | solution.py:958
  432.9 28.9 %collective-permute-start.55 = (bf16[272,1024]{1,0:T(8,128)(2,1)S(1)}, bf16[272,1024]{1,0:T(8,128)(2,1)S(1)}, u32[]{:S(2)}, u32[]{:S(2)}) collective-permute-start(bf16[272,1024]{1,0:T(8,128)(2,1)S(1)} %fusion.4), channel_id=1, source_target_pairs={{0,4},{1,5},{2,6},{3,7},{4,0},{5,1},{6,2},{7,3},{8,12},{9,13},{10,... | collective-permute-start | bytes 1671176 | tf_op jit(solution)/shard_map/ppermute | solution.py:1197
  433.5 47.5 %collective-permute-start.52 = (bf16[272,1024]{1,0:T(8,128)(2,1)S(1)}, bf16[272,1024]{1,0:T(8,128)(2,1)S(1)}, u32[]{:S(2)}, u32[]{:S(2)}) collective-permute-start(bf16[272,1024]{1,0:T(8,128)(2,1)S(1)} %slice_bitcast_fusion.3), channel_id=1, source_target_pairs={{0,8},{8,0},{1,9},{9,1},{2,10},{10,2},{3,11},{11,3},{4,12},{12,4},... | collective-permute-start | bytes 1671176 | tf_op jit(solution)/shard_map/ppermute | solution.py:958
  459.5 59.9 %collective-permute-start.59 = (bf16[512,1024]{1,0:T(8,128)(2,1)}, bf16[512,1024]{1,0:T(8,128)(2,1)}, u32[]{:S(2)}, u32[]{:S(2)}) collective-permute-start(bf16[512,1024]{1,0:T(8,128)(2,1)} %shard_map.208), channel_id=1, source_target_pairs={{0,16},{1,17},{2,18},{3,19},{4,20},{5,21},{6,22},{7,23},{8,24},{9,... | collective-permute-start | bytes 3145736 | tf_op jit(solution)/shard_map/ppermute | solution.py:1130
  462.0 34.5 %collective-permute-start.56 = (bf16[272,1024]{1,0:T(8,128)(2,1)S(1)}, bf16[272,1024]{1,0:T(8,128)(2,1)S(1)}, u32[]{:S(2)}, u32[]{:S(2)}) collective-permute-start(bf16[272,1024]{1,0:T(8,128)(2,1)S(1)} %add_convert_fusion.4), channel_id=1, source_target_pairs={{0,1},{1,0},{2,3},{3,2},{4,5},{5,4},{6,7},{7,6},{8,9},{9,8},{10,11... | collective-permute-start | bytes 1671176 | tf_op jit(solution)/shard_map/ppermute | solution.py:1197
  496.7 28.2 %collective-permute-start.63 = (bf16[272,1024]{1,0:T(8,128)(2,1)S(1)}, bf16[272,1024]{1,0:T(8,128)(2,1)S(1)}, u32[]{:S(2)}, u32[]{:S(2)}) collective-permute-start(bf16[272,1024]{1,0:T(8,128)(2,1)S(1)} %add_convert_fusion.3), channel_id=1, source_target_pairs={{0,2},{1,3},{2,0},{3,1},{4,6},{5,7},{6,4},{7,5},{8,10},{9,11},{10,... | collective-permute-start | bytes 1671176 | tf_op jit(solution)/shard_map/ppermute | solution.py:1197
  517.6 26.1 %collective-permute-start.46 = (bf16[512,1024]{1,0:T(8,128)(2,1)S(1)}, bf16[512,1024]{1,0:T(8,128)(2,1)S(1)}, u32[]{:S(2)}, u32[]{:S(2)}) collective-permute-start(bf16[512,1024]{1,0:T(8,128)(2,1)S(1)} %get-tuple-element.195), channel_id=1, source_target_pairs={{0,8},{8,0},{1,9},{9,1},{2,10},{10,2},{3,11},{11,3},{4,12},{12,4},... | collective-permute-start | bytes 3145736 | tf_op jit(solution)/shard_map/ppermute | solution.py:958
  523.2 31.1 %collective-permute-start.60 = (bf16[512,1024]{1,0:T(8,128)(2,1)}, bf16[512,1024]{1,0:T(8,128)(2,1)}, u32[]{:S(2)}, u32[]{:S(2)}) collective-permute-start(bf16[512,1024]{1,0:T(8,128)(2,1)} %get-tuple-element.191), channel_id=1, source_target_pairs={{16,24},{17,25},{18,26},{19,27},{20,28},{21,29},{22,30},{23,31},{2... | collective-permute-start | bytes 3145736 | tf_op jit(solution)/shard_map/ppermute | solution.py:1133
  531.7 34.6 %collective-permute-start.58 = (bf16[512,1024]{1,0:T(8,128)(2,1)}, bf16[512,1024]{1,0:T(8,128)(2,1)}, u32[]{:S(2)}, u32[]{:S(2)}) collective-permute-start(bf16[512,1024]{1,0:T(8,128)(2,1)} %get-tuple-element.193), channel_id=1, source_target_pairs={{0,8},{1,9},{2,10},{3,11},{4,12},{5,13},{6,14},{7,15},{8,0},{9,1},... | collective-permute-start | bytes 3145736 | tf_op jit(solution)/shard_map/ppermute | solution.py:1133
  (99 other events, 1148.5 us)

commit v6 on v5

--- a/solution.py
+++ b/solution.py
@@ -1228,17 +1228,12 @@
     e_total = summed_side(e_both, dx_dec)
     d_total = summed_rows(d_total, flips[:1], dx_dec)
     e_first = after(e_first, (dx_dec, e_total, outputs))
-    dx_enc = self_part(0, e_first, e_first, e_qkv, e_lse, enc_col, enc_row, 0, bunches // 2)
+    dx_dec_back = layer_back(1, dx_dec)
+    dx_enc = self_part(0, e_first, e_first, e_qkv, e_lse, enc_col, enc_row, 0, bunches)
     e_total = summed_rows(e_total, flips[:1], dx_enc)
     d_total = summed_rows(d_total, flips[1:2], dx_enc)
-    dx_dec_back = layer_back(1, dx_dec)
-    dx_enc = self_part(
-        0, e_first, after(dx_enc, (e_total, d_total, dx_dec_back)), e_qkv, e_lse, enc_col, enc_row,
-        bunches // 2, bunches // 2,
-    )
-    e_total = summed_rows(e_total, flips[1:2], dx_enc)
+    e_total = summed_rows(e_total, flips[1:], dx_enc)
     d_total = summed_rows(d_total, flips[2:], dx_enc)
-    e_total = summed_rows(e_total, flips[2:], dx_enc)
     dx = jnp.where(first_core, layer_back(0, dx_enc), dx_dec_back)
     mine = jnp.where(first_core, e_total, d_total)
     other = swap(jnp.where(first_core, d_total, e_total), "section")

time: 577 us -> 560 us (0.971)
  waiting for transfers between devices: 142 us -> 129 us
    ppermute x28, waiting for transfers between devices: 25.7 us -> 8.19 us  [swap(): lax.ppermute(a, axis, [(0, 1), (1, 0)])]
    ppermute x6, waiting for transfers between devices: 3.7 us -> 20.2 us  [summed_rows(): got = after(lax.ppermute(value, MESH_AXES, route('dp', flip)), token)]
    ppermute x2, waiting for transfers between devices: 12 us -> 0.01 us  [layer_back(): return by_row(keep, lax.ppermute(give, MESH_AXES, route('mp', 1, layer)))]
    pallas_call x13 -> x12, Pallas kernels: 252 us -> 247 us  [call(): pl.pallas_call(kernel, grid=(len(plan.steps),), in_specs=list(in_blocks)...]
    unnamed x117 -> x113, local copies, waits for them, and re-layouts: 22.2 us -> 20.2 us
  transfers between devices with their start and end apart: 65 -> 65, of which waited for: 23 -> 21; matrix products, arithmetic and copies ran while one was open for 10% -> 10% of each run, Pallas kernels for 31% -> 31%
where the time goes in v6:
time: 560 us; the launch traced here: 555 us
  Pallas kernels  253 us (45%)
  waiting for transfers between devices  129 us (23%)
  starting transfers between devices  80.4 us (14%)
  local copies, waits for them, and re-layouts  48.3 us (9%)
  other arithmetic  37.1 us (7%)
  between operations  7.64 us (1%)
    pallas_call x12, Pallas kernels, call(): pl.pallas_call(kernel, grid=(len(plan.steps),), in_specs=list(in_blocks)...  247 us
    ppermute x27, waiting for transfers between devices, send(): got = lax.ppermute(value, axes, route)  101 us
    ppermute x6, starting transfers between devices, summed_rows(): got = after(lax.ppermute(value, MESH_AXES, route('dp', flip)), token)  25 us
    ppermute x27, starting transfers between devices, send(): got = lax.ppermute(value, axes, route)  25 us
    ppermute x28, starting transfers between devices, swap(): lax.ppermute(a, axis, [(0, 1), (1, 0)])  22.5 us
    ppermute x6, waiting for transfers between devices, summed_rows(): got = after(lax.ppermute(value, MESH_AXES, route('dp', flip)), token)  20.2 us
    unnamed x113, local copies, waits for them, and re-layouts  20.2 us
  transfers between devices with their start and end apart: 65, of which 21 were waited for; matrix products, arithmetic and copies ran while one was open for 10% of the time, Pallas kernels for 31%

profile of v6, /device:TPU:0, one launch (start us, length us, event | category | flops | bytes accessed | tf_op | source)
XLA Modules:
  0.0 555.5 jit_solution(16788748667121339190)
XLA Ops:
  1.1 5.5 collective-permute-done.4.refs_5_.refs_7_
  15.1 6.6 %collective-permute-done.5.refs_7_.refs_9_ = bf16[512,1024]{1,0:T(8,128)(2,1)} collective-permute-done((bf16[512,1024]{1,0:T(8,128)(2,1)}, bf16[512,1024]{1,0:T(8,128)(2,1)}, u32[]{:S(2)}, u32[]{:S(2)}) %collective-permute-start.5) | collective-permute-done | bytes 1048608 | tf_op jit(solution)/shard_map/ppermute | solution.py:930
  23.5 15.8 %collective-permute-done.1 = bf16[512,1024]{1,0:T(8,128)(2,1)S(1)} collective-permute-done((bf16[512,1024]{1,0:T(8,128)(2,1)S(1)}, bf16[512,1024]{1,0:T(8,128)(2,1)S(1)}, u32[]{:S(2)}, u32[]{:S(2)}) %collective-permute-start.1) | collective-permute-done | bytes 1048608 | tf_op jit(solution)/shard_map/ppermute | solution.py:930
  42.6 21.1 %collective-permute-done.6.refs_8_.refs_10_ = bf16[4,1024,128]{2,1,0:T(8,128)(2,1)} collective-permute-done((bf16[4,1024,128]{2,1,0:T(8,128)(2,1)S(1)}, bf16[4,1024,128]{2,1,0:T(8,128)(2,1)}, u32[]{:S(2)}, u32[]{:S(2)}) %collective-permute-start.6) | collective-permute-done | bytes 1048608 | tf_op jit(solution)/shard_map/ppermute | solution.py:930
  81.3 6.1 %collective-permute-done.18.refs_14_.refs_16_ = bf16[4,1024,128]{2,1,0:T(8,128)(2,1)} collective-permute-done((bf16[4,1024,128]{2,1,0:T(8,128)(2,1)}, bf16[4,1024,128]{2,1,0:T(8,128)(2,1)}, u32[]{:S(2)}, u32[]{:S(2)}) %collective-permute-start.18) | collective-permute-done | bytes 1048608 | tf_op jit(solution)/shard_map/ppermute | solution.py:930
  108.2 19.8 %shard_map.192 = (bf16[4,3,512,256]{3,2,1,0:T(8,128)(2,1)}, f32[4,4,512]{2,1,0:T(4,128)}, bf16[512,1024]{1,0:T(8,128)(2,1)}, f32[512,1]{1,0:T(8,128)}) custom-call(bf16[512,1024]{1,0:T(8,128)(2,1)} %get-tuple-element.186.refs_0_, s32[512,1]{1,0:T(8,128)} %copy.33.refs_1_.refs_4_, s32[1,512]{1,0:T(1,128)} %bitcast.151, ...), custom_call_target="tpu_custom_call" | custom-call | flops 25769803776 | bytes 42949672 | tf_op jit(solution)/shard_map/pallas_call | solution.py:134
  128.4 7.2 %collective-permute-done.21.refs_13_.refs_18_ = bf16[2304,256]{1,0:T(8,128)(2,1)} collective-permute-done((bf16[2304,256]{1,0:T(8,128)(2,1)}, bf16[2304,256]{1,0:T(8,128)(2,1)}, u32[]{:S(2)}, u32[]{:S(2)}) %collective-permute-start.21) | collective-permute-done | bytes 1179680 | tf_op jit(solution)/shard_map/ppermute | solution.py:930
  138.4 19.5 %shard_map.193 = (bf16[4,3,512,256]{3,2,1,0:T(8,128)(2,1)}, f32[4,4,512]{2,1,0:T(4,128)}, bf16[512,1024]{1,0:T(8,128)(2,1)}, f32[512,1]{1,0:T(8,128)}) custom-call(bf16[512,1024]{1,0:T(8,128)(2,1)} %get-tuple-element.107.refs_0_, s32[512,1]{1,0:T(8,128)} %copy.34.refs_1_.refs_4_, s32[1,512]{1,0:T(1,128)} %bitcast.157, ...), custom_call_target="tpu_custom_call" | custom-call | flops 25769803776 | bytes 42949672 | tf_op jit(solution)/shard_map/pallas_call | solution.py:134
  175.5 20.8 %shard_map.197 = (bf16[4,512,1024]{2,1,0:T(8,128)(2,1)}, bf16[2,512,256]{2,1,0:T(8,128)(2,1)}, bf16[2,512,256]{2,1,0:T(8,128)(2,1)}, bf16[512,1024]{1,0:T(8,128)...) custom-call(bf16[512,1024]{1,0:T(8,128)(2,1)} %get-tuple-element.109.refs_0_.refs_4_, ...), custom_call_target="tpu_custom_call" | custom-call | flops 28991029248 | bytes 48318384 | tf_op jit(solution)/shard_map/pallas_call | solution.py:134
  197.5 13.0 %collective-permute-done.29.refs_13_.refs_18_ = bf16[2304,256]{1,0:T(8,128)(2,1)} collective-permute-done((bf16[2304,256]{1,0:T(8,128)(2,1)S(1)}, bf16[2304,256]{1,0:T(8,128)(2,1)}, u32[]{:S(2)}, u32[]{:S(2)}) %collective-permute-start.29) | collective-permute-done | bytes 1179680 | tf_op jit(solution)/shard_map/ppermute | solution.py:930
  211.6 6.9 %shard_map.200.refs_2_.refs_6_ = bf16[4,2,512,256]{3,2,1,0:T(8,128)(2,1)} custom-call(bf16[512,1024]{1,0:T(8,128)(2,1)} %get-tuple-element.124.refs_0_, bf16[1024,512]{1,0:T(8,128)(2,1)} %bitcast.131, bf16[1024,512]{1,0:T(8,128)(2,1)} %copy-done.49, bf16[1024,512]{1,0:T(8,128)(2,1)} %bitcast.138, bf16[1024,512]{1,0:T(8,128)(2,1)} %copy-done.48, ...), custom_call_target="tpu_custom_call" | custom-call | flops 6442450944 | bytes 10737418 | tf_op jit(solution)/shard_map/pallas_call | solution.py:134
  233.1 15.1 %collective-permute-done.47 = bf16[512,1024]{1,0:T(8,128)(2,1)} collective-permute-done((bf16[512,1024]{1,0:T(8,128)(2,1)}, bf16[512,1024]{1,0:T(8,128)(2,1)}, u32[]{:S(2)}, u32[]{:S(2)}) %collective-permute-start.47) | collective-permute-done | bytes 1048608 | tf_op jit(solution)/shard_map/ppermute | solution.py:930
  253.3 22.8 %shard_map.201 = (bf16[4,512,256]{2,1,0:T(8,128)(2,1)}, f32[4,2,4,512]{3,2,1,0:T(4,128)}, bf16[512,1024]{1,0:T(8,128)(2,1)}, f32[512,1]{1,0:T(8,128)}) custom-call(bf16[512,1024]{1,0:T(8,128)(2,1)} %get-tuple-element.121.refs_0_.refs_1_, f32[1,1024]{1,0:T(1,128)} %get-tuple-element.204.refs_3_.refs_1_, bf16[4,2,512,256]{3,2,1,0:T(8,128)(2,1)} %shard_map.200.refs_2_.refs_6_, ...), custom_call_target="tpu_custom_call" | custom-call | flops 32212254720 | bytes 53687092 | tf_op jit(solution)/shard_map/pallas_call | solution.py:134
  284.6 21.0 %shard_map.203 = (bf16[4,512,1024]{2,1,0:T(8,128)(2,1)}, bf16[2,512,256]{2,1,0:T(8,128)(2,1)}, bf16[2,512,256]{2,1,0:T(8,128)(2,1)}, bf16[512,1024]{1,0:T(8,128)...) custom-call(bf16[512,1024]{1,0:T(8,128)(2,1)} %get-tuple-element.135.refs_0_.refs_4_, f32[1,1024]{1,0:T(1,128)} %bitcast.162, ...), custom_call_target="tpu_custom_call" | custom-call | flops 28991029248 | bytes 48318384 | tf_op jit(solution)/shard_map/pallas_call | solution.py:134
  305.6 23.6 %shard_map.204 = (bf16[512,1024]{1,0:T(8,128)(2,1)}, bf16[2,2,272,1024]{3,2,1,0:T(8,128)(2,1)}) custom-call(bf16[512,1024]{1,0:T(8,128)(2,1)} %get-tuple-element.184.refs_0_, bf16[512,1024]{1,0:T(8,128)(2,1)} %get-tuple-element.149.refs_1_, f32[512,1]{1,0:T(8,128)} %get-tuple-element.150.refs_2_, f32[1,1024]{1,0:T(1,128)} %get-tuple-element.203.refs_2_.refs_3_, ...), custom_call_target="tpu_custom_call" | custom-call | flops 28991029248 | bytes 48318384 | tf_op jit(solution)/shard_map/pallas_call | solution.py:134
  335.4 29.2 %shard_map.205 = (bf16[512,1024]{1,0:T(8,128)(2,1)}, bf16[4,2,512,256]{3,2,1,0:T(8,128)(2,1)}, bf16[4,2,512,256]{3,2,1,0:T(8,128)(2,1)}) custom-call(bf16[512,1024]{1,0:T(8,128)(2,1)} %get-tuple-element.156.refs_0_, bf16[512,1024]{1,0:T(8,128)(2,1)} %get-tuple-element.121.refs_0_.refs_1_, f32[512,1]{1,0:T(8,128)} %get-tuple-element.108.refs_2_, ...), custom_call_target="tpu_custom_call" | custom-call | flops 70866960384 | bytes 118111600 | tf_op jit(solution)/shard_map/pallas_call | solution.py:134
  369.6 17.1 %collective-permute-start.60 = (bf16[272,1024]{1,0:T(8,128)(2,1)}, bf16[272,1024]{1,0:T(8,128)(2,1)S(1)}, u32[]{:S(2)}, u32[]{:S(2)}) collective-permute-start(bf16[272,1024]{1,0:T(8,128)(2,1)} %slice_bitcast_fusion.1), channel_id=1, source_target_pairs={{0,8},{8,0},{1,9},{9,1},{2,10},{10,2},{3,11},{11,3},{4,12},{12,4},... | collective-permute-start | bytes 1671176 | tf_op jit(solution)/shard_map/ppermute | solution.py:958
  386.7 8.1 %shard_map.206.refs_0_ = bf16[512,1024]{1,0:T(8,128)(2,1)} custom-call(bf16[512,1024]{1,0:T(8,128)(2,1)} %get-tuple-element.185.refs_0_, bf16[4,2,512,256]{3,2,1,0:T(8,128)(2,1)} %get-tuple-element.159.refs_1_, bf16[4,2,512,256]{3,2,1,0:T(8,128)(2,1)} %collective-permute-done.50.refs_2_, bf16[1024,512]{1,0:T(8,128)(2,1)} %bitcast.134, ...), custom_call_target="tpu_custom_call" | custom-call | flops 6442450944 | bytes 10737418 | tf_op jit(solution)/shard_map/pallas_call | solution.py:134
  394.8 24.0 %shard_map.207 = (bf16[512,1024]{1,0:T(8,128)(2,1)}, bf16[2,2,272,1024]{3,2,1,0:T(8,128)(2,1)}) custom-call(bf16[512,1024]{1,0:T(8,128)(2,1)} %shard_map.206.refs_0_, bf16[512,1024]{1,0:T(8,128)(2,1)} %get-tuple-element.161.refs_1_, f32[512,1]{1,0:T(8,128)} %get-tuple-element.125.refs_2_, f32[1,1024]{1,0:T(1,128)} %get-tuple-element.208.refs_2_.refs_3_, ...), custom_call_target="tpu_custom_call" | custom-call | flops 28991029248 | bytes 48318384 | tf_op jit(solution)/shard_map/pallas_call | solution.py:134
  428.7 25.8 %shard_map.208 = bf16[512,1024]{1,0:T(8,128)(2,1)} custom-call(bf16[512,1024]{1,0:T(8,128)(2,1)} %get-tuple-element.168.refs_0_.refs_1_, bf16[512,1024]{1,0:T(8,128)(2,1)} %get-tuple-element.168.refs_0_.refs_1_, bf16[4,3,512,256]{3,2,1,0:T(8,128)(2,1)} %get-tuple-element.169.refs_2_, f32[4,4,512]{2,1,0:T(4,128)} %get-tuple-element.170.refs_3_, ...), custom_call_target="tpu_custom_call" | custom-call | flops 45097156608 | bytes 75161928 | tf_op jit(solution)/shard_map/pallas_call | solution.py:134
  464.0 25.2 %shard_map.209 = bf16[512,1024]{1,0:T(8,128)(2,1)} custom-call(bf16[512,1024]{1,0:T(8,128)(2,1)} %get-tuple-element.172.refs_0_.refs_1_, bf16[512,1024]{1,0:T(8,128)(2,1)} %get-tuple-element.172.refs_0_.refs_1_, bf16[4,3,512,256]{3,2,1,0:T(8,128)(2,1)} %get-tuple-element.173.refs_2_, f32[4,4,512]{2,1,0:T(4,128)} %get-tuple-element.174.refs_3_, ...), custom_call_target="tpu_custom_call" | custom-call | flops 45097156608 | bytes 75161928 | tf_op jit(solution)/shard_map/pallas_call | solution.py:134
  490.9 18.7 %collective-permute-start.63 = (bf16[272,1024]{1,0:T(8,128)(2,1)S(1)}, bf16[272,1024]{1,0:T(8,128)(2,1)}, u32[]{:S(2)}, u32[]{:S(2)}) collective-permute-start(bf16[272,1024]{1,0:T(8,128)(2,1)S(1)} %add_convert_fusion.1), channel_id=1, source_target_pairs={{0,2},{1,3},{2,0},{3,1},{4,6},{5,7},{6,4},{7,5},{8,10},{9,11},{10,... | collective-permute-start | bytes 1671176 | tf_op jit(solution)/shard_map/ppermute | solution.py:1197
  515.6 9.6 %collective-permute-done.58 = bf16[272,1024]{1,0:T(8,128)(2,1)S(1)} collective-permute-done((bf16[272,1024]{1,0:T(8,128)(2,1)S(1)}, bf16[272,1024]{1,0:T(8,128)(2,1)S(1)}, u32[]{:S(2)}, u32[]{:S(2)}) %collective-permute-start.58) | collective-permute-done | bytes 557088 | tf_op jit(solution)/shard_map/ppermute | solution.py:1197
  529.7 10.6 %collective-permute-done.59 = bf16[272,1024]{1,0:T(8,128)(2,1)} collective-permute-done((bf16[272,1024]{1,0:T(8,128)(2,1)S(1)}, bf16[272,1024]{1,0:T(8,128)(2,1)}, u32[]{:S(2)}, u32[]{:S(2)}) %collective-permute-start.59) | collective-permute-done | bytes 557088 | tf_op jit(solution)/shard_map/ppermute | solution.py:1197
  (299 shorter events, 154.6 us)
Async XLA Ops:
  6.6 33.0 %collective-permute-start.9 = (bf16[2048,1024]{1,0:T(8,128)(2,1)}, bf16[2048,1024]{1,0:T(8,128)(2,1)}, u32[]{:S(2)}, u32[]{:S(2)}) collective-permute-start(bf16[2048,1024]{1,0:T(8,128)(2,1)} %bitcast.90), channel_id=1, source_target_pairs={{0,16},{1,17},{2,18},{3,19},{4,20},{5,21},{6,22},{7,23},{8,24},{9,... | collective-permute-start | bytes 12582920 | tf_op jit(solution)/shard_map/ppermute | solution.py:930
  7.0 34.4 %collective-permute-start.8 = (bf16[1024,2048]{1,0:T(8,128)(2,1)}, bf16[1024,2048]{1,0:T(8,128)(2,1)}, u32[]{:S(2)}, u32[]{:S(2)}) collective-permute-start(bf16[1024,2048]{1,0:T(8,128)(2,1)} %bitcast.81), channel_id=1, source_target_pairs={{0,16},{1,17},{2,18},{3,19},{4,20},{5,21},{6,22},{7,23},{8,24},{9,... | collective-permute-start | bytes 12582920 | tf_op jit(solution)/shard_map/ppermute | solution.py:930
  106.4 29.2 %collective-permute-start.21 = (bf16[2304,256]{1,0:T(8,128)(2,1)}, bf16[2304,256]{1,0:T(8,128)(2,1)}, u32[]{:S(2)}, u32[]{:S(2)}) collective-permute-start(bf16[2304,256]{1,0:T(8,128)(2,1)} %shard_map.194), channel_id=1, source_target_pairs={{0,8},{1,9},{2,10},{3,11},{4,12},{5,13},{6,14},{7,15},{8,0},{9,1},... | collective-permute-start | bytes 3538952 | tf_op jit(solution)/shard_map/ppermute | solution.py:930
  128.0 31.6 %collective-permute-start.27 = (bf16[2304,256]{1,0:T(8,128)(2,1)}, bf16[2304,256]{1,0:T(8,128)(2,1)}, u32[]{:S(2)}, u32[]{:S(2)}) collective-permute-start(bf16[2304,256]{1,0:T(8,128)(2,1)} %copy-done.24), channel_id=1, source_target_pairs={{0,8},{1,9},{2,10},{3,11},{4,12},{5,13},{6,14},{7,15},{8,0},{9,1},... | collective-permute-start | bytes 3538952 | tf_op jit(solution)/shard_map/ppermute | solution.py:930
  135.6 25.8 %collective-permute-start.25 = (bf16[2304,256]{1,0:T(8,128)(2,1)}, bf16[2304,256]{1,0:T(8,128)(2,1)}, u32[]{:S(2)}, u32[]{:S(2)}) collective-permute-start(bf16[2304,256]{1,0:T(8,128)(2,1)} %collective-permute-done.21.refs_13_.refs_18_), channel_id=1, source_target_pairs={{0,2},{1,3},{2,0},{3,1},{4,6},{5,7},{6,4},{7,5},{8,10},{9,11},{10,... | collective-permute-start | bytes 3538952 | tf_op jit(solution)/shard_map/ppermute | solution.py:930
  170.2 26.3 %collective-permute-start.33 = (bf16[2,1024,128]{2,1,0:T(8,128)(2,1)}, bf16[2,1024,128]{2,1,0:T(8,128)(2,1)S(1)}, u32[]{:S(2)}, u32[]{:S(2)}) collective-permute-start(bf16[2,1024,128]{2,1,0:T(8,128)(2,1)} %collective-permute-done.20.refs_5_.refs_10_.refs_14_.refs_7_), channel_id=1, source_target_pairs={{0,2},{1,3},{2,0},{3,1},{4,6},{5,7},{6,4},{7,5},{8,10},{9,11},{10,... | collective-permute-start | bytes 1572872 | tf_op jit(solution)/shard_map/ppermute | solution.py:930
  171.0 26.0 %collective-permute-start.31 = (bf16[2,1024,128]{2,1,0:T(8,128)(2,1)}, bf16[2,1024,128]{2,1,0:T(8,128)(2,1)S(1)}, u32[]{:S(2)}, u32[]{:S(2)}) collective-permute-start(bf16[2,1024,128]{2,1,0:T(8,128)(2,1)} %collective-permute-done.20.refs_5_.refs_10_.refs_14_.refs_7_), channel_id=1, source_target_pairs={{0,1},{1,0},{2,3},{3,2},{4,5},{5,4},{6,7},{7,6},{8,9},{9,8},{10,11... | collective-permute-start | bytes 1572872 | tf_op jit(solution)/shard_map/ppermute | solution.py:930
  174.0 36.5 %collective-permute-start.29 = (bf16[2304,256]{1,0:T(8,128)(2,1)S(1)}, bf16[2304,256]{1,0:T(8,128)(2,1)}, u32[]{:S(2)}, u32[]{:S(2)}) collective-permute-start(bf16[2304,256]{1,0:T(8,128)(2,1)S(1)} %shard_map.198), channel_id=1, source_target_pairs={{0,8},{1,9},{2,10},{3,11},{4,12},{5,13},{6,14},{7,15},{8,0},{9,1},... | collective-permute-start | bytes 3538952 | tf_op jit(solution)/shard_map/ppermute | solution.py:930
  218.6 34.7 %collective-permute-start.37 = (bf16[4,2,512,256]{3,2,1,0:T(8,128)(2,1)}, bf16[4,2,512,256]{3,2,1,0:T(8,128)(2,1)}, u32[]{:S(2)}, u32[]{:S(2)}) collective-permute-start(bf16[4,2,512,256]{3,2,1,0:T(8,128)(2,1)} %shard_map.200.refs_2_.refs_6_), channel_id=1, source_target_pairs={{0,16},{16,0},{1,17},{17,1},{2,18},{18,2},{3,19},{19,3},{4,20},{20... | collective-permute-start | bytes 6291464 | tf_op jit(solution)/shard_map/ppermute | solution.py:958
  222.0 26.3 %collective-permute-start.47 = (bf16[512,1024]{1,0:T(8,128)(2,1)}, bf16[512,1024]{1,0:T(8,128)(2,1)}, u32[]{:S(2)}, u32[]{:S(2)}) collective-permute-start(bf16[512,1024]{1,0:T(8,128)(2,1)} %get-tuple-element.148), channel_id=1, source_target_pairs={{0,8},{1,9},{2,10},{3,11},{4,12},{5,13},{6,14},{7,15},{8,0},{9,1},... | collective-permute-start | bytes 3145736 | tf_op jit(solution)/shard_map/ppermute | solution.py:930
  230.5 45.7 %collective-permute-start.43 = (bf16[2304,256]{1,0:T(8,128)(2,1)S(1)}, bf16[2304,256]{1,0:T(8,128)(2,1)}, u32[]{:S(2)}, u32[]{:S(2)}) collective-permute-start(bf16[2304,256]{1,0:T(8,128)(2,1)S(1)} %shard_map.202), channel_id=1, source_target_pairs={{0,8},{1,9},{2,10},{3,11},{4,12},{5,13},{6,14},{7,15},{8,0},{9,1},... | collective-permute-start | bytes 3538952 | tf_op jit(solution)/shard_map/ppermute | solution.py:930
  230.8 45.9 %collective-permute-start.41 = (bf16[2304,256]{1,0:T(8,128)(2,1)}, bf16[2304,256]{1,0:T(8,128)(2,1)}, u32[]{:S(2)}, u32[]{:S(2)}) collective-permute-start(bf16[2304,256]{1,0:T(8,128)(2,1)} %collective-permute-done.29.refs_13_.refs_18_), channel_id=1, source_target_pairs={{0,2},{1,3},{2,0},{3,1},{4,6},{5,7},{6,4},{7,5},{8,10},{9,11},{10,... | collective-permute-start | bytes 3538952 | tf_op jit(solution)/shard_map/ppermute | solution.py:930
  232.4 44.4 %collective-permute-start.39 = (bf16[2304,256]{1,0:T(8,128)(2,1)}, bf16[2304,256]{1,0:T(8,128)(2,1)}, u32[]{:S(2)}, u32[]{:S(2)}) collective-permute-start(bf16[2304,256]{1,0:T(8,128)(2,1)} %collective-permute-done.29.refs_13_.refs_18_), channel_id=1, source_target_pairs={{0,1},{1,0},{2,3},{3,2},{4,5},{5,4},{6,7},{7,6},{8,9},{9,8},{10,11... | collective-permute-start | bytes 3538952 | tf_op jit(solution)/shard_map/ppermute | solution.py:930
  368.6 51.8 %collective-permute-start.45 = (bf16[512,1024]{1,0:T(8,128)(2,1)}, bf16[512,1024]{1,0:T(8,128)(2,1)}, u32[]{:S(2)}, u32[]{:S(2)}) collective-permute-start(bf16[512,1024]{1,0:T(8,128)(2,1)} %broadcast_select_fusion.4), channel_id=1, source_target_pairs={{0,16},{16,0},{1,17},{17,1},{2,18},{18,2},{3,19},{19,3},{4,20},{20... | collective-permute-start | bytes 3145736 | tf_op jit(solution)/shard_map/ppermute | solution.py:958
  369.6 54.6 %collective-permute-start.60 = (bf16[272,1024]{1,0:T(8,128)(2,1)}, bf16[272,1024]{1,0:T(8,128)(2,1)S(1)}, u32[]{:S(2)}, u32[]{:S(2)}) collective-permute-start(bf16[272,1024]{1,0:T(8,128)(2,1)} %slice_bitcast_fusion.1), channel_id=1, source_target_pairs={{0,8},{8,0},{1,9},{9,1},{2,10},{10,2},{3,11},{11,3},{4,12},{12,4},... | collective-permute-start | bytes 1671176 | tf_op jit(solution)/shard_map/ppermute | solution.py:958
  423.9 118.0 %collective-permute-start.46 = (bf16[512,1024]{1,0:T(8,128)(2,1)}, bf16[512,1024]{1,0:T(8,128)(2,1)}, u32[]{:S(2)}, u32[]{:S(2)}) collective-permute-start(bf16[512,1024]{1,0:T(8,128)(2,1)} %get-tuple-element.193), channel_id=1, source_target_pairs={{0,8},{8,0},{1,9},{9,1},{2,10},{10,2},{3,11},{11,3},{4,12},{12,4},... | collective-permute-start | bytes 3145736 | tf_op jit(solution)/shard_map/ppermute | solution.py:958
  424.4 32.4 %collective-permute-start.61 = (bf16[272,1024]{1,0:T(8,128)(2,1)S(1)}, bf16[272,1024]{1,0:T(8,128)(2,1)S(1)}, u32[]{:S(2)}, u32[]{:S(2)}) collective-permute-start(bf16[272,1024]{1,0:T(8,128)(2,1)S(1)} %fusion.4), channel_id=1, source_target_pairs={{0,4},{1,5},{2,6},{3,7},{4,0},{5,1},{6,2},{7,3},{8,12},{9,13},{10,... | collective-permute-start | bytes 1671176 | tf_op jit(solution)/shard_map/ppermute | solution.py:1197
  428.4 33.2 %collective-permute-start.52 = (bf16[272,1024]{1,0:T(8,128)(2,1)}, bf16[272,1024]{1,0:T(8,128)(2,1)}, u32[]{:S(2)}, u32[]{:S(2)}) collective-permute-start(bf16[272,1024]{1,0:T(8,128)(2,1)} %slice_bitcast_fusion.3), channel_id=1, source_target_pairs={{0,8},{8,0},{1,9},{9,1},{2,10},{10,2},{3,11},{11,3},{4,12},{12,4},... | collective-permute-start | bytes 1671176 | tf_op jit(solution)/shard_map/ppermute | solution.py:958
  454.5 55.4 %collective-permute-start.55 = (bf16[512,1024]{1,0:T(8,128)(2,1)}, bf16[512,1024]{1,0:T(8,128)(2,1)}, u32[]{:S(2)}, u32[]{:S(2)}) collective-permute-start(bf16[512,1024]{1,0:T(8,128)(2,1)} %shard_map.208), channel_id=1, source_target_pairs={{0,16},{1,17},{2,18},{3,19},{4,20},{5,21},{6,22},{7,23},{8,24},{9,... | collective-permute-start | bytes 3145736 | tf_op jit(solution)/shard_map/ppermute | solution.py:1130
  457.0 33.6 %collective-permute-start.62 = (bf16[272,1024]{1,0:T(8,128)(2,1)S(1)}, bf16[272,1024]{1,0:T(8,128)(2,1)S(1)}, u32[]{:S(2)}, u32[]{:S(2)}) collective-permute-start(bf16[272,1024]{1,0:T(8,128)(2,1)S(1)} %add_convert_fusion.2), channel_id=1, source_target_pairs={{0,1},{1,0},{2,3},{3,2},{4,5},{5,4},{6,7},{7,6},{8,9},{9,8},{10,11... | collective-permute-start | bytes 1671176 | tf_op jit(solution)/shard_map/ppermute | solution.py:1197
  462.8 46.7 %collective-permute-start.57 = (bf16[272,1024]{1,0:T(8,128)(2,1)S(1)}, bf16[272,1024]{1,0:T(8,128)(2,1)S(1)}, u32[]{:S(2)}, u32[]{:S(2)}) collective-permute-start(bf16[272,1024]{1,0:T(8,128)(2,1)S(1)} %fusion.5), channel_id=1, source_target_pairs={{0,4},{1,5},{2,6},{3,7},{4,0},{5,1},{6,2},{7,3},{8,12},{9,13},{10,... | collective-permute-start | bytes 1671176 | tf_op jit(solution)/shard_map/ppermute | solution.py:1197
  489.2 25.9 %collective-permute-start.53 = (bf16[512,1024]{1,0:T(8,128)(2,1)}, bf16[512,1024]{1,0:T(8,128)(2,1)S(1)}, u32[]{:S(2)}, u32[]{:S(2)}) collective-permute-start(bf16[512,1024]{1,0:T(8,128)(2,1)} %shard_map.209), channel_id=1, source_target_pairs={{16,0},{17,1},{18,2},{19,3},{20,4},{21,5},{22,6},{23,7},{24,8},{25... | collective-permute-start | bytes 3145736 | tf_op jit(solution)/shard_map/ppermute | solution.py:1130
  490.9 38.8 %collective-permute-start.63 = (bf16[272,1024]{1,0:T(8,128)(2,1)S(1)}, bf16[272,1024]{1,0:T(8,128)(2,1)}, u32[]{:S(2)}, u32[]{:S(2)}) collective-permute-start(bf16[272,1024]{1,0:T(8,128)(2,1)S(1)} %add_convert_fusion.1), channel_id=1, source_target_pairs={{0,2},{1,3},{2,0},{3,1},{4,6},{5,7},{6,4},{7,5},{8,10},{9,11},{10,... | collective-permute-start | bytes 1671176 | tf_op jit(solution)/shard_map/ppermute | solution.py:1197
  513.3 31.9 %collective-permute-start.56 = (bf16[512,1024]{1,0:T(8,128)(2,1)}, bf16[512,1024]{1,0:T(8,128)(2,1)}, u32[]{:S(2)}, u32[]{:S(2)}) collective-permute-start(bf16[512,1024]{1,0:T(8,128)(2,1)} %get-tuple-element.189), channel_id=1, source_target_pairs={{16,24},{17,25},{18,26},{19,27},{20,28},{21,29},{22,30},{23,31},{2... | collective-permute-start | bytes 3145736 | tf_op jit(solution)/shard_map/ppermute | solution.py:1133
  (97 other events, 1134.2 us)
